TPU v7x, 256 devices: a whole 4x4x8 slice. The times are simulated.
256 devices in a mesh: row: 16 (over x, z_lo, core), col: 16 (over y, z_hi).
Axes of the slice: x: 4, y: 4, z: 8 (z_hi: 4, z_lo: 2; z = z_hi * 2 + z_lo), core: 2. Of those that a mesh axis runs over, the one named last changes fastest.
Arguments:
- panel_prev: float32 [64, 262144], P(None, 'col'), may hold values from -6 to 6
- panel_cur: float32 [64, 262144], P(None, 'col'), may hold values from -6 to 6
- tiles: float32 [16, 16, 163, 128, 128], P('row', 'col'), may hold values from -0.25 to 0.25
- tile_rows: int32 [16, 16, 163], P('row', 'col'), may hold values from 0 to 127, as said below
- tile_cols: int32 [16, 16, 163], P('row', 'col'), may hold values from 0 to 127, as said below
- tile_count: int32 [16, 16], P('row', 'col'), may hold values from 1 to 163, as said below
- center: float32 [], replicated, may hold values from -0.3 to 0.3
- halfwidth: float32 [], replicated, may hold values from 0.8 to 1.6
Outputs:
- panel_next: float32 [64, 262144], P(None, 'col')
- panel_last: float32 [64, 262144], P(None, 'col')
Inputs may be any that keep to these rules, and one draw needn't show every extreme that they name: `tile_rows`: in each grid cell the first tile_count slots name distinct block pairs; later slots hold 0. `tile_cols`: paired with tile_rows slot by slot; later slots hold 0. `tile_count`: some grid cell holds exactly 163 tiles in every draw.
All inputs are finite; a program needn't handle non-finite values.
Results may differ from a plain program's by a relative error of at most 0.0003.
Values sent between devices are 32-bit elements; how exact they have to be, the bound alone decides.
No kernel may reach another device: no remote copies, remote signals or barrier semaphores. Data moves between devices by JAX's collectives and lax.ppermute only.
A program may use at most 128 MiB of HBM per device.

v0:
```python
import jax
import jax.numpy as jnp
from jax import lax
from jax.sharding import PartitionSpec as P


def tile_product(piece, tile_block, rows, cols, count, row_blocks):
    vectors = piece.shape[0]
    block_size = tile_block.shape[-1]
    slots = tile_block.shape[0]
    blocked = piece.reshape(vectors, piece.shape[1] // block_size, block_size)
    chosen = jnp.take(blocked, cols, axis=1)
    products = jnp.einsum("vtk,tjk->tvj", chosen, tile_block, precision=lax.Precision.HIGHEST)
    live = (lax.iota(jnp.int32, slots) < count).astype(jnp.float32)
    onehot = (rows[:, None] == lax.iota(jnp.int32, row_blocks)[None, :]).astype(jnp.float32) * live[
        :, None
    ]
    summed = jnp.einsum("tr,tvj->vrj", onehot, products, precision=lax.Precision.HIGHEST)
    return summed.reshape(vectors, row_blocks * block_size)


def degree_step(current, previous, tile_block, rows, cols, count, factor, center):
    piece_length = current.shape[1]
    block_size = tile_block.shape[-1]
    row_count = lax.axis_size("row")
    row_blocks = piece_length * lax.axis_size("col") // row_count // block_size
    share_length = piece_length // row_count
    partial_value = tile_product(current, tile_block, rows, cols, count, row_blocks)
    total = lax.psum(partial_value, "col")
    mine = lax.dynamic_slice_in_dim(total, lax.axis_index("col") * share_length, share_length, 1)
    gathered = lax.all_gather(mine, "row", axis=1, tiled=True)
    gathered = factor * (gathered - center * current) - previous
    return gathered


def body(panel_prev, panel_cur, tiles, tile_rows, tile_cols, tile_count, center, halfwidth):
    tile_block = tiles.reshape(tiles.shape[2], tiles.shape[3], tiles.shape[4])
    rows = tile_rows.reshape(tile_rows.shape[2])
    cols = tile_cols.reshape(tile_cols.shape[2])
    count = tile_count.reshape(())
    factor = 2.0 / halfwidth
    panel_next = degree_step(panel_cur, panel_prev, tile_block, rows, cols, count, factor, center)
    panel_last = degree_step(panel_next, panel_cur, tile_block, rows, cols, count, factor, center)
    return (panel_next, panel_last)


def solution(mesh):
    placed = (
        P(None, "col"),
        P(None, "col"),
        P("row", "col", None, None, None),
        P("row", "col", None),
        P("row", "col", None),
        P("row", "col"),
        P(),
        P(),
    )
    return jax.shard_map(
        body,
        mesh=mesh,
        in_specs=placed,
        out_specs=(P(None, "col"), P(None, "col")),
        check_vma=False,
    )
```

profile of v0, /device:TPU:1, one launch (start us, length us, event | category | flops | bytes accessed | tf_op | source)
XLA Modules:
  0.0 682.0 jit_solution(14906881324160290806)
XLA Ops:
  7.2 0.0 all-reduce.3.cloned.1.call-start
  7.2 0.7 compare_and_fusion
  7.9 0.7 compare_select_fusion
  9.3 4.8 copy_bitcast_fusion.3
  14.0 5.4 gather_fusion
  19.5 23.3 %fusion.2 = f32[163,64,128]{2,1,0:T(8,128)S(1)} fusion(f32[1,1,163,128,128]{4,3,2,1,0:T(8,128)} %param.12, f32[163,64,128]{2,1,0:T(8,128)} %gather_fusion, pred[163]{0:T(512)(128)(4,1)S(1)} %compare_and_fusion), kind=kOutput, calls=%fused_computation.4 | convolution fusion | flops 2052349952 | bytes 21364900 | tf_op jit(solution)/shard_map/vtk,tjk->tvj/dot_general | solution.py:13
  42.8 18.8 %fusion.16 = f32[64,128,128]{1,2,0:T(8,128)} fusion(f32[163,64,128]{2,1,0:T(8,128)S(1)} %fusion.2, f32[163]{0:T(256)S(1)} %compare_convert_fusion, s32[163]{0:T(256)S(1)} %bitcast.46), kind=kOutput, calls=%fused_computation.24 | convolution fusion | flops 2051056384 | bytes 9536792 | tf_op jit(solution)/shard_map/tr,tvj->vrj/dot_general | solution.py:18
  61.7 5.6 copy.14
  67.3 6.6 copy.35
  73.8 0.0 all-reduce.3.cloned.1.call-update
  73.9 0.0 all-gather.3.cloned.1.call-start
  73.9 217.0 %all-reduce.3.cloned.1.call-done = f32[64,16384]{1,0:T(8,128)} async-done(((f32[64,16384]{1,0:T(8,128)}), f32[64,16384]{1,0:T(8,128)}) %all-reduce.3.cloned.1.call-update) | async-done | bytes 4194320 | tf_op jit(solution)/shard_map/psum | solution.py:29
  290.9 1.7 constant_dynamic-slice_fusion.1
  292.6 0.0 all-gather.3.cloned.1.call-update
  292.6 13.2 %all-reduce.5.cloned.1.call-start = ((), (), s32[]{:S(2)}) async-start(), calls=%async_computation.2 | async-start | bytes 8388608 | tf_op jit(solution)/shard_map/psum | solution.py:29
  307.1 30.4 %all-gather.3.cloned.1.call-done = f32[64,16384]{1,0:T(8,128)} async-done(((f32[64,1024]{1,0:T(8,128)}), f32[64,16384]{1,0:T(8,128)}) %all-gather.3.cloned.1.call-update) | async-done | bytes 4194320 | tf_op jit(solution)/shard_map/all_gather | solution.py:31
  337.5 5.3 multiply_subtract_fusion.1
  342.8 0.0 copy-start
  342.8 2.0 copy-done
  344.8 2.6 copy_bitcast_fusion.2
  347.4 5.4 gather_fusion.1
  352.8 23.3 %fusion = f32[163,64,128]{2,1,0:T(8,128)S(1)} fusion(f32[1,1,163,128,128]{4,3,2,1,0:T(8,128)} %param.12, f32[163,64,128]{2,1,0:T(8,128)} %gather_fusion.1, pred[163]{0:T(512)(128)(4,1)S(1)} %compare_and_fusion), kind=kOutput, calls=%fused_computation.2 | convolution fusion | flops 2052349952 | bytes 21364900 | tf_op jit(solution)/shard_map/vtk,tjk->tvj/dot_general | solution.py:13
  376.1 18.6 %fusion.19 = f32[64,128,128]{1,2,0:T(8,128)} fusion(f32[163,64,128]{2,1,0:T(8,128)S(1)} %fusion, f32[163]{0:T(256)S(1)} %compare_convert_fusion, s32[163]{0:T(256)S(1)} %bitcast.47), kind=kOutput, calls=%fused_computation.25 | convolution fusion | flops 2051056384 | bytes 9536792 | tf_op jit(solution)/shard_map/tr,tvj->vrj/dot_general | solution.py:18
  394.7 5.6 copy.17
  400.3 6.6 copy.34
  406.9 0.0 all-reduce.5.cloned.1.call-update
  406.9 0.0 all-gather.5.cloned.1.call-start
  407.0 214.6 %all-reduce.5.cloned.1.call-done = f32[64,16384]{1,0:T(8,128)} async-done(((f32[64,16384]{1,0:T(8,128)}), f32[64,16384]{1,0:T(8,128)}) %all-reduce.5.cloned.1.call-update) | async-done | bytes 4194320 | tf_op jit(solution)/shard_map/psum | solution.py:29
  621.6 1.7 constant_dynamic-slice_fusion
  623.2 0.0 all-gather.5.cloned.1.call-update
  623.3 44.7 %all-gather.5.cloned.1.call-done = f32[64,16384]{1,0:T(8,128)} async-done(((f32[64,1024]{1,0:T(8,128)}), f32[64,16384]{1,0:T(8,128)}) %all-gather.5.cloned.1.call-update) | async-done | bytes 4194320 | tf_op jit(solution)/shard_map/all_gather | solution.py:31
  668.0 7.3 %multiply_subtract_fusion = f32[64,16384]{1,0:T(8,128)} fusion(f32[64,16384]{1,0:T(8,128)} %param.11, f32[64,16384]{1,0:T(8,128)} %all-gather.5.cloned.1.call-done, f32[64,16384]{1,0:T(8,128)} %copy-done, f32[]{:T(128)S(6)} %copy.39, f32[]{:T(128)S(6)} %div.3), kind=kLoop, calls=%fused_computation.18 | loop fusion | flops 4194304 | bytes 16777224 | tf_op jit(solution)/shard_map/sub | solution.py:32
  (4 shorter events, 0.0 us)
Async XLA Ops:
  7.2 283.8 %all-reduce.3.cloned.1.call-start = ((), (), s32[]{:S(2)}) async-start(), calls=%async_computation | async-start | bytes 8388608 | tf_op jit(solution)/shard_map/psum | solution.py:29
  19.5 23.4 %copy-start.1 = (s32[1,1,163]{2,1,0:T(1,128)S(1)}, s32[1,1,163]{2,1,0:T(1,128)}, u32[]{:S(2)}) copy-start(s32[1,1,163]{2,1,0:T(1,128)} %param.13) | copy-start | bytes 1960
  73.9 263.7 %all-gather.3.cloned.1.call-start = ((), (), s32[]{:S(2)}) async-start(), calls=%async_computation.1 | async-start | bytes 4456448 | tf_op jit(solution)/shard_map/all_gather | solution.py:31
  292.6 328.9 %all-reduce.5.cloned.1.call-start = ((), (), s32[]{:S(2)}) async-start(), calls=%async_computation.2 | async-start | bytes 8388608 | tf_op jit(solution)/shard_map/psum | solution.py:29
  342.8 2.0 copy-start
  406.9 261.1 %all-gather.5.cloned.1.call-start = ((), (), s32[]{:S(2)}) async-start(), calls=%async_computation.3 | async-start | bytes 4456448 | tf_op jit(solution)/shard_map/all_gather | solution.py:31
Sparse Core Ops, SparseCore 0:
  74.0 216.9 all-reduce.2
  293.3 44.1 all-gather.2
  407.0 214.4 all-reduce.4
  623.8 44.1 all-gather.4
where the time goes:
time: 688 us; the launch traced here: 682 us
  waiting for transfers between devices  507 us (74%)
  matrix products  84.1 us (12%)
  local copies, waits for them, and re-layouts  47.9 us (7%)
  between operations  16 us (2%)
  other arithmetic  13.9 us (2%)
  starting transfers between devices  13.3 us (2%)
    psum x2, waiting for transfers between devices, degree_step(): total = lax.psum(partial_value, 'col')  432 us
    all_gather x2, waiting for transfers between devices, degree_step(): gathered = lax.all_gather(mine, 'row', axis=1, tiled=True)  75.1 us
    dot_general x2, matrix products, tile_product(): jnp.einsum('vtk,tjk->tvj', chosen, tile_block, precision=lax.Precision.HI...  46.7 us
    dot_general x2, matrix products, tile_product(): jnp.einsum('tr,tvj->vrj', onehot, products, precision=lax.Precision.HIGHEST)  37.4 us
    unnamed x6, local copies, waits for them, and re-layouts  15.2 us
  transfers between devices with their start and end apart: 4, of which 4 were waited for; matrix products, arithmetic and copies ran while one was open for 0% of the time, Pallas kernels for 0%

commit v1 on v0

v1 whole, which is shorter than its diff:
```python
import functools

import jax
import jax.numpy as jnp
from jax import lax
from jax.experimental import pallas as pl
from jax.experimental.pallas import tpu as pltpu
from jax.sharding import Mesh, PartitionSpec as P

B = 128
BLK = 128
CAP = 163
CHUNK = 8
GROUPS = 2
VEC = 64
V = VEC // GROUPS
ROW = ("x", "zl", "core")
COL = ("y", "zh")


def split(value):
    high = value.astype(jnp.bfloat16)
    return high, (value - high.astype(jnp.float32)).astype(jnp.bfloat16)


def product_kernel(flat, rows, cols, info, x_ref, tiles, own, plus, minus, far, xs, acc, held, sems):
    count, mine = info[0], info[1]
    chunks = -(-CAP // CHUNK)
    for c in range(chunks):
        size = min(CHUNK, CAP - c * CHUNK)

        @pl.when(c * CHUNK < count)
        def _():
            span = pl.ds(c * CHUNK, size)
            pltpu.make_async_copy(tiles.at[span], held.at[span], sems.at[c]).start()

    for c in range(BLK):
        block = x_ref[:, c * B : (c + 1) * B] if flat else x_ref[c]
        high, low = split(block)
        xs[c, :V] = high
        xs[c, V:] = low
    acc[...] = jnp.zeros_like(acc)

    def some(first, size):
        sums = []
        for u in range(size):
            slot = first + u
            high, low = split(held[slot])
            both = jnp.concatenate([high, low], axis=0)
            p = lax.dot_general(
                xs[cols[slot]], both, (((1,), (1,)), ((), ())), preferred_element_type=jnp.float32
            )
            sums.append(p[:V, :B] + (p[V:, :B] + p[:V, B:]))
        for u in range(size):
            slot = first + u
            at = jnp.where(slot < count, lax.rem(rows[slot] + (4 - mine) * 32, BLK), BLK)
            acc[at] += sums[u]

    whole = CAP // CHUNK

    def step(c, carry):
        span = pl.ds(c * CHUNK, CHUNK)
        pltpu.make_async_copy(tiles.at[span], held.at[span], sems.at[c]).wait()
        some(c * CHUNK, CHUNK)
        return carry

    lax.fori_loop(0, jnp.minimum((count + CHUNK - 1) // CHUNK, whole), step, 0)

    if CAP % CHUNK:

        @pl.when(count > whole * CHUNK)
        def _():
            span = pl.ds(whole * CHUNK, CAP % CHUNK)
            pltpu.make_async_copy(tiles.at[span], held.at[span], sems.at[whole]).wait()
            some(whole * CHUNK, CAP % CHUNK)

    own[...] = acc[0:32]
    plus[...] = acc[32:64]
    far[...] = acc[64:96]
    minus[...] = acc[96:128]


def product(x, tiles, rows, cols, info, group):
    flat = x.ndim == 2
    x_spec = (
        pl.BlockSpec((V, BLK * B), lambda _: (group, 0))
        if flat
        else pl.BlockSpec((BLK, V, B), lambda _: (0, 0, 0))
    )
    smem = pl.BlockSpec(memory_space=pltpu.SMEM)
    piece = pl.BlockSpec((32, V, B), lambda _: (0, 0, 0))
    return pl.pallas_call(
        functools.partial(product_kernel, flat),
        grid=(1,),
        out_shape=[jax.ShapeDtypeStruct((32, V, B), jnp.float32)] * 4,
        in_specs=[smem, smem, smem, x_spec, pl.BlockSpec(memory_space=pl.ANY)],
        out_specs=[piece] * 4,
        scratch_shapes=[
            pltpu.VMEM((BLK, 2 * V, B), jnp.bfloat16),
            pltpu.VMEM((BLK + 1, V, B), jnp.float32),
            pltpu.VMEM((CAP, B, B), jnp.float32),
            pltpu.SemaphoreType.DMA((-(-CAP // CHUNK),)),
        ],
        compiler_params=pltpu.CompilerParams(vmem_limit_bytes=40 << 20),
        cost_estimate=pl.CostEstimate(
            flops=CAP * B * B * VEC * 8, bytes_accessed=CAP * B * B * 4, transcendentals=0
        ),
        name="product",
    )(rows, cols, info, x, tiles)


def add_kernel(info, a, b, c, d, own, plus, minus, far):
    mine = info[2]
    for k, out in enumerate((own, plus, far, minus)):
        span = pl.ds(lax.rem(mine + k, 4) * 8, 8)
        out[...] = (a[span] + b[span]) + (c[span] + d[span])


def add_pieces(info, parts):
    smem = pl.BlockSpec(memory_space=pltpu.SMEM)
    return pl.pallas_call(
        add_kernel,
        out_shape=[jax.ShapeDtypeStruct((8, V, B), jnp.float32)] * 4,
        in_specs=[smem] + [pl.BlockSpec(memory_space=pltpu.VMEM)] * 4,
        out_specs=[pl.BlockSpec(memory_space=pltpu.VMEM)] * 4,
        name="add_pieces",
    )(info, *parts)


def combine_kernel(scal, a, b, c, d, cur, prev, out):
    factor, center = scal[0], scal[1]
    image = (a[...] + b[...]) + (c[...] + d[...])
    out[...] = factor * (image - center * cur[...]) - prev[...]


def combine(scal, parts, cur, prev):
    smem = pl.BlockSpec(memory_space=pltpu.SMEM)
    vmem = pl.BlockSpec(memory_space=pltpu.VMEM)
    return pl.pallas_call(
        combine_kernel,
        out_shape=jax.ShapeDtypeStruct((8, V, B), jnp.float32),
        in_specs=[smem] + [vmem] * 6,
        out_specs=vmem,
        name="combine",
    )(scal, *parts, cur, prev)


def spread(parts, axis):
    own, plus, minus, far = parts
    return (
        own,
        lax.ppermute(plus, axis, [(i, (i + 1) % 4) for i in range(4)]),
        lax.ppermute(minus, axis, [(i, (i + 3) % 4) for i in range(4)]),
        lax.ppermute(far, axis, [(i, (i + 2) % 4) for i in range(4)]),
    )


def own_share(panel, row):
    mine = lax.dynamic_slice_in_dim(panel, row * 8 * B, 8 * B, 1)
    blocked = jnp.transpose(mine.reshape(GROUPS, V, 8, B), (0, 2, 1, 3))
    return [blocked[g] for g in range(GROUPS)]


def body(panel_prev, panel_cur, tiles, tile_rows, tile_cols, tile_count, center, halfwidth):
    tiles = tiles.reshape(CAP, B, B)
    rows = tile_rows.reshape(CAP)
    cols = tile_cols.reshape(CAP)
    info = jnp.stack([tile_count.reshape(()), lax.axis_index("y"), lax.axis_index("zh")]).astype(jnp.int32)
    scal = jnp.stack([2.0 / halfwidth, center])
    row = lax.axis_index(ROW)
    cur = own_share(panel_cur, row)
    prev = own_share(panel_prev, row)

    def degree(x, group, cur, prev):
        parts = product(x, tiles, rows, cols, info, group)
        parts = add_pieces(info, spread(parts, "y"))
        share = combine(scal, spread(parts, "zh"), cur, prev)
        whole = lax.all_gather(share, ROW).reshape(BLK, V, B)
        return share, whole

    nexts = [degree(panel_cur, g, cur[g], prev[g]) for g in range(GROUPS)]
    lasts = [degree(nexts[g][1], g, nexts[g][0], cur[g]) for g in range(GROUPS)]

    def panel(wholes):
        return jnp.concatenate([jnp.transpose(w, (1, 0, 2)).reshape(V, BLK * B) for _, w in wholes])

    return panel(nexts), panel(lasts)


def solution(mesh):
    fine = Mesh(mesh.devices.reshape(4, 2, 2, 4, 4), ROW + COL)
    placed = (
        P(None, COL),
        P(None, COL),
        P(ROW, COL, None, None, None),
        P(ROW, COL, None),
        P(ROW, COL, None),
        P(ROW, COL),
        P(),
        P(),
    )
    return jax.shard_map(
        body, mesh=fine, in_specs=placed, out_specs=(P(None, COL), P(None, COL)), check_vma=False
    )
```

time: 688 us -> 278 us (0.40)
  waiting for transfers between devices: 507 us -> 143 us
  matrix products: 84.1 us -> 0 us
  starting transfers between devices: 13.3 us -> 53.9 us
  Pallas kernels: 0 us -> 29.8 us
  local copies, waits for them, and re-layouts: 47.9 us -> 25.7 us
    psum x2 -> x0, waiting for transfers between devices: 432 us -> none  [degree_step(): total = lax.psum(partial_value, 'col')]
    ppermute x0 -> x24, waiting for transfers between devices: none -> 111 us  [the longest x8 59.4 us: spread(): lax.ppermute(far, axis, [(i, (i + 2) % 4) for i in range(4)])]
    dot_general x4 -> x0, matrix products: 84.1 us -> none  [the longest x2 46.7 us: tile_product(): jnp.einsum('vtk,tjk->tvj', chosen, tile_block, precision=lax.Precision.HI...]
    ppermute x0 -> x24, starting transfers between devices: none -> 53.7 us  [the longest x8 24.8 us: spread(): lax.ppermute(minus, axis, [(i, (i + 3) % 4) for i in range(4)])]
    all_gather x2 -> x4, waiting for transfers between devices: 75.1 us -> 32.2 us  [degree(): whole = lax.all_gather(share, ROW).reshape(BLK, V, B)]
    pallas_call x0 -> x12, Pallas kernels: none -> 29.8 us  [the longest x4 12.4 us: product(): pl.pallas_call(functools.partial(product_kernel, flat), grid=(1,), out_sh...]
    psum x2 -> x0, starting transfers between devices: 13.2 us -> none  [degree_step(): total = lax.psum(partial_value, 'col')]
    sub x2 -> x0, other arithmetic: 12.5 us -> none  [degree_step(): gathered = factor * (gathered - center * current) - previous]
  transfers between devices with their start and end apart: 4 -> 28, of which waited for: 4 -> 18; matrix products, arithmetic and copies ran while one was open for 0% -> 5% of each run, Pallas kernels for 0% -> 8%
where the time goes in v1:
time: 278 us; the launch traced here: 276 us
  waiting for transfers between devices  143 us (51%)
  starting transfers between devices  53.9 us (19%)
  Pallas kernels  29.8 us (11%)
  local copies, waits for them, and re-layouts  25.7 us (9%)
  between operations  16 us (6%)
  other arithmetic  7.53 us (3%)
    ppermute x8, waiting for transfers between devices, spread(): lax.ppermute(far, axis, [(i, (i + 2) % 4) for i in range(4)])  59.4 us
    ppermute x8, waiting for transfers between devices, spread(): lax.ppermute(plus, axis, [(i, (i + 1) % 4) for i in range(4)])  35.6 us
    all_gather x4, waiting for transfers between devices, degree(): whole = lax.all_gather(share, ROW).reshape(BLK, V, B)  32.2 us
    ppermute x8, starting transfers between devices, spread(): lax.ppermute(minus, axis, [(i, (i + 3) % 4) for i in range(4)])  24.8 us
    unnamed x80, local copies, waits for them, and re-layouts  18.4 us
    ppermute x8, waiting for transfers between devices, spread(): lax.ppermute(minus, axis, [(i, (i + 3) % 4) for i in range(4)])  15.7 us
    ppermute x8, starting transfers between devices, spread(): lax.ppermute(far, axis, [(i, (i + 2) % 4) for i in range(4)])  15.2 us
    ppermute x8, starting transfers between devices, spread(): lax.ppermute(plus, axis, [(i, (i + 1) % 4) for i in range(4)])  13.6 us
  transfers between devices with their start and end apart: 28, of which 18 were waited for; matrix products, arithmetic and copies ran while one was open for 5% of the time, Pallas kernels for 8%

profile of v1, /device:TPU:1, one launch (start us, length us, event | category | flops | bytes accessed | tf_op | source)
XLA Modules:
  0.0 275.9 jit_solution(11773127852799598314)
XLA Ops:
  11.5 2.9 %product.4 = (f32[32,32,128]{2,1,0:T(8,128)S(1)}, f32[32,32,128]{2,1,0:T(8,128)S(1)}, f32[32,32,128]{2,1,0:T(8,128)S(1)}, f32[32,32,128]{2,1,0:T(8,128)S(1)}) custom-call(s32[163]{0:T(256)S(1)} %bitcast.56, s32[163]{0:T(256)S(1)} %bitcast.60, s32[3]{0:T(128)S(1)} %pad_add_fusion.info, f32[64,16384]{1,0:T(8,128)S(1)} %copy-done, f32[163,128,128]{2,1,0:T(8,128)} %bitcast.64), custom_call_target="tpu_custom_call" | custom-call | flops 1367343104 | bytes 10682368 | tf_op jit(solution)/shard_map/product/pallas_call | solution.py:92
  17.6 3.3 %collective-permute-start.1 = (f32[32,32,128]{2,1,0:T(8,128)S(1)}, f32[32,32,128]{2,1,0:T(8,128)S(1)}, u32[]{:S(2)}, u32[]{:S(2)}) collective-permute-start(f32[32,32,128]{2,1,0:T(8,128)S(1)} %get-tuple-element.36), channel_id=1, source_target_pairs={{0,12},{4,0},{8,4},{12,8},{1,13},{5,1},{9,5},{13,9},{2,14},{6,2},{... | collective-permute-start | bytes 1572872 | tf_op jit(solution)/shard_map/ppermute | solution.py:153
  20.9 3.2 %collective-permute-start.2 = (f32[32,32,128]{2,1,0:T(8,128)S(1)}, f32[32,32,128]{2,1,0:T(8,128)}, u32[]{:S(2)}, u32[]{:S(2)}) collective-permute-start(f32[32,32,128]{2,1,0:T(8,128)S(1)} %get-tuple-element.37), channel_id=1, source_target_pairs={{0,8},{4,12},{8,0},{12,4},{1,9},{5,13},{9,1},{13,5},{2,10},{6,14},... | collective-permute-start | bytes 1572872 | tf_op jit(solution)/shard_map/ppermute | solution.py:154
  26.3 5.5 %collective-permute-done.b = f32[32,32,128]{2,1,0:T(8,128)S(1)} collective-permute-done((f32[32,32,128]{2,1,0:T(8,128)S(1)}, f32[32,32,128]{2,1,0:T(8,128)S(1)}, u32[]{:S(2)}, u32[]{:S(2)}) %collective-permute-start) | collective-permute-done | bytes 524320 | tf_op jit(solution)/shard_map/ppermute | solution.py:152
  31.7 3.2 %collective-permute-done.1.c = f32[32,32,128]{2,1,0:T(8,128)S(1)} collective-permute-done((f32[32,32,128]{2,1,0:T(8,128)S(1)}, f32[32,32,128]{2,1,0:T(8,128)S(1)}, u32[]{:S(2)}, u32[]{:S(2)}) %collective-permute-start.1) | collective-permute-done | bytes 524320 | tf_op jit(solution)/shard_map/ppermute | solution.py:153
  34.9 10.0 %collective-permute-done.2.d = f32[32,32,128]{2,1,0:T(8,128)} collective-permute-done((f32[32,32,128]{2,1,0:T(8,128)S(1)}, f32[32,32,128]{2,1,0:T(8,128)}, u32[]{:S(2)}, u32[]{:S(2)}) %collective-permute-start.2) | collective-permute-done | bytes 524320 | tf_op jit(solution)/shard_map/ppermute | solution.py:154
  44.9 2.4 add_pieces.4
  47.4 3.6 %collective-permute-start.3 = (f32[8,32,128]{2,1,0:T(8,128)}, f32[8,32,128]{2,1,0:T(8,128)S(1)}, u32[]{:S(2)}, u32[]{:S(2)}) collective-permute-start(f32[8,32,128]{2,1,0:T(8,128)} %get-tuple-element.39), channel_id=1, source_target_pairs={{0,1},{1,2},{2,3},{3,0},{4,5},{5,6},{6,7},{7,4},{8,9},{9,10},{10,1... | collective-permute-start | bytes 393224 | tf_op jit(solution)/shard_map/ppermute | solution.py:152
  52.4 5.5 %collective-permute-start.5 = (f32[8,32,128]{2,1,0:T(8,128)}, f32[8,32,128]{2,1,0:T(8,128)S(1)}, u32[]{:S(2)}, u32[]{:S(2)}) collective-permute-start(f32[8,32,128]{2,1,0:T(8,128)} %get-tuple-element.41), channel_id=1, source_target_pairs={{0,2},{1,3},{2,0},{3,1},{4,6},{5,7},{6,4},{7,5},{8,10},{9,11},{10,... | collective-permute-start | bytes 393224 | tf_op jit(solution)/shard_map/ppermute | solution.py:154
  60.7 3.3 %collective-permute-done.4.c = f32[8,32,128]{2,1,0:T(8,128)S(1)} collective-permute-done((f32[8,32,128]{2,1,0:T(8,128)}, f32[8,32,128]{2,1,0:T(8,128)S(1)}, u32[]{:S(2)}, u32[]{:S(2)}) %collective-permute-start.4) | collective-permute-done | bytes 131104 | tf_op jit(solution)/shard_map/ppermute | solution.py:153
  69.7 2.9 %product.5 = (f32[32,32,128]{2,1,0:T(8,128)S(1)}, f32[32,32,128]{2,1,0:T(8,128)S(1)}, f32[32,32,128]{2,1,0:T(8,128)S(1)}, f32[32,32,128]{2,1,0:T(8,128)S(1)}) custom-call(s32[163]{0:T(256)S(1)} %bitcast.57, s32[163]{0:T(256)S(1)} %bitcast.61, s32[3]{0:T(128)S(1)} %copy-done.11, f32[64,16384]{1,0:T(8,128)S(1)} %copy-done.1, f32[163,128,128]{2,1,0:T(8,128)} %bitcast.65), custom_call_target="tpu_custom_call" | custom-call | flops 1367343104 | bytes 10682368 | tf_op jit(solution)/shard_map/product/pallas_call | solution.py:92
  77.6 7.4 %collective-permute-done.6.b = f32[32,32,128]{2,1,0:T(8,128)S(1)} collective-permute-done((f32[32,32,128]{2,1,0:T(8,128)S(1)}, f32[32,32,128]{2,1,0:T(8,128)S(1)}, u32[]{:S(2)}, u32[]{:S(2)}) %collective-permute-start.6) | collective-permute-done | bytes 524320 | tf_op jit(solution)/shard_map/ppermute | solution.py:152
  86.6 14.6 %collective-permute-done.8.d = f32[32,32,128]{2,1,0:T(8,128)S(1)} collective-permute-done((f32[32,32,128]{2,1,0:T(8,128)S(1)}, f32[32,32,128]{2,1,0:T(8,128)S(1)}, u32[]{:S(2)}, u32[]{:S(2)}) %collective-permute-start.8) | collective-permute-done | bytes 524320 | tf_op jit(solution)/shard_map/ppermute | solution.py:154
  102.0 2.4 add_pieces.5
  104.4 4.9 %collective-permute-start.10 = (f32[8,32,128]{2,1,0:T(8,128)}, f32[8,32,128]{2,1,0:T(8,128)S(1)}, u32[]{:S(2)}, u32[]{:S(2)}) collective-permute-start(f32[8,32,128]{2,1,0:T(8,128)} %get-tuple-element.48), channel_id=1, source_target_pairs={{0,3},{1,0},{2,1},{3,2},{4,7},{5,4},{6,5},{7,6},{8,11},{9,8},{10,9... | collective-permute-start | bytes 393224 | tf_op jit(solution)/shard_map/ppermute | solution.py:153
  111.5 6.8 %collective-permute-done.10.c = f32[8,32,128]{2,1,0:T(8,128)S(1)} collective-permute-done((f32[8,32,128]{2,1,0:T(8,128)}, f32[8,32,128]{2,1,0:T(8,128)S(1)}, u32[]{:S(2)}, u32[]{:S(2)}) %collective-permute-start.10) | collective-permute-done | bytes 131104 | tf_op jit(solution)/shard_map/ppermute | solution.py:153
  118.3 3.2 %collective-permute-done.11.d = f32[8,32,128]{2,1,0:T(8,128)S(1)} collective-permute-done((f32[8,32,128]{2,1,0:T(8,128)}, f32[8,32,128]{2,1,0:T(8,128)S(1)}, u32[]{:S(2)}, u32[]{:S(2)}) %collective-permute-start.11) | collective-permute-done | bytes 131104 | tf_op jit(solution)/shard_map/ppermute | solution.py:154
  125.8 3.0 %product.6 = (f32[32,32,128]{2,1,0:T(8,128)S(1)}, f32[32,32,128]{2,1,0:T(8,128)S(1)}, f32[32,32,128]{2,1,0:T(8,128)S(1)}, f32[32,32,128]{2,1,0:T(8,128)S(1)}) custom-call(s32[163]{0:T(256)S(1)} %bitcast.58, s32[163]{0:T(256)S(1)} %bitcast.62, s32[3]{0:T(128)S(1)} %copy-done.12, f32[128,32,128]{2,1,0:T(8,128)S(1)} %copy-done.2, f32[163,128,128]{2,1,0:T(8,128)} %bitcast.66), custom_call_target="tpu_custom_call" | custom-call | flops 1367343104 | bytes 10682368 | tf_op jit(solution)/shard_map/product/pallas_call | solution.py:92
  134.7 8.9 %collective-permute-done.12.b = f32[32,32,128]{2,1,0:T(8,128)S(1)} collective-permute-done((f32[32,32,128]{2,1,0:T(8,128)S(1)}, f32[32,32,128]{2,1,0:T(8,128)S(1)}, u32[]{:S(2)}, u32[]{:S(2)}) %collective-permute-start.12) | collective-permute-done | bytes 524320 | tf_op jit(solution)/shard_map/ppermute | solution.py:152
  143.6 14.7 %collective-permute-done.14.d = f32[32,32,128]{2,1,0:T(8,128)S(1)} collective-permute-done((f32[32,32,128]{2,1,0:T(8,128)S(1)}, f32[32,32,128]{2,1,0:T(8,128)S(1)}, u32[]{:S(2)}, u32[]{:S(2)}) %collective-permute-start.14) | collective-permute-done | bytes 524320 | tf_op jit(solution)/shard_map/ppermute | solution.py:154
  159.2 2.4 add_pieces.6
  161.6 4.2 %collective-permute-start.16 = (f32[8,32,128]{2,1,0:T(8,128)}, f32[8,32,128]{2,1,0:T(8,128)S(1)}, u32[]{:S(2)}, u32[]{:S(2)}) collective-permute-start(f32[8,32,128]{2,1,0:T(8,128)} %get-tuple-element.56), channel_id=1, source_target_pairs={{0,3},{1,0},{2,1},{3,2},{4,7},{5,4},{6,5},{7,6},{8,11},{9,8},{10,9... | collective-permute-start | bytes 393224 | tf_op jit(solution)/shard_map/ppermute | solution.py:153
  169.5 3.6 %product.7 = (f32[32,32,128]{2,1,0:T(8,128)S(1)}, f32[32,32,128]{2,1,0:T(8,128)}, f32[32,32,128]{2,1,0:T(8,128)S(1)}, f32[32,32,128]{2,1,0:T(8,128)S(1)}) custom-call(s32[163]{0:T(256)S(1)} %bitcast.59, s32[163]{0:T(256)S(1)} %bitcast.63, s32[3]{0:T(128)S(1)} %copy-done.13, f32[128,32,128]{2,1,0:T(8,128)S(1)} %copy-done.4, f32[163,128,128]{2,1,0:T(8,128)} %bitcast.67), custom_call_target="tpu_custom_call" | custom-call | flops 1367343104 | bytes 10682368 | tf_op jit(solution)/shard_map/product/pallas_call | solution.py:92
  175.6 4.2 %collective-permute-start.19 = (f32[32,32,128]{2,1,0:T(8,128)S(1)}, f32[32,32,128]{2,1,0:T(8,128)}, u32[]{:S(2)}, u32[]{:S(2)}) collective-permute-start(f32[32,32,128]{2,1,0:T(8,128)S(1)} %get-tuple-element.60), channel_id=1, source_target_pairs={{0,12},{4,0},{8,4},{12,8},{1,13},{5,1},{9,5},{13,9},{2,14},{6,2},{... | collective-permute-start | bytes 1572872 | tf_op jit(solution)/shard_map/ppermute | solution.py:153
  185.8 5.7 %collective-permute-done.18.b = f32[32,32,128]{2,1,0:T(8,128)} collective-permute-done((f32[32,32,128]{2,1,0:T(8,128)}, f32[32,32,128]{2,1,0:T(8,128)}, u32[]{:S(2)}, u32[]{:S(2)}) %collective-permute-start.18) | collective-permute-done | bytes 524320 | tf_op jit(solution)/shard_map/ppermute | solution.py:152
  192.5 11.6 %collective-permute-done.20.d = f32[32,32,128]{2,1,0:T(8,128)} collective-permute-done((f32[32,32,128]{2,1,0:T(8,128)S(1)}, f32[32,32,128]{2,1,0:T(8,128)}, u32[]{:S(2)}, u32[]{:S(2)}) %collective-permute-start.20) | collective-permute-done | bytes 524320 | tf_op jit(solution)/shard_map/ppermute | solution.py:154
  204.1 2.5 add_pieces.7
  207.0 3.1 %collective-permute-start.22 = (f32[8,32,128]{2,1,0:T(8,128)}, f32[8,32,128]{2,1,0:T(8,128)S(1)}, u32[]{:S(2)}, u32[]{:S(2)}) collective-permute-start(f32[8,32,128]{2,1,0:T(8,128)} %get-tuple-element.64), channel_id=1, source_target_pairs={{0,3},{1,0},{2,1},{3,2},{4,7},{5,4},{6,5},{7,6},{8,11},{9,8},{10,9... | collective-permute-start | bytes 393224 | tf_op jit(solution)/shard_map/ppermute | solution.py:153
  211.8 8.1 %collective-permute-done.21.b = f32[8,32,128]{2,1,0:T(8,128)S(1)} collective-permute-done((f32[8,32,128]{2,1,0:T(8,128)}, f32[8,32,128]{2,1,0:T(8,128)S(1)}, u32[]{:S(2)}, u32[]{:S(2)}) %collective-permute-start.21) | collective-permute-done | bytes 131104 | tf_op jit(solution)/shard_map/ppermute | solution.py:152
  220.0 4.4 %collective-permute-done.23.d = f32[8,32,128]{2,1,0:T(8,128)S(1)} collective-permute-done((f32[8,32,128]{2,1,0:T(8,128)}, f32[8,32,128]{2,1,0:T(8,128)S(1)}, u32[]{:S(2)}, u32[]{:S(2)}) %collective-permute-start.23) | collective-permute-done | bytes 131104 | tf_op jit(solution)/shard_map/ppermute | solution.py:154
  226.9 4.5 %pad_maximum_fusion = f32[64,16384]{1,0:T(8,128)} fusion(f32[32,16384]{1,0:T(8,128)} %copy_bitcast_fusion.2, f32[32,16384]{1,0:T(8,128)} %copy_bitcast_fusion.3), kind=kLoop, calls=%fused_computation | loop fusion | flops 1048576 | bytes 8388608 | tf_op jit(solution)/shard_map/concatenate | solution.py:185
  233.2 32.2 %all-gather.15.cloned.1.call-done = f32[128,32,128]{2,1,0:T(8,128)} async-done(((f32[8,32,128]{2,1,0:T(8,128)}), f32[128,32,128]{2,1,0:T(8,128)}) %all-gather.15.cloned.1.call-update) | async-done | bytes 2097168 | tf_op jit(solution)/shard_map/all_gather | solution.py:178
  (131 shorter events, 61.6 us)
Async XLA Ops:
  7.2 117.1 %all-gather.9.cloned.1.call-start = ((), (), s32[]{:S(2)}) async-start(), calls=%async_computation | async-start | bytes 2228224 | tf_op jit(solution)/shard_map/all_gather | solution.py:178
  15.2 16.6 %collective-permute-start = (f32[32,32,128]{2,1,0:T(8,128)S(1)}, f32[32,32,128]{2,1,0:T(8,128)S(1)}, u32[]{:S(2)}, u32[]{:S(2)}) collective-permute-start(f32[32,32,128]{2,1,0:T(8,128)S(1)} %get-tuple-element.35), channel_id=1, source_target_pairs={{0,4},{4,8},{8,12},{12,0},{1,5},{5,9},{9,13},{13,1},{2,6},{6,10},{... | collective-permute-start | bytes 1572872 | tf_op jit(solution)/shard_map/ppermute | solution.py:152
  17.6 17.3 %collective-permute-start.1 = (f32[32,32,128]{2,1,0:T(8,128)S(1)}, f32[32,32,128]{2,1,0:T(8,128)S(1)}, u32[]{:S(2)}, u32[]{:S(2)}) collective-permute-start(f32[32,32,128]{2,1,0:T(8,128)S(1)} %get-tuple-element.36), channel_id=1, source_target_pairs={{0,12},{4,0},{8,4},{12,8},{1,13},{5,1},{9,5},{13,9},{2,14},{6,2},{... | collective-permute-start | bytes 1572872 | tf_op jit(solution)/shard_map/ppermute | solution.py:153
  20.9 24.0 %collective-permute-start.2 = (f32[32,32,128]{2,1,0:T(8,128)S(1)}, f32[32,32,128]{2,1,0:T(8,128)}, u32[]{:S(2)}, u32[]{:S(2)}) collective-permute-start(f32[32,32,128]{2,1,0:T(8,128)S(1)} %get-tuple-element.37), channel_id=1, source_target_pairs={{0,8},{4,12},{8,0},{12,4},{1,9},{5,13},{9,1},{13,5},{2,10},{6,14},... | collective-permute-start | bytes 1572872 | tf_op jit(solution)/shard_map/ppermute | solution.py:154
  44.9 22.6 %copy-start.17 = (s32[1,1,163]{2,1,0:T(1,128)S(1)}, s32[1,1,163]{2,1,0:T(1,128)}, u32[]{:S(2)}) copy-start(s32[1,1,163]{2,1,0:T(1,128)} %param.12) | copy-start | bytes 1960
  47.4 13.3 %collective-permute-start.3 = (f32[8,32,128]{2,1,0:T(8,128)}, f32[8,32,128]{2,1,0:T(8,128)S(1)}, u32[]{:S(2)}, u32[]{:S(2)}) collective-permute-start(f32[8,32,128]{2,1,0:T(8,128)} %get-tuple-element.39), channel_id=1, source_target_pairs={{0,1},{1,2},{2,3},{3,0},{4,5},{5,6},{6,7},{7,4},{8,9},{9,10},{10,1... | collective-permute-start | bytes 393224 | tf_op jit(solution)/shard_map/ppermute | solution.py:152
  50.9 13.1 %collective-permute-start.4 = (f32[8,32,128]{2,1,0:T(8,128)}, f32[8,32,128]{2,1,0:T(8,128)S(1)}, u32[]{:S(2)}, u32[]{:S(2)}) collective-permute-start(f32[8,32,128]{2,1,0:T(8,128)} %get-tuple-element.40), channel_id=1, source_target_pairs={{0,3},{1,0},{2,1},{3,2},{4,7},{5,4},{6,5},{7,6},{8,11},{9,8},{10,9... | collective-permute-start | bytes 393224 | tf_op jit(solution)/shard_map/ppermute | solution.py:153
  52.4 12.5 %collective-permute-start.5 = (f32[8,32,128]{2,1,0:T(8,128)}, f32[8,32,128]{2,1,0:T(8,128)S(1)}, u32[]{:S(2)}, u32[]{:S(2)}) collective-permute-start(f32[8,32,128]{2,1,0:T(8,128)} %get-tuple-element.41), channel_id=1, source_target_pairs={{0,2},{1,3},{2,0},{3,1},{4,6},{5,7},{6,4},{7,5},{8,10},{9,11},{10,... | collective-permute-start | bytes 393224 | tf_op jit(solution)/shard_map/ppermute | solution.py:154
  67.5 100.4 %all-gather.11.cloned.1.call-start = ((), (), s32[]{:S(2)}) async-start(), calls=%async_computation.1 | async-start | bytes 2228224 | tf_op jit(solution)/shard_map/all_gather | solution.py:178
  73.4 50.8 %copy-start.12 = (s32[3]{0:T(128)S(1)}, s32[3]{0:T(128)}, u32[]{:S(2)}) copy-start(s32[3]{0:T(128)} %copy-done.10) | copy-start | bytes 40
  73.4 11.6 %collective-permute-start.6 = (f32[32,32,128]{2,1,0:T(8,128)S(1)}, f32[32,32,128]{2,1,0:T(8,128)S(1)}, u32[]{:S(2)}, u32[]{:S(2)}) collective-permute-start(f32[32,32,128]{2,1,0:T(8,128)S(1)} %get-tuple-element.43), channel_id=1, source_target_pairs={{0,4},{4,8},{8,12},{12,0},{1,5},{5,9},{9,13},{13,1},{2,6},{6,10},{... | collective-permute-start | bytes 1572872 | tf_op jit(solution)/shard_map/ppermute | solution.py:152
  75.1 11.4 %collective-permute-start.7 = (f32[32,32,128]{2,1,0:T(8,128)S(1)}, f32[32,32,128]{2,1,0:T(8,128)S(1)}, u32[]{:S(2)}, u32[]{:S(2)}) collective-permute-start(f32[32,32,128]{2,1,0:T(8,128)S(1)} %get-tuple-element.44), channel_id=1, source_target_pairs={{0,12},{4,0},{8,4},{12,8},{1,13},{5,1},{9,5},{13,9},{2,14},{6,2},{... | collective-permute-start | bytes 1572872 | tf_op jit(solution)/shard_map/ppermute | solution.py:153
  76.4 24.8 %collective-permute-start.8 = (f32[32,32,128]{2,1,0:T(8,128)S(1)}, f32[32,32,128]{2,1,0:T(8,128)S(1)}, u32[]{:S(2)}, u32[]{:S(2)}) collective-permute-start(f32[32,32,128]{2,1,0:T(8,128)S(1)} %get-tuple-element.45), channel_id=1, source_target_pairs={{0,8},{4,12},{8,0},{12,4},{1,9},{5,13},{9,1},{13,5},{2,10},{6,14},... | collective-permute-start | bytes 1572872 | tf_op jit(solution)/shard_map/ppermute | solution.py:154
  104.4 13.9 %collective-permute-start.10 = (f32[8,32,128]{2,1,0:T(8,128)}, f32[8,32,128]{2,1,0:T(8,128)S(1)}, u32[]{:S(2)}, u32[]{:S(2)}) collective-permute-start(f32[8,32,128]{2,1,0:T(8,128)} %get-tuple-element.48), channel_id=1, source_target_pairs={{0,3},{1,0},{2,1},{3,2},{4,7},{5,4},{6,5},{7,6},{8,11},{9,8},{10,9... | collective-permute-start | bytes 393224 | tf_op jit(solution)/shard_map/ppermute | solution.py:153
  109.4 12.2 %collective-permute-start.11 = (f32[8,32,128]{2,1,0:T(8,128)}, f32[8,32,128]{2,1,0:T(8,128)S(1)}, u32[]{:S(2)}, u32[]{:S(2)}) collective-permute-start(f32[8,32,128]{2,1,0:T(8,128)} %get-tuple-element.49), channel_id=1, source_target_pairs={{0,2},{1,3},{2,0},{3,1},{4,6},{5,7},{6,4},{7,5},{8,10},{9,11},{10,... | collective-permute-start | bytes 393224 | tf_op jit(solution)/shard_map/ppermute | solution.py:154
  109.4 12.2 %collective-permute-start.9 = (f32[8,32,128]{2,1,0:T(8,128)}, f32[8,32,128]{2,1,0:T(8,128)S(1)}, u32[]{:S(2)}, u32[]{:S(2)}) collective-permute-start(f32[8,32,128]{2,1,0:T(8,128)} %get-tuple-element.47), channel_id=1, source_target_pairs={{0,1},{1,2},{2,3},{3,0},{4,5},{5,6},{6,7},{7,4},{8,9},{9,10},{10,1... | collective-permute-start | bytes 393224 | tf_op jit(solution)/shard_map/ppermute | solution.py:152
  124.2 107.3 %all-gather.13.cloned.1.call-start = ((), (), s32[]{:S(2)}) async-start(), calls=%async_computation.2 | async-start | bytes 2228224 | tf_op jit(solution)/shard_map/all_gather | solution.py:178
  129.7 38.2 %copy-start.13 = (s32[3]{0:T(128)S(1)}, s32[3]{0:T(128)}, u32[]{:S(2)}) copy-start(s32[3]{0:T(128)} %copy-done.10) | copy-start | bytes 40
  129.7 13.9 %collective-permute-start.12 = (f32[32,32,128]{2,1,0:T(8,128)S(1)}, f32[32,32,128]{2,1,0:T(8,128)S(1)}, u32[]{:S(2)}, u32[]{:S(2)}) collective-permute-start(f32[32,32,128]{2,1,0:T(8,128)S(1)} %get-tuple-element.51), channel_id=1, source_target_pairs={{0,4},{4,8},{8,12},{12,0},{1,5},{5,9},{9,13},{13,1},{2,6},{6,10},{... | collective-permute-start | bytes 1572872 | tf_op jit(solution)/shard_map/ppermute | solution.py:152
  131.3 12.3 %collective-permute-start.13 = (f32[32,32,128]{2,1,0:T(8,128)S(1)}, f32[32,32,128]{2,1,0:T(8,128)S(1)}, u32[]{:S(2)}, u32[]{:S(2)}) collective-permute-start(f32[32,32,128]{2,1,0:T(8,128)S(1)} %get-tuple-element.52), channel_id=1, source_target_pairs={{0,12},{4,0},{8,4},{12,8},{1,13},{5,1},{9,5},{13,9},{2,14},{6,2},{... | collective-permute-start | bytes 1572872 | tf_op jit(solution)/shard_map/ppermute | solution.py:153
  133.5 24.8 %collective-permute-start.14 = (f32[32,32,128]{2,1,0:T(8,128)S(1)}, f32[32,32,128]{2,1,0:T(8,128)S(1)}, u32[]{:S(2)}, u32[]{:S(2)}) collective-permute-start(f32[32,32,128]{2,1,0:T(8,128)S(1)} %get-tuple-element.53), channel_id=1, source_target_pairs={{0,8},{4,12},{8,0},{12,4},{1,9},{5,13},{9,1},{13,5},{2,10},{6,14},... | collective-permute-start | bytes 1572872 | tf_op jit(solution)/shard_map/ppermute | solution.py:154
  161.6 18.2 %collective-permute-start.15 = (f32[8,32,128]{2,1,0:T(8,128)}, f32[8,32,128]{2,1,0:T(8,128)S(1)}, u32[]{:S(2)}, u32[]{:S(2)}) collective-permute-start(f32[8,32,128]{2,1,0:T(8,128)} %get-tuple-element.55), channel_id=1, source_target_pairs={{0,1},{1,2},{2,3},{3,0},{4,5},{5,6},{6,7},{7,4},{8,9},{9,10},{10,1... | collective-permute-start | bytes 393224 | tf_op jit(solution)/shard_map/ppermute | solution.py:152
  161.6 20.1 %collective-permute-start.16 = (f32[8,32,128]{2,1,0:T(8,128)}, f32[8,32,128]{2,1,0:T(8,128)S(1)}, u32[]{:S(2)}, u32[]{:S(2)}) collective-permute-start(f32[8,32,128]{2,1,0:T(8,128)} %get-tuple-element.56), channel_id=1, source_target_pairs={{0,3},{1,0},{2,1},{3,2},{4,7},{5,4},{6,5},{7,6},{8,11},{9,8},{10,9... | collective-permute-start | bytes 393224 | tf_op jit(solution)/shard_map/ppermute | solution.py:153
  165.8 15.9 %collective-permute-start.17 = (f32[8,32,128]{2,1,0:T(8,128)}, f32[8,32,128]{2,1,0:T(8,128)S(1)}, u32[]{:S(2)}, u32[]{:S(2)}) collective-permute-start(f32[8,32,128]{2,1,0:T(8,128)} %get-tuple-element.57), channel_id=1, source_target_pairs={{0,2},{1,3},{2,0},{3,1},{4,6},{5,7},{6,4},{7,5},{8,10},{9,11},{10,... | collective-permute-start | bytes 393224 | tf_op jit(solution)/shard_map/ppermute | solution.py:154
  173.9 17.7 %collective-permute-start.18 = (f32[32,32,128]{2,1,0:T(8,128)}, f32[32,32,128]{2,1,0:T(8,128)}, u32[]{:S(2)}, u32[]{:S(2)}) collective-permute-start(f32[32,32,128]{2,1,0:T(8,128)} %get-tuple-element.59), channel_id=1, source_target_pairs={{0,4},{4,8},{8,12},{12,0},{1,5},{5,9},{9,13},{13,1},{2,6},{6,10},{... | collective-permute-start | bytes 1572872 | tf_op jit(solution)/shard_map/ppermute | solution.py:152
  175.6 16.9 %collective-permute-start.19 = (f32[32,32,128]{2,1,0:T(8,128)S(1)}, f32[32,32,128]{2,1,0:T(8,128)}, u32[]{:S(2)}, u32[]{:S(2)}) collective-permute-start(f32[32,32,128]{2,1,0:T(8,128)S(1)} %get-tuple-element.60), channel_id=1, source_target_pairs={{0,12},{4,0},{8,4},{12,8},{1,13},{5,1},{9,5},{13,9},{2,14},{6,2},{... | collective-permute-start | bytes 1572872 | tf_op jit(solution)/shard_map/ppermute | solution.py:153
  179.8 24.3 %collective-permute-start.20 = (f32[32,32,128]{2,1,0:T(8,128)S(1)}, f32[32,32,128]{2,1,0:T(8,128)}, u32[]{:S(2)}, u32[]{:S(2)}) collective-permute-start(f32[32,32,128]{2,1,0:T(8,128)S(1)} %get-tuple-element.61), channel_id=1, source_target_pairs={{0,8},{4,12},{8,0},{12,4},{1,9},{5,13},{9,1},{13,5},{2,10},{6,14},... | collective-permute-start | bytes 1572872 | tf_op jit(solution)/shard_map/ppermute | solution.py:154
  184.3 81.0 %all-gather.15.cloned.1.call-start = ((), (), s32[]{:S(2)}) async-start(), calls=%async_computation.3 | async-start | bytes 2228224 | tf_op jit(solution)/shard_map/all_gather | solution.py:178
  185.8 24.5 %copy-start.5 = (f32[128,32,128]{2,1,0:T(8,128)S(1)}, f32[128,32,128]{2,1,0:T(8,128)}, u32[]{:S(2)}) copy-start(f32[128,32,128]{2,1,0:T(8,128)} %all-gather.11.cloned.1.call-done.x_ref) | copy-start | bytes 6291460
  206.6 13.4 %collective-permute-start.21 = (f32[8,32,128]{2,1,0:T(8,128)}, f32[8,32,128]{2,1,0:T(8,128)S(1)}, u32[]{:S(2)}, u32[]{:S(2)}) collective-permute-start(f32[8,32,128]{2,1,0:T(8,128)} %get-tuple-element.63), channel_id=1, source_target_pairs={{0,1},{1,2},{2,3},{3,0},{4,5},{5,6},{6,7},{7,4},{8,9},{9,10},{10,1... | collective-permute-start | bytes 393224 | tf_op jit(solution)/shard_map/ppermute | solution.py:152
  207.0 12.9 %collective-permute-start.22 = (f32[8,32,128]{2,1,0:T(8,128)}, f32[8,32,128]{2,1,0:T(8,128)S(1)}, u32[]{:S(2)}, u32[]{:S(2)}) collective-permute-start(f32[8,32,128]{2,1,0:T(8,128)} %get-tuple-element.64), channel_id=1, source_target_pairs={{0,3},{1,0},{2,1},{3,2},{4,7},{5,4},{6,5},{7,6},{8,11},{9,8},{10,9... | collective-permute-start | bytes 393224 | tf_op jit(solution)/shard_map/ppermute | solution.py:153
  210.2 14.2 %collective-permute-start.23 = (f32[8,32,128]{2,1,0:T(8,128)}, f32[8,32,128]{2,1,0:T(8,128)S(1)}, u32[]{:S(2)}, u32[]{:S(2)}) collective-permute-start(f32[8,32,128]{2,1,0:T(8,128)} %get-tuple-element.65), channel_id=1, source_target_pairs={{0,2},{1,3},{2,0},{3,1},{4,6},{5,7},{6,4},{7,5},{8,10},{9,11},{10,... | collective-permute-start | bytes 393224 | tf_op jit(solution)/shard_map/ppermute | solution.py:154
  (34 other events, 188.4 us)
Sparse Core Ops, SparseCore 0:
  67.6 38.9 all-gather.8
  124.3 39.2 all-gather.10
  184.5 42.0 all-gather.12
  228.3 37.0 all-gather.14

commit v2 on v0

v2 whole, which is shorter than its diff:
```python
import functools

import jax
import jax.numpy as jnp
from jax import lax
from jax.experimental import pallas as pl
from jax.experimental.pallas import tpu as pltpu
from jax.sharding import Mesh, PartitionSpec as P

B = 128
BLK = 128
CAP = 163
CHUNK = 16
VEC = 64
SIZES = (16, 24, 24)
FIRST = tuple(sum(SIZES[:g]) for g in range(len(SIZES)))
ROW = ("x", "zl", "core")
COL = ("y", "zh")
ORDER = (
    "A0s", "B0s", "A0a", "C0s", "A0b", "B0a", "C0a", "A0c", "B0b", "C0b", "A0d", "B0c", "A0e",
    "C0c", "A0f", "B0d", "C0d", "A0g", "B0e", "C0e", "A1p", "C0f", "B0f", "A1a", "C0g", "B0g",
    "C1p", "A1b", "B1p", "A1c", "C1a", "A1d", "B1a", "C1b", "A1e", "B1b", "A1f", "C1c", "B1c",
    "C1d", "B1d", "C1e", "B1e", "C1f", "B1f", "A1g", "C1g", "A1m", "B1g", "C1m", "B1m",
)


def split(value):
    high = value.astype(jnp.bfloat16).astype(jnp.float32)
    return jnp.concatenate([high, value - high], axis=0).astype(jnp.bfloat16)


def ring_place(rel, core):
    one, three = 2 - core, 1 + core
    return jnp.where(rel == 0, 0, jnp.where(rel == 2, 3, jnp.where(rel == 1, one, three)))


def row_places(table):
    core, y, zh = (lax.axis_index(a) for a in ("core", "y", "zh"))
    for q in range(16):
        table[q] = ring_place(q // 4 ^ y, core) * 32 + ring_place(q % 4 ^ zh, core) * 8


def col_places(table, owners):
    x, zl, core = (lax.axis_index(a) for a in ROW)
    for r in range(16):
        side = r % 2
        spot = (side ^ core) * 8 + ring_place(r // 4 ^ x, 1 - side) * 2 + (r // 2 % 2 ^ zl)
        table[r] = spot * 8
        owners[spot] = r


def read_pattern(pattern, held, sems):
    copies = [pltpu.make_async_copy(p, h, sems.at[k]) for k, (p, h) in enumerate(zip(pattern, held))]
    for copy in copies:
        copy.start()
    return copies


def copy_tiles(tiles, held, sems):
    def one(c, size):
        span = pl.ds(c * CHUNK, size)
        return pltpu.make_async_copy(tiles.at[0, 0, span], held.at[span], sems.at[c])

    return one


def multiply(start, size, count, rows, cols, row_table, col_table, xs, held, acc):
    v = acc.shape[1]
    sums = []
    for u in range(size):
        col = cols[0, 0, start + u]
        if col_table is not None:
            col = col_table[col // 8] + col % 8
        p = lax.dot_general(
            xs[col], split(held[start + u]), (((1,), (1,)), ((), ())), preferred_element_type=jnp.float32
        )
        sums.append(p[:v, :B] + (p[v:, :B] + p[:v, B:]))
    for u in range(size):
        row = rows[0, 0, start + u]
        acc[jnp.where(start + u < count, row_table[row // 8] + row % 8, BLK)] += sums[u]


def over_chunks(count, work):
    whole = CAP // CHUNK

    def step(c, carry):
        work(c, CHUNK)
        return carry

    lax.fori_loop(0, jnp.minimum((count + CHUNK - 1) // CHUNK, whole), step, 0)
    if CAP % CHUNK:

        @pl.when(count > whole * CHUNK)
        def _():
            work(whole, CAP % CHUNK)


def send_out(acc, parts, outs, sems):
    copies = []
    for k, out in enumerate(outs):
        place = acc.at[pl.ds(k % 2 * 64, 64), pl.ds(sum(parts[: k // 2]), parts[k // 2])]
        copies.append(pltpu.make_async_copy(place, out, sems.at[k]))
    for copy in copies:
        copy.start()
    for copy in copies:
        copy.wait()


PATTERN = [pltpu.SMEM((1, 1, CAP), jnp.int32)] * 2
TABLES = [pltpu.SMEM((16,), jnp.int32)] * 3
TILES = [
    pltpu.VMEM((CAP, B, B), jnp.float32),
    pltpu.SemaphoreType.DMA((-(-CAP // CHUNK),)),
    pltpu.SemaphoreType.DMA((2,)),
]


def start_tiles(count, tile_copy):
    for c in range(-(-CAP // CHUNK)):

        @pl.when(c * CHUNK < count)
        def _():
            tile_copy(c, min(CHUNK, CAP - c * CHUNK)).start()


def first_kernel(live, rows_in, cols_in, tiles, panel_cur, panel_prev, *refs):
    n = 2 * len(SIZES)
    outs, (cur, prev), refs = refs[:n], refs[n : n + 2], refs[n + 2 :]
    (rows, cols), (row_table, _, _), (held, sems, p_sems) = refs[:2], refs[2:5], refs[5:8]
    xf, xp, xs, acc, x_sems, out_sems = refs[8:]
    mine = pl.multiple_of(((lax.axis_index("x") * 2 + lax.axis_index("zl")) * 2 + lax.axis_index("core")) * (8 * B), 8 * B)
    pattern = read_pattern((rows_in, cols_in), (rows, cols), p_sems)
    x_copy = pltpu.make_async_copy(panel_cur, xf, x_sems.at[0])
    p_copy = pltpu.make_async_copy(panel_prev.at[:, pl.ds(mine, 8 * B)], xp, x_sems.at[1])
    x_copy.start()
    count = live[0, 0]
    tile_copy = copy_tiles(tiles, held, sems)
    start_tiles(count, tile_copy)
    p_copy.start()
    row_places(row_table)
    acc[...] = jnp.zeros_like(acc)
    x_copy.wait()
    for c in range(BLK):
        xs[c] = split(xf[:, c * B : (c + 1) * B])
    for copy in pattern:
        copy.wait()
    for b in range(8):
        cur[b] = xf[:, pl.ds(mine + b * B, B)]

    def work(c, size):
        tile_copy(c, size).wait()
        multiply(c * CHUNK, size, count, rows, cols, row_table, None, xs, held, acc)

    over_chunks(count, work)
    p_copy.wait()
    for b in range(8):
        prev[b] = xp[:, b * B : (b + 1) * B]
    send_out(acc, SIZES, outs, out_sems)


def first_products(count, pattern, tiles, panel_cur, panel_prev):
    hbm = [pltpu.with_memory_space_constraint(a, pltpu.HBM) for a in (*pattern, tiles, panel_cur, panel_prev)]
    free = pl.BlockSpec(memory_space=pl.ANY)
    vmem = pl.BlockSpec(memory_space=pltpu.VMEM)
    n = 2 * len(SIZES)
    outs = pl.pallas_call(
        first_kernel,
        out_shape=[pltpu.VMEM((64, v, B), jnp.float32) for v in SIZES for _ in range(2)]
        + [pltpu.VMEM((8, VEC, B), jnp.float32)] * 2,
        in_specs=[pl.BlockSpec(memory_space=pltpu.SMEM)] + [free] * 5,
        out_specs=[free] * n + [vmem] * 2,
        scratch_shapes=PATTERN + TABLES + TILES + [
            pltpu.VMEM((VEC, BLK * B), jnp.float32),
            pltpu.VMEM((VEC, 8 * B), jnp.float32),
            pltpu.VMEM((BLK, 2 * VEC, B), jnp.bfloat16),
            pltpu.VMEM((BLK + 1, VEC, B), jnp.float32),
            pltpu.SemaphoreType.DMA((2,)),
            pltpu.SemaphoreType.DMA((n,)),
        ],
        compiler_params=pltpu.CompilerParams(vmem_limit_bytes=26 << 20),
        cost_estimate=pl.CostEstimate(flops=1, bytes_accessed=1, transcendentals=0),
        name="first",
    )(count, *hbm)
    return [outs[i : i + 2] for i in range(0, n, 2)], outs[n], outs[n + 1]


def lay_out(x_own, x_other, owners, flat):
    for k in range(BLK // 8):
        start = pl.multiple_of(owners[k] * (8 * B), 8 * B)
        ref = x_own if k < 8 else x_other
        for b in range(8):
            flat[:, pl.ds(start + b * B, B)] = ref[k % 8 * 8 + b]


def second_kernel(first, live, rows_in, cols_in, tiles, x_own, x_other, *refs):
    keep, send, panel = refs[-16:-13]
    refs = refs[-13:]
    (rows, cols), (row_table, col_table, owners), (held, sems, p_sems) = refs[:2], refs[2:5], refs[5:8]
    xs, acc, flat, sem, out_sems = refs[8:]
    v = acc.shape[1]
    pattern = read_pattern((rows_in, cols_in), (rows, cols), p_sems)
    count = live[0, 0]
    tile_copy = copy_tiles(tiles, held, sems)
    start_tiles(count, tile_copy)
    row_places(row_table)
    col_places(col_table, owners)
    lay_out(x_own, x_other, owners, flat)
    rows_copy = pltpu.make_async_copy(flat, panel.at[pl.ds(first, v)], sem)
    rows_copy.start()
    acc[...] = jnp.zeros_like(acc)
    for c in range(BLK):
        xs[c] = split((x_own if c < 64 else x_other)[c % 64])
    for copy in pattern:
        copy.wait()

    def work(c, size):
        tile_copy(c, size).wait()
        multiply(c * CHUNK, size, count, rows, cols, row_table, col_table, xs, held, acc)

    over_chunks(count, work)
    send_out(acc, (v,), (keep, send), out_sems)
    rows_copy.wait()


def second_products(count, pattern, tiles, x, panel, g):
    v = SIZES[g]
    free = pl.BlockSpec(memory_space=pl.ANY)
    vmem = pl.BlockSpec(memory_space=pltpu.VMEM)
    hbm = [pltpu.with_memory_space_constraint(a, pltpu.HBM) for a in (*pattern, tiles)]
    near = [pltpu.with_memory_space_constraint(a, pltpu.VMEM) for a in x]
    old = [] if panel is None else [panel]
    return pl.pallas_call(
        functools.partial(second_kernel, FIRST[g]),
        out_shape=[pltpu.VMEM((64, v, B), jnp.float32)] * 2 + [pltpu.HBM((VEC, BLK * B), jnp.float32)],
        in_specs=[pl.BlockSpec(memory_space=pltpu.SMEM)] + [free] * 3 + [vmem] * 2 + [free] * len(old),
        out_specs=[free] * 3,
        scratch_shapes=PATTERN + TABLES + TILES + [
            pltpu.VMEM((BLK, 2 * v, B), jnp.bfloat16),
            pltpu.VMEM((BLK + 1, v, B), jnp.float32),
            pltpu.VMEM((v, BLK * B), jnp.float32),
            pltpu.SemaphoreType.DMA,
            pltpu.SemaphoreType.DMA((2,)),
        ],
        input_output_aliases={6: 2} if old else {},
        compiler_params=pltpu.CompilerParams(vmem_limit_bytes=20 << 20),
        cost_estimate=pl.CostEstimate(flops=1, bytes_accessed=1, transcendentals=0),
        name="second",
    )(count, *hbm, *near, *old)


def assemble_kernel(first, v, x_own, x_other, *rest):
    out, table, owners, flat, sem = rest[-5:]
    col_places(table, owners)
    lay_out(x_own, x_other, owners, flat)
    copy = pltpu.make_async_copy(flat, out.at[pl.ds(first, v)], sem)
    copy.start()
    copy.wait()


def assemble(x, panel, g):
    v = SIZES[g]
    free = pl.BlockSpec(memory_space=pl.ANY)
    vmem = pl.BlockSpec(memory_space=pltpu.VMEM)
    held = [pltpu.with_memory_space_constraint(a, pltpu.VMEM) for a in x]
    old = [] if panel is None else [panel]
    return pl.pallas_call(
        functools.partial(assemble_kernel, FIRST[g], v),
        out_shape=pltpu.HBM((VEC, BLK * B), jnp.float32),
        in_specs=[vmem, vmem] + [free] * len(old),
        out_specs=free,
        scratch_shapes=TABLES[:2] + [pltpu.VMEM((v, BLK * B), jnp.float32), pltpu.SemaphoreType.DMA],
        input_output_aliases={2: 0} if old else {},
        compiler_params=pltpu.CompilerParams(vmem_limit_bytes=8 << 20),
        cost_estimate=pl.CostEstimate(flops=1, bytes_accessed=1, transcendentals=0),
        name="assemble",
    )(*held, *old)


def swap(value, axis):
    return lax.ppermute(value, axis, [(0, 1), (1, 0)])


def exchange(value, axis, turn):
    flip = {(0, 0): 1, (0, 1): 3, (1, 0): 3, (1, 1): 1}
    both, at = (("x", "core"), lambda c, i: i * 2 + c) if axis == "x" else (("core", axis), lambda c, i: c * 4 + i)
    pairs = [(at(c, i), at(c, i ^ flip[c, turn])) for c in range(2) for i in range(4)]
    return lax.ppermute(value, both, pairs)


def body(panel_prev, panel_cur, tiles, tile_rows, tile_cols, tile_count, center, halfwidth):
    pattern = (tile_rows, tile_cols)
    factor = 2.0 / halfwidth
    shares = {}
    panels = [None, None]

    first, cur, prev = first_products(tile_count, pattern, tiles, panel_cur, panel_prev)
    token = first[0][0]
    state = {(g, 0): [[keep], send] for g, (keep, send) in enumerate(first)}

    for event in ORDER:
        g, step, stage = ord(event[0]) - 65, int(event[1]), event[2]
        key = (g, step)
        if stage == "s":
            (state[key][1],), token = lax.optimization_barrier(((state[key][1],), token))
            continue
        if stage == "p":
            args, token = lax.optimization_barrier((state[g, 0], token))
            keep, token, panels[0] = second_products(tile_count, pattern, tiles, args, panels[0], g)
            state[key] = [[keep], token]
            continue
        if stage == "m":
            args, token = lax.optimization_barrier((state[key], token))
            panels[1] = token = assemble(args, panels[1], g)
            continue
        if stage in "abcd":
            kept, send = state[key]
            got = exchange(send, "y" if stage in "ab" else "zh", "abcd".index(stage) % 2)
        elif stage == "e":
            kept, got = [state[key]], swap(state[key], "zl")
        else:
            kept, got = [state[key]], exchange(state[key], "x", "fg".index(stage))
        (kept, got), token = lax.optimization_barrier(((kept, got), token))
        kept = [*kept, got]
        if stage in "abc":
            half = got.shape[0] // 2
            token = functools.reduce(jnp.add, [piece[half : 2 * half] for piece in kept])
            state[key] = [kept, token]
        elif stage == "d":
            mine = slice(FIRST[g], FIRST[g] + SIZES[g])
            now, before = (cur[:, mine], prev[:, mine]) if step == 0 else (shares[g], cur[:, mine])
            image = functools.reduce(jnp.add, [piece[: got.shape[0]] for piece in kept])
            state[key] = shares[g] = token = factor * (image - center * now) - before
        else:
            state[key] = token = jnp.concatenate(kept)
            if stage == "g":
                state[key] = [state[key], swap(state[key], "core")]
    return tuple(panels)


def solution(mesh):
    fine = Mesh(mesh.devices.reshape(4, 2, 2, 4, 4), ROW + COL)
    placed = (
        P(None, COL),
        P(None, COL),
        P(ROW, COL, None, None, None),
        P(ROW, COL, None),
        P(ROW, COL, None),
        P(ROW, COL),
        P(),
        P(),
    )
    return jax.shard_map(
        body, mesh=fine, in_specs=placed, out_specs=(P(None, COL), P(None, COL)), check_vma=False
    )
```

time: 688 us -> 199 us (0.29)
  waiting for transfers between devices: 507 us -> 69.9 us
  matrix products: 84.1 us -> 0 us
  starting transfers between devices: 13.3 us -> 90.4 us
  local copies, waits for them, and re-layouts: 47.9 us -> 0.55 us
  Pallas kernels: 0 us -> 20.8 us
  between operations: 16 us -> 3.37 us
    psum x2 -> x0, waiting for transfers between devices: 432 us -> none  [degree_step(): total = lax.psum(partial_value, 'col')]
    ppermute x0 -> x48, starting transfers between devices: none -> 90.4 us  [the longest x36 55.6 us: exchange(): return lax.ppermute(value, both, pairs)]
    dot_general x4 -> x0, matrix products: 84.1 us -> none  [the longest x2 46.7 us: tile_product(): jnp.einsum('vtk,tjk->tvj', chosen, tile_block, precision=lax.Precision.HI...]
    all_gather x2 -> x0, waiting for transfers between devices: 75.1 us -> none  [degree_step(): gathered = lax.all_gather(mine, 'row', axis=1, tiled=True)]
    ppermute x0 -> x48, waiting for transfers between devices: none -> 69.9 us  [the longest x36 61.9 us: exchange(): return lax.ppermute(value, both, pairs)]
    pallas_call x0 -> x7, Pallas kernels: none -> 20.8 us  [the longest x3 10.4 us: second_products(): pl.pallas_call(functools.partial(second_kernel, FIRST[g]), out_shape=[plt...]
    unnamed x6 -> x20, local copies, waits for them, and re-layouts: 15.2 us -> 0.26 us
    psum x2 -> x0, starting transfers between devices: 13.2 us -> none  [degree_step(): total = lax.psum(partial_value, 'col')]
  transfers between devices with their start and end apart: 4 -> 48, of which waited for: 4 -> 26; matrix products, arithmetic and copies ran while one was open for 0% -> 6% of each run, Pallas kernels for 0% -> 7%
where the time goes in v2:
time: 199 us; the launch traced here: 197 us
  starting transfers between devices  90.4 us (45%)
  waiting for transfers between devices  69.9 us (35%)
  Pallas kernels  20.8 us (10%)
  other arithmetic  11.7 us (6%)
  between operations  3.37 us (2%)
    ppermute x36, waiting for transfers between devices, exchange(): return lax.ppermute(value, both, pairs)  61.9 us
    ppermute x36, starting transfers between devices, exchange(): return lax.ppermute(value, both, pairs)  55.6 us
    ppermute x12, starting transfers between devices, swap(): return lax.ppermute(value, axis, [(0, 1), (1, 0)])  34.7 us
    pallas_call x3, Pallas kernels, second_products(): pl.pallas_call(functools.partial(second_kernel, FIRST[g]), out_shape=[plt...  10.4 us
    add x18, other arithmetic, body(): token = functools.reduce(jnp.add, [piece[half:2 * half] for piece in kept])  8.77 us
    ppermute x12, waiting for transfers between devices, swap(): return lax.ppermute(value, axis, [(0, 1), (1, 0)])  7.98 us
    pallas_call x1, Pallas kernels, first_products(): pl.pallas_call(first_kernel, out_shape=[pltpu.VMEM((64, v, B), jnp.float3...  6.35 us
    pallas_call x3, Pallas kernels, assemble(): pl.pallas_call(functools.partial(assemble_kernel, FIRST[g], v), out_shape...  4.03 us
  transfers between devices with their start and end apart: 48, of which 26 were waited for; matrix products, arithmetic and copies ran while one was open for 6% of the time, Pallas kernels for 7%

profile of v2, /device:TPU:1, one launch (start us, length us, event | category | flops | bytes accessed | tf_op | source)
XLA Modules:
  0.0 196.7 jit_solution(14382612119138041968)
XLA Ops:
  1.3 6.4 %first.1 = (f32[64,16,128]{2,1,0:T(8,128)S(1)}, f32[64,16,128]{2,1,0:T(8,128)S(1)}, f32[64,24,128]{2,1,0:T(8,128)S(1)}, f32[64,24,128]{2,1,0:T(8,128)}, f32[64,2...) custom-call(s32[1,1]{1,0:T(1,128)S(6)} %copy.36.live, ...), custom_call_target="tpu_custom_call" | custom-call | flops 1 | bytes 1 | tf_op jit(solution)/shard_map/first/pallas_call | solution.py:166
  7.6 6.7 %collective-permute-start.1 = (f32[64,16,128]{2,1,0:T(8,128)S(1)}, f32[64,16,128]{2,1,0:T(8,128)S(1)}, u32[]{:S(2)}, u32[]{:S(2)}) collective-permute-start(f32[64,16,128]{2,1,0:T(8,128)S(1)} %get-tuple-element.157), channel_id=1, source_target_pairs={{0,4},{4,0},{8,12},{12,8},{16,28},{20,24},{24,20},{28,16},{1,5},{5... | collective-permute-start | bytes 1572872 | tf_op jit(solution)/shard_map/ppermute | solution.py:287
  14.4 6.5 %collective-permute-done.1 = f32[64,16,128]{2,1,0:T(8,128)S(1)} collective-permute-done((f32[64,16,128]{2,1,0:T(8,128)S(1)}, f32[64,16,128]{2,1,0:T(8,128)S(1)}, u32[]{:S(2)}, u32[]{:S(2)}) %collective-permute-start.1) | collective-permute-done | bytes 524320 | tf_op jit(solution)/shard_map/ppermute | solution.py:287
  21.7 2.7 %collective-permute-start.5 = (f32[64,24,128]{2,1,0:T(8,128)S(1)}, f32[64,24,128]{2,1,0:T(8,128)}, u32[]{:S(2)}, u32[]{:S(2)}) collective-permute-start(f32[64,24,128]{2,1,0:T(8,128)S(1)} %get-tuple-element.167), channel_id=1, source_target_pairs={{0,4},{4,0},{8,12},{12,8},{16,28},{20,24},{24,20},{28,16},{1,5},{5... | collective-permute-start | bytes 2359304 | tf_op jit(solution)/shard_map/ppermute | solution.py:287
  25.7 7.4 %collective-permute-done.2 = f32[32,16,128]{2,1,0:T(8,128)} collective-permute-done((f32[32,16,128]{2,1,0:T(8,128)}, f32[32,16,128]{2,1,0:T(8,128)}, u32[]{:S(2)}, u32[]{:S(2)}) %collective-permute-start.2) | collective-permute-done | bytes 262176 | tf_op jit(solution)/shard_map/ppermute | solution.py:287
  34.1 2.5 %collective-permute-start.4 = (f32[16,16,128]{2,1,0:T(8,128)S(1)}, f32[16,16,128]{2,1,0:T(8,128)S(1)}, u32[]{:S(2)}, u32[]{:S(2)}) collective-permute-start(f32[16,16,128]{2,1,0:T(8,128)S(1)} %slice_add_fusion.11), channel_id=1, source_target_pairs={{0,1},{1,0},{2,3},{3,2},{16,19},{17,18},{18,17},{19,16},{4,5},{5,4... | collective-permute-start | bytes 393224 | tf_op jit(solution)/shard_map/ppermute | solution.py:287
  46.1 9.9 %collective-permute-start.6 = (f32[16,24,128]{2,1,0:T(8,128)S(1)}, f32[16,24,128]{2,1,0:T(8,128)S(1)}, u32[]{:S(2)}, u32[]{:S(2)}) collective-permute-start(f32[16,24,128]{2,1,0:T(8,128)S(1)} %slice_add_fusion.9), channel_id=1, source_target_pairs={{0,1},{1,0},{2,3},{3,2},{16,19},{17,18},{18,17},{19,16},{4,5},{5,4... | collective-permute-start | bytes 589832 | tf_op jit(solution)/shard_map/ppermute | solution.py:287
  58.0 2.0 %collective-permute-start.10 = (f32[8,16,128]{2,1,0:T(8,128)S(1)}, f32[8,16,128]{2,1,0:T(8,128)S(1)}, u32[]{:S(2)}, u32[]{:S(2)}) collective-permute-start(f32[8,16,128]{2,1,0:T(8,128)S(1)} %slice_subtract_fusion.2), channel_id=1, source_target_pairs={{0,32},{32,0},{1,33},{33,1},{2,34},{34,2},{3,35},{35,3},{4,36},{36... | collective-permute-start | bytes 196616 | tf_op jit(solution)/shard_map/ppermute | solution.py:280
  62.5 3.7 %collective-permute-done.10 = f32[8,16,128]{2,1,0:T(8,128)S(1)} collective-permute-done((f32[8,16,128]{2,1,0:T(8,128)S(1)}, f32[8,16,128]{2,1,0:T(8,128)S(1)}, u32[]{:S(2)}, u32[]{:S(2)}) %collective-permute-start.10) | collective-permute-done | bytes 65568 | tf_op jit(solution)/shard_map/ppermute | solution.py:280
  66.3 4.6 %collective-permute-start.11 = (f32[16,16,128]{2,1,0:T(8,128)S(1)}, f32[16,16,128]{2,1,0:T(8,128)S(1)}, u32[]{:S(2)}, u32[]{:S(2)}) collective-permute-start(f32[16,16,128]{2,1,0:T(8,128)S(1)} %constant_dynamic-update-slice_fusion), channel_id=1, source_target_pairs={{0,64},{64,0},{128,192},{192,128},{16,208},{80,144},{144,80},{208,... | collective-permute-start | bytes 393224 | tf_op jit(solution)/shard_map/ppermute | solution.py:287
  79.1 7.1 %collective-permute-start.19 = (f32[64,16,128]{2,1,0:T(8,128)S(1)}, f32[64,16,128]{2,1,0:T(8,128)S(1)}, u32[]{:S(2)}, u32[]{:S(2)}) collective-permute-start(f32[64,16,128]{2,1,0:T(8,128)S(1)} %constant_dynamic-update-slice_fusion.4.x_own), channel_id=1, source_target_pairs={{0,16},{16,0},{1,17},{17,1},{2,18},{18,2},{3,19},{19,3},{4,20},{20... | collective-permute-start | bytes 1572872 | tf_op jit(solution)/shard_map/ppermute | solution.py:280
  87.7 3.4 %second.3 = (f32[64,16,128]{2,1,0:T(8,128)S(1)}, f32[64,16,128]{2,1,0:T(8,128)S(1)}, f32[64,16384]{1,0:T(8,128)}) custom-call(s32[1,1]{1,0:T(1,128)S(6)} %copy.36.live, s32[1,1,163]{2,1,0:T(1,128)} %rows_in.7, s32[1,1,163]{2,1,0:T(1,128)} %cols_in.7, f32[1,1,163,128,128]{4,3,2,1,0:T(8,128)} %tiles.7, ...), custom_call_target="tpu_custom_call" | custom-call | flops 1 | bytes 1 | tf_op jit(solution)/shard_map/second/pallas_call | solution.py:232
  91.2 3.8 %collective-permute-start.22 = (f32[64,16,128]{2,1,0:T(8,128)S(1)}, f32[64,16,128]{2,1,0:T(8,128)S(1)}, u32[]{:S(2)}, u32[]{:S(2)}) collective-permute-start(f32[64,16,128]{2,1,0:T(8,128)S(1)} %get-tuple-element.217), channel_id=1, source_target_pairs={{0,4},{4,0},{8,12},{12,8},{16,28},{20,24},{24,20},{28,16},{1,5},{5... | collective-permute-start | bytes 1572872 | tf_op jit(solution)/shard_map/ppermute | solution.py:287
  95.1 6.3 %collective-permute-done.16 = f32[16,24,128]{2,1,0:T(8,128)S(1)} collective-permute-done((f32[16,24,128]{2,1,0:T(8,128)S(1)}, f32[16,24,128]{2,1,0:T(8,128)S(1)}, u32[]{:S(2)}, u32[]{:S(2)}) %collective-permute-start.16) | collective-permute-done | bytes 196640 | tf_op jit(solution)/shard_map/ppermute | solution.py:287
  102.4 3.3 %collective-permute-start.25 = (f32[64,24,128]{2,1,0:T(8,128)S(1)}, f32[64,24,128]{2,1,0:T(8,128)S(1)}, u32[]{:S(2)}, u32[]{:S(2)}) collective-permute-start(f32[64,24,128]{2,1,0:T(8,128)S(1)} %constant_dynamic-update-slice_fusion.14.x_own), channel_id=1, source_target_pairs={{0,16},{16,0},{1,17},{17,1},{2,18},{18,2},{3,19},{19,3},{4,20},{20... | collective-permute-start | bytes 2359304 | tf_op jit(solution)/shard_map/ppermute | solution.py:280
  105.7 2.7 %collective-permute-done.20 = f32[32,24,128]{2,1,0:T(8,128)S(1)} collective-permute-done((f32[32,24,128]{2,1,0:T(8,128)S(1)}, f32[32,24,128]{2,1,0:T(8,128)S(1)}, u32[]{:S(2)}, u32[]{:S(2)}) %collective-permute-start.20) | collective-permute-done | bytes 393248 | tf_op jit(solution)/shard_map/ppermute | solution.py:287
  108.5 2.1 %collective-permute-start.23 = (f32[64,24,128]{2,1,0:T(8,128)S(1)}, f32[64,24,128]{2,1,0:T(8,128)S(1)}, u32[]{:S(2)}, u32[]{:S(2)}) collective-permute-start(f32[64,24,128]{2,1,0:T(8,128)S(1)} %constant_dynamic-update-slice_fusion.16.x_own), channel_id=1, source_target_pairs={{0,16},{16,0},{1,17},{17,1},{2,18},{18,2},{3,19},{19,3},{4,20},{20... | collective-permute-start | bytes 2359304 | tf_op jit(solution)/shard_map/ppermute | solution.py:280
  111.3 3.5 %second.4 = (f32[64,24,128]{2,1,0:T(8,128)S(1)}, f32[64,24,128]{2,1,0:T(8,128)S(1)}, f32[64,16384]{1,0:T(8,128)}) custom-call(s32[1,1]{1,0:T(1,128)S(6)} %copy.36.live, s32[1,1,163]{2,1,0:T(1,128)} %rows_in.7, s32[1,1,163]{2,1,0:T(1,128)} %cols_in.7, f32[1,1,163,128,128]{4,3,2,1,0:T(8,128)} %tiles.7, ...), custom_call_target="tpu_custom_call", output_to_operand_aliasing={{2}: (6, {})} | custom-call | flops 1 | bytes 1 | tf_op jit(solution)/shard_map/second/pallas_call | solution.py:232
  114.8 5.7 %collective-permute-start.29 = (f32[64,24,128]{2,1,0:T(8,128)S(1)}, f32[64,24,128]{2,1,0:T(8,128)S(1)}, u32[]{:S(2)}, u32[]{:S(2)}) collective-permute-start(f32[64,24,128]{2,1,0:T(8,128)S(1)} %get-tuple-element.232), channel_id=1, source_target_pairs={{0,4},{4,0},{8,12},{12,8},{16,28},{20,24},{24,20},{28,16},{1,5},{5... | collective-permute-start | bytes 2359304 | tf_op jit(solution)/shard_map/ppermute | solution.py:287
  120.7 3.5 %second.5 = (f32[64,24,128]{2,1,0:T(8,128)S(1)}, f32[64,24,128]{2,1,0:T(8,128)S(1)}, f32[64,16384]{1,0:T(8,128)}) custom-call(s32[1,1]{1,0:T(1,128)S(6)} %copy.36.live, s32[1,1,163]{2,1,0:T(1,128)} %rows_in.7, s32[1,1,163]{2,1,0:T(1,128)} %cols_in.7, f32[1,1,163,128,128]{4,3,2,1,0:T(8,128)} %tiles.7, ...), custom_call_target="tpu_custom_call", output_to_operand_aliasing={{2}: (6, {})} | custom-call | flops 1 | bytes 1 | tf_op jit(solution)/shard_map/second/pallas_call | solution.py:232
  124.2 2.1 %collective-permute-start.26 = (f32[64,24,128]{2,1,0:T(8,128)S(1)}, f32[64,24,128]{2,1,0:T(8,128)S(1)}, u32[]{:S(2)}, u32[]{:S(2)}) collective-permute-start(f32[64,24,128]{2,1,0:T(8,128)S(1)} %get-tuple-element.241), channel_id=1, source_target_pairs={{0,4},{4,0},{8,12},{12,8},{16,28},{20,24},{24,20},{28,16},{1,5},{5... | collective-permute-start | bytes 2359304 | tf_op jit(solution)/shard_map/ppermute | solution.py:287
  130.0 2.3 %collective-permute-done.28 = f32[8,16,128]{2,1,0:T(8,128)S(1)} collective-permute-done((f32[8,16,128]{2,1,0:T(8,128)S(1)}, f32[8,16,128]{2,1,0:T(8,128)S(1)}, u32[]{:S(2)}, u32[]{:S(2)}) %collective-permute-start.28) | collective-permute-done | bytes 65568 | tf_op jit(solution)/shard_map/ppermute | solution.py:287
  132.5 9.6 %collective-permute-done.26 = f32[64,24,128]{2,1,0:T(8,128)S(1)} collective-permute-done((f32[64,24,128]{2,1,0:T(8,128)S(1)}, f32[64,24,128]{2,1,0:T(8,128)S(1)}, u32[]{:S(2)}, u32[]{:S(2)}) %collective-permute-start.26) | collective-permute-done | bytes 786464 | tf_op jit(solution)/shard_map/ppermute | solution.py:287
  142.3 2.1 %collective-permute-start.34 = (f32[16,24,128]{2,1,0:T(8,128)S(1)}, f32[16,24,128]{2,1,0:T(8,128)S(1)}, u32[]{:S(2)}, u32[]{:S(2)}) collective-permute-start(f32[16,24,128]{2,1,0:T(8,128)S(1)} %slice_add_fusion.7), channel_id=1, source_target_pairs={{0,1},{1,0},{2,3},{3,2},{16,19},{17,18},{18,17},{19,16},{4,5},{5,4... | collective-permute-start | bytes 589832 | tf_op jit(solution)/shard_map/ppermute | solution.py:287
  144.5 4.7 %collective-permute-done.30 = f32[32,24,128]{2,1,0:T(8,128)S(1)} collective-permute-done((f32[32,24,128]{2,1,0:T(8,128)S(1)}, f32[32,24,128]{2,1,0:T(8,128)S(1)}, u32[]{:S(2)}, u32[]{:S(2)}) %collective-permute-start.30) | collective-permute-done | bytes 393248 | tf_op jit(solution)/shard_map/ppermute | solution.py:287
  150.9 2.8 %collective-permute-start.37 = (f32[8,24,128]{2,1,0:T(8,128)S(1)}, f32[8,24,128]{2,1,0:T(8,128)S(1)}, u32[]{:S(2)}, u32[]{:S(2)}) collective-permute-start(f32[8,24,128]{2,1,0:T(8,128)S(1)} %slice_add_fusion.13), channel_id=1, source_target_pairs={{0,3},{1,2},{2,1},{3,0},{16,17},{17,16},{18,19},{19,18},{4,7},{5,6... | collective-permute-start | bytes 294920 | tf_op jit(solution)/shard_map/ppermute | solution.py:287
  153.7 2.8 %collective-permute-done.33 = f32[16,24,128]{2,1,0:T(8,128)S(1)} collective-permute-done((f32[16,24,128]{2,1,0:T(8,128)S(1)}, f32[16,24,128]{2,1,0:T(8,128)S(1)}, u32[]{:S(2)}, u32[]{:S(2)}) %collective-permute-start.33) | collective-permute-done | bytes 196640 | tf_op jit(solution)/shard_map/ppermute | solution.py:287
  157.2 3.2 %collective-permute-done.37 = f32[8,24,128]{2,1,0:T(8,128)S(1)} collective-permute-done((f32[8,24,128]{2,1,0:T(8,128)S(1)}, f32[8,24,128]{2,1,0:T(8,128)S(1)}, u32[]{:S(2)}, u32[]{:S(2)}) %collective-permute-start.37) | collective-permute-done | bytes 98336 | tf_op jit(solution)/shard_map/ppermute | solution.py:287
  166.1 2.8 %collective-permute-start.40 = (f32[16,24,128]{2,1,0:T(8,128)S(1)}, f32[16,24,128]{2,1,0:T(8,128)S(1)}, u32[]{:S(2)}, u32[]{:S(2)}) collective-permute-start(f32[16,24,128]{2,1,0:T(8,128)S(1)} %constant_dynamic-update-slice_fusion.24), channel_id=1, source_target_pairs={{0,64},{64,0},{128,192},{192,128},{16,208},{80,144},{144,80},{208,... | collective-permute-start | bytes 589832 | tf_op jit(solution)/shard_map/ppermute | solution.py:287
  172.1 9.9 %collective-permute-start.44 = (f32[64,16,128]{2,1,0:T(8,128)S(1)}, f32[64,16,128]{2,1,0:T(8,128)S(1)}, u32[]{:S(2)}, u32[]{:S(2)}) collective-permute-start(f32[64,16,128]{2,1,0:T(8,128)S(1)} %constant_dynamic-update-slice_fusion.30.x_own), channel_id=1, source_target_pairs={{0,16},{16,0},{1,17},{17,1},{2,18},{18,2},{3,19},{19,3},{4,20},{20... | collective-permute-start | bytes 1572872 | tf_op jit(solution)/shard_map/ppermute | solution.py:280
  182.0 6.9 %collective-permute-start.47 = (f32[64,24,128]{2,1,0:T(8,128)S(1)}, f32[64,24,128]{2,1,0:T(8,128)S(1)}, u32[]{:S(2)}, u32[]{:S(2)}) collective-permute-start(f32[64,24,128]{2,1,0:T(8,128)S(1)} %constant_dynamic-update-slice_fusion.32.x_own), channel_id=1, source_target_pairs={{0,16},{16,0},{1,17},{17,1},{2,18},{18,2},{3,19},{19,3},{4,20},{20... | collective-permute-start | bytes 2359304 | tf_op jit(solution)/shard_map/ppermute | solution.py:280
  190.2 2.9 %collective-permute-start.46 = (f32[64,24,128]{2,1,0:T(8,128)S(1)}, f32[64,24,128]{2,1,0:T(8,128)S(1)}, u32[]{:S(2)}, u32[]{:S(2)}) collective-permute-start(f32[64,24,128]{2,1,0:T(8,128)S(1)} %constant_dynamic-update-slice_fusion.34.x_own), channel_id=1, source_target_pairs={{0,16},{16,0},{1,17},{17,1},{2,18},{18,2},{3,19},{19,3},{4,20},{20... | collective-permute-start | bytes 2359304 | tf_op jit(solution)/shard_map/ppermute | solution.py:280
  (133 shorter events, 47.5 us)
Async XLA Ops:
  7.6 13.3 %collective-permute-start.1 = (f32[64,16,128]{2,1,0:T(8,128)S(1)}, f32[64,16,128]{2,1,0:T(8,128)S(1)}, u32[]{:S(2)}, u32[]{:S(2)}) collective-permute-start(f32[64,16,128]{2,1,0:T(8,128)S(1)} %get-tuple-element.157), channel_id=1, source_target_pairs={{0,4},{4,0},{8,12},{12,8},{16,28},{20,24},{24,20},{28,16},{1,5},{5... | collective-permute-start | bytes 1572872 | tf_op jit(solution)/shard_map/ppermute | solution.py:287
  14.3 22.2 %collective-permute-start = (f32[64,24,128]{2,1,0:T(8,128)}, f32[64,24,128]{2,1,0:T(8,128)}, u32[]{:S(2)}, u32[]{:S(2)}) collective-permute-start(f32[64,24,128]{2,1,0:T(8,128)} %get-tuple-element.154), channel_id=1, source_target_pairs={{0,4},{4,0},{8,12},{12,8},{16,28},{20,24},{24,20},{28,16},{1,5},{5... | collective-permute-start | bytes 2359304 | tf_op jit(solution)/shard_map/ppermute | solution.py:287
  21.7 19.0 %collective-permute-start.5 = (f32[64,24,128]{2,1,0:T(8,128)S(1)}, f32[64,24,128]{2,1,0:T(8,128)}, u32[]{:S(2)}, u32[]{:S(2)}) collective-permute-start(f32[64,24,128]{2,1,0:T(8,128)S(1)} %get-tuple-element.167), channel_id=1, source_target_pairs={{0,4},{4,0},{8,12},{12,8},{16,28},{20,24},{24,20},{28,16},{1,5},{5... | collective-permute-start | bytes 2359304 | tf_op jit(solution)/shard_map/ppermute | solution.py:287
  24.4 8.7 %collective-permute-start.2 = (f32[32,16,128]{2,1,0:T(8,128)}, f32[32,16,128]{2,1,0:T(8,128)}, u32[]{:S(2)}, u32[]{:S(2)}) collective-permute-start(f32[32,16,128]{2,1,0:T(8,128)} %slice_add_fusion.5), channel_id=1, source_target_pairs={{0,12},{4,8},{8,4},{12,0},{16,20},{20,16},{24,28},{28,24},{1,13},{... | collective-permute-start | bytes 786440 | tf_op jit(solution)/shard_map/ppermute | solution.py:287
  34.1 7.8 %collective-permute-start.4 = (f32[16,16,128]{2,1,0:T(8,128)S(1)}, f32[16,16,128]{2,1,0:T(8,128)S(1)}, u32[]{:S(2)}, u32[]{:S(2)}) collective-permute-start(f32[16,16,128]{2,1,0:T(8,128)S(1)} %slice_add_fusion.11), channel_id=1, source_target_pairs={{0,1},{1,0},{2,3},{3,2},{16,19},{17,18},{18,17},{19,16},{4,5},{5,4... | collective-permute-start | bytes 393224 | tf_op jit(solution)/shard_map/ppermute | solution.py:287
  37.6 7.6 %collective-permute-start.3 = (f32[32,24,128]{2,1,0:T(8,128)S(1)}, f32[32,24,128]{2,1,0:T(8,128)S(1)}, u32[]{:S(2)}, u32[]{:S(2)}) collective-permute-start(f32[32,24,128]{2,1,0:T(8,128)S(1)} %slice_add_fusion.3), channel_id=1, source_target_pairs={{0,12},{4,8},{8,4},{12,0},{16,20},{20,16},{24,28},{28,24},{1,13},{... | collective-permute-start | bytes 1179656 | tf_op jit(solution)/shard_map/ppermute | solution.py:287
  41.8 14.3 %collective-permute-start.8 = (f32[32,24,128]{2,1,0:T(8,128)S(1)}, f32[32,24,128]{2,1,0:T(8,128)S(1)}, u32[]{:S(2)}, u32[]{:S(2)}) collective-permute-start(f32[32,24,128]{2,1,0:T(8,128)S(1)} %slice_add_fusion.2), channel_id=1, source_target_pairs={{0,12},{4,8},{8,4},{12,0},{16,20},{20,16},{24,28},{28,24},{1,13},{... | collective-permute-start | bytes 1179656 | tf_op jit(solution)/shard_map/ppermute | solution.py:287
  42.8 14.3 %collective-permute-start.7 = (f32[8,16,128]{2,1,0:T(8,128)S(1)}, f32[8,16,128]{2,1,0:T(8,128)S(1)}, u32[]{:S(2)}, u32[]{:S(2)}) collective-permute-start(f32[8,16,128]{2,1,0:T(8,128)S(1)} %slice_add_fusion.17), channel_id=1, source_target_pairs={{0,3},{1,2},{2,1},{3,0},{16,17},{17,16},{18,19},{19,18},{4,7},{5,6... | collective-permute-start | bytes 196616 | tf_op jit(solution)/shard_map/ppermute | solution.py:287
  46.1 13.9 %collective-permute-start.6 = (f32[16,24,128]{2,1,0:T(8,128)S(1)}, f32[16,24,128]{2,1,0:T(8,128)S(1)}, u32[]{:S(2)}, u32[]{:S(2)}) collective-permute-start(f32[16,24,128]{2,1,0:T(8,128)S(1)} %slice_add_fusion.9), channel_id=1, source_target_pairs={{0,1},{1,0},{2,3},{3,2},{16,19},{17,18},{18,17},{19,16},{4,5},{5,4... | collective-permute-start | bytes 589832 | tf_op jit(solution)/shard_map/ppermute | solution.py:287
  57.0 13.9 %collective-permute-start.12 = (f32[16,24,128]{2,1,0:T(8,128)S(1)}, f32[16,24,128]{2,1,0:T(8,128)S(1)}, u32[]{:S(2)}, u32[]{:S(2)}) collective-permute-start(f32[16,24,128]{2,1,0:T(8,128)S(1)} %slice_add_fusion.8), channel_id=1, source_target_pairs={{0,1},{1,0},{2,3},{3,2},{16,19},{17,18},{18,17},{19,16},{4,5},{5,4... | collective-permute-start | bytes 589832 | tf_op jit(solution)/shard_map/ppermute | solution.py:287
  58.0 8.2 %collective-permute-start.10 = (f32[8,16,128]{2,1,0:T(8,128)S(1)}, f32[8,16,128]{2,1,0:T(8,128)S(1)}, u32[]{:S(2)}, u32[]{:S(2)}) collective-permute-start(f32[8,16,128]{2,1,0:T(8,128)S(1)} %slice_subtract_fusion.2), channel_id=1, source_target_pairs={{0,32},{32,0},{1,33},{33,1},{2,34},{34,2},{3,35},{35,3},{4,36},{36... | collective-permute-start | bytes 196616 | tf_op jit(solution)/shard_map/ppermute | solution.py:280
  60.9 12.4 %collective-permute-start.9 = (f32[8,24,128]{2,1,0:T(8,128)S(1)}, f32[8,24,128]{2,1,0:T(8,128)S(1)}, u32[]{:S(2)}, u32[]{:S(2)}) collective-permute-start(f32[8,24,128]{2,1,0:T(8,128)S(1)} %slice_add_fusion.15), channel_id=1, source_target_pairs={{0,3},{1,2},{2,1},{3,0},{16,17},{17,16},{18,19},{19,18},{4,7},{5,6... | collective-permute-start | bytes 294920 | tf_op jit(solution)/shard_map/ppermute | solution.py:287
  74.3 11.9 %collective-permute-start.13 = (f32[8,24,128]{2,1,0:T(8,128)S(1)}, f32[8,24,128]{2,1,0:T(8,128)S(1)}, u32[]{:S(2)}, u32[]{:S(2)}) collective-permute-start(f32[8,24,128]{2,1,0:T(8,128)S(1)} %slice_subtract_fusion.1), channel_id=1, source_target_pairs={{0,32},{32,0},{1,33},{33,1},{2,34},{34,2},{3,35},{35,3},{4,36},{36... | collective-permute-start | bytes 294920 | tf_op jit(solution)/shard_map/ppermute | solution.py:280
  77.1 9.1 %collective-permute-start.17 = (f32[8,24,128]{2,1,0:T(8,128)S(1)}, f32[8,24,128]{2,1,0:T(8,128)S(1)}, u32[]{:S(2)}, u32[]{:S(2)}) collective-permute-start(f32[8,24,128]{2,1,0:T(8,128)S(1)} %slice_subtract_fusion), channel_id=1, source_target_pairs={{0,32},{32,0},{1,33},{33,1},{2,34},{34,2},{3,35},{35,3},{4,36},{36... | collective-permute-start | bytes 294920 | tf_op jit(solution)/shard_map/ppermute | solution.py:280
  79.1 8.7 %collective-permute-start.19 = (f32[64,16,128]{2,1,0:T(8,128)S(1)}, f32[64,16,128]{2,1,0:T(8,128)S(1)}, u32[]{:S(2)}, u32[]{:S(2)}) collective-permute-start(f32[64,16,128]{2,1,0:T(8,128)S(1)} %constant_dynamic-update-slice_fusion.4.x_own), channel_id=1, source_target_pairs={{0,16},{16,0},{1,17},{17,1},{2,18},{18,2},{3,19},{19,3},{4,20},{20... | collective-permute-start | bytes 1572872 | tf_op jit(solution)/shard_map/ppermute | solution.py:280
  86.3 8.7 %collective-permute-start.18 = (f32[16,24,128]{2,1,0:T(8,128)S(1)}, f32[16,24,128]{2,1,0:T(8,128)S(1)}, u32[]{:S(2)}, u32[]{:S(2)}) collective-permute-start(f32[16,24,128]{2,1,0:T(8,128)S(1)} %constant_dynamic-update-slice_fusion.8), channel_id=1, source_target_pairs={{0,64},{64,0},{128,192},{192,128},{16,208},{80,144},{144,80},{208,... | collective-permute-start | bytes 589832 | tf_op jit(solution)/shard_map/ppermute | solution.py:287
  91.2 10.7 %collective-permute-start.22 = (f32[64,16,128]{2,1,0:T(8,128)S(1)}, f32[64,16,128]{2,1,0:T(8,128)S(1)}, u32[]{:S(2)}, u32[]{:S(2)}) collective-permute-start(f32[64,16,128]{2,1,0:T(8,128)S(1)} %get-tuple-element.217), channel_id=1, source_target_pairs={{0,4},{4,0},{8,12},{12,8},{16,28},{20,24},{24,20},{28,16},{1,5},{5... | collective-permute-start | bytes 1572872 | tf_op jit(solution)/shard_map/ppermute | solution.py:287
  102.4 8.8 %collective-permute-start.25 = (f32[64,24,128]{2,1,0:T(8,128)S(1)}, f32[64,24,128]{2,1,0:T(8,128)S(1)}, u32[]{:S(2)}, u32[]{:S(2)}) collective-permute-start(f32[64,24,128]{2,1,0:T(8,128)S(1)} %constant_dynamic-update-slice_fusion.14.x_own), channel_id=1, source_target_pairs={{0,16},{16,0},{1,17},{17,1},{2,18},{18,2},{3,19},{19,3},{4,20},{20... | collective-permute-start | bytes 2359304 | tf_op jit(solution)/shard_map/ppermute | solution.py:280
  108.5 12.1 %collective-permute-start.23 = (f32[64,24,128]{2,1,0:T(8,128)S(1)}, f32[64,24,128]{2,1,0:T(8,128)S(1)}, u32[]{:S(2)}, u32[]{:S(2)}) collective-permute-start(f32[64,24,128]{2,1,0:T(8,128)S(1)} %constant_dynamic-update-slice_fusion.16.x_own), channel_id=1, source_target_pairs={{0,16},{16,0},{1,17},{17,1},{2,18},{18,2},{3,19},{19,3},{4,20},{20... | collective-permute-start | bytes 2359304 | tf_op jit(solution)/shard_map/ppermute | solution.py:280
  110.7 9.9 %collective-permute-start.24 = (f32[32,16,128]{2,1,0:T(8,128)S(1)}, f32[32,16,128]{2,1,0:T(8,128)S(1)}, u32[]{:S(2)}, u32[]{:S(2)}) collective-permute-start(f32[32,16,128]{2,1,0:T(8,128)S(1)} %slice_add_fusion.4), channel_id=1, source_target_pairs={{0,12},{4,8},{8,4},{12,0},{16,20},{20,16},{24,28},{28,24},{1,13},{... | collective-permute-start | bytes 786440 | tf_op jit(solution)/shard_map/ppermute | solution.py:287
  114.8 15.1 %collective-permute-start.29 = (f32[64,24,128]{2,1,0:T(8,128)S(1)}, f32[64,24,128]{2,1,0:T(8,128)S(1)}, u32[]{:S(2)}, u32[]{:S(2)}) collective-permute-start(f32[64,24,128]{2,1,0:T(8,128)S(1)} %get-tuple-element.232), channel_id=1, source_target_pairs={{0,4},{4,0},{8,12},{12,8},{16,28},{20,24},{24,20},{28,16},{1,5},{5... | collective-permute-start | bytes 2359304 | tf_op jit(solution)/shard_map/ppermute | solution.py:287
  120.5 7.4 %collective-permute-start.27 = (f32[16,16,128]{2,1,0:T(8,128)S(1)}, f32[16,16,128]{2,1,0:T(8,128)S(1)}, u32[]{:S(2)}, u32[]{:S(2)}) collective-permute-start(f32[16,16,128]{2,1,0:T(8,128)S(1)} %slice_add_fusion.10), channel_id=1, source_target_pairs={{0,1},{1,0},{2,3},{3,2},{16,19},{17,18},{18,17},{19,16},{4,5},{5,4... | collective-permute-start | bytes 393224 | tf_op jit(solution)/shard_map/ppermute | solution.py:287
  124.2 17.9 %collective-permute-start.26 = (f32[64,24,128]{2,1,0:T(8,128)S(1)}, f32[64,24,128]{2,1,0:T(8,128)S(1)}, u32[]{:S(2)}, u32[]{:S(2)}) collective-permute-start(f32[64,24,128]{2,1,0:T(8,128)S(1)} %get-tuple-element.241), channel_id=1, source_target_pairs={{0,4},{4,0},{8,12},{12,8},{16,28},{20,24},{24,20},{28,16},{1,5},{5... | collective-permute-start | bytes 2359304 | tf_op jit(solution)/shard_map/ppermute | solution.py:287
  129.9 12.3 %collective-permute-start.32 = (f32[32,24,128]{2,1,0:T(8,128)S(1)}, f32[32,24,128]{2,1,0:T(8,128)S(1)}, u32[]{:S(2)}, u32[]{:S(2)}) collective-permute-start(f32[32,24,128]{2,1,0:T(8,128)S(1)} %slice_add_fusion.1), channel_id=1, source_target_pairs={{0,12},{4,8},{8,4},{12,0},{16,20},{20,16},{24,28},{28,24},{1,13},{... | collective-permute-start | bytes 1179656 | tf_op jit(solution)/shard_map/ppermute | solution.py:287
  132.4 11.9 %collective-permute-start.31 = (f32[8,16,128]{2,1,0:T(8,128)S(1)}, f32[8,16,128]{2,1,0:T(8,128)S(1)}, u32[]{:S(2)}, u32[]{:S(2)}) collective-permute-start(f32[8,16,128]{2,1,0:T(8,128)S(1)} %multiply_subtract_fusion.2), channel_id=1, source_target_pairs={{0,32},{32,0},{1,33},{33,1},{2,34},{34,2},{3,35},{35,3},{4,36},{36... | collective-permute-start | bytes 196616 | tf_op jit(solution)/shard_map/ppermute | solution.py:280
  142.3 8.6 %collective-permute-start.34 = (f32[16,24,128]{2,1,0:T(8,128)S(1)}, f32[16,24,128]{2,1,0:T(8,128)S(1)}, u32[]{:S(2)}, u32[]{:S(2)}) collective-permute-start(f32[16,24,128]{2,1,0:T(8,128)S(1)} %slice_add_fusion.7), channel_id=1, source_target_pairs={{0,1},{1,0},{2,3},{3,2},{16,19},{17,18},{18,17},{19,16},{4,5},{5,4... | collective-permute-start | bytes 589832 | tf_op jit(solution)/shard_map/ppermute | solution.py:287
  150.8 21.3 %collective-permute-start.43 = (f32[32,16,128]{2,1,0:T(8,128)S(1)}, f32[32,16,128]{2,1,0:T(8,128)S(1)}, u32[]{:S(2)}, u32[]{:S(2)}) collective-permute-start(f32[32,16,128]{2,1,0:T(8,128)S(1)} %constant_dynamic-update-slice_fusion.20), channel_id=1, source_target_pairs={{0,192},{64,128},{128,64},{192,0},{16,80},{80,16},{144,208},{208,1... | collective-permute-start | bytes 786440 | tf_op jit(solution)/shard_map/ppermute | solution.py:287
  150.9 9.5 %collective-permute-start.37 = (f32[8,24,128]{2,1,0:T(8,128)S(1)}, f32[8,24,128]{2,1,0:T(8,128)S(1)}, u32[]{:S(2)}, u32[]{:S(2)}) collective-permute-start(f32[8,24,128]{2,1,0:T(8,128)S(1)} %slice_add_fusion.13), channel_id=1, source_target_pairs={{0,3},{1,2},{2,1},{3,0},{16,17},{17,16},{18,19},{19,18},{4,7},{5,6... | collective-permute-start | bytes 294920 | tf_op jit(solution)/shard_map/ppermute | solution.py:287
  170.2 11.8 %collective-permute-start.45 = (f32[32,24,128]{2,1,0:T(8,128)S(1)}, f32[32,24,128]{2,1,0:T(8,128)S(1)}, u32[]{:S(2)}, u32[]{:S(2)}) collective-permute-start(f32[32,24,128]{2,1,0:T(8,128)S(1)} %constant_dynamic-update-slice_fusion.26), channel_id=1, source_target_pairs={{0,192},{64,128},{128,64},{192,0},{16,80},{80,16},{144,208},{208,1... | collective-permute-start | bytes 1179656 | tf_op jit(solution)/shard_map/ppermute | solution.py:287
  172.1 16.9 %collective-permute-start.44 = (f32[64,16,128]{2,1,0:T(8,128)S(1)}, f32[64,16,128]{2,1,0:T(8,128)S(1)}, u32[]{:S(2)}, u32[]{:S(2)}) collective-permute-start(f32[64,16,128]{2,1,0:T(8,128)S(1)} %constant_dynamic-update-slice_fusion.30.x_own), channel_id=1, source_target_pairs={{0,16},{16,0},{1,17},{17,1},{2,18},{18,2},{3,19},{19,3},{4,20},{20... | collective-permute-start | bytes 1572872 | tf_op jit(solution)/shard_map/ppermute | solution.py:280
  182.0 8.2 %collective-permute-start.42 = (f32[32,24,128]{2,1,0:T(8,128)S(1)}, f32[32,24,128]{2,1,0:T(8,128)S(1)}, u32[]{:S(2)}, u32[]{:S(2)}) collective-permute-start(f32[32,24,128]{2,1,0:T(8,128)S(1)} %constant_dynamic-update-slice_fusion.28), channel_id=1, source_target_pairs={{0,192},{64,128},{128,64},{192,0},{16,80},{80,16},{144,208},{208,1... | collective-permute-start | bytes 1179656 | tf_op jit(solution)/shard_map/ppermute | solution.py:287
  182.0 11.1 %collective-permute-start.47 = (f32[64,24,128]{2,1,0:T(8,128)S(1)}, f32[64,24,128]{2,1,0:T(8,128)S(1)}, u32[]{:S(2)}, u32[]{:S(2)}) collective-permute-start(f32[64,24,128]{2,1,0:T(8,128)S(1)} %constant_dynamic-update-slice_fusion.32.x_own), channel_id=1, source_target_pairs={{0,16},{16,0},{1,17},{17,1},{2,18},{18,2},{3,19},{19,3},{4,20},{20... | collective-permute-start | bytes 2359304 | tf_op jit(solution)/shard_map/ppermute | solution.py:280
  (17 other events, 96.4 us)

commit v3 on v2

--- a/solution.py
+++ b/solution.py
@@ -10,17 +10,17 @@
 B = 128
 BLK = 128
 CAP = 163
-CHUNK = 16
+CHUNKS = (32, 16)
 VEC = 64
 SIZES = (16, 24, 24)
 FIRST = tuple(sum(SIZES[:g]) for g in range(len(SIZES)))
 ROW = ("x", "zl", "core")
 COL = ("y", "zh")
 ORDER = (
-    "A0s", "B0s", "A0a", "C0s", "A0b", "B0a", "C0a", "A0c", "B0b", "C0b", "A0d", "B0c", "A0e",
-    "C0c", "A0f", "B0d", "C0d", "A0g", "B0e", "C0e", "A1p", "C0f", "B0f", "A1a", "C0g", "B0g",
-    "C1p", "A1b", "B1p", "A1c", "C1a", "A1d", "B1a", "C1b", "A1e", "B1b", "A1f", "C1c", "B1c",
-    "C1d", "B1d", "C1e", "B1e", "C1f", "B1f", "A1g", "C1g", "A1m", "B1g", "C1m", "B1m",
+    "A0s", "B0s", "C0s", "A0a", "A0b", "B0a", "C0a", "A0c", "B0b", "C0b", "A0d", "B0c", "A0e",
+    "C0c", "A0f", "B0d", "C0d", "B0e", "A0g", "C0e", "B0f", "C0f", "A1p", "B0g", "C0g", "B1p",
+    "A1a", "C1p", "A1b", "B1a", "A1c", "C1a", "B1b", "A1d", "C1b", "B1c", "A1e", "C1c", "A1f",
+    "B1d", "C1d", "B1e", "A1g", "C1e", "B1f", "C1f", "A1m", "B1g", "C1g", "B1m", "C1m",
 )
 
 
@@ -56,9 +56,9 @@
     return copies
 
 
-def copy_tiles(tiles, held, sems):
+def copy_tiles(tiles, held, sems, chunk):
     def one(c, size):
-        span = pl.ds(c * CHUNK, size)
+        span = pl.ds(c * chunk, size)
         return pltpu.make_async_copy(tiles.at[0, 0, span], held.at[span], sems.at[c])
 
     return one
@@ -80,19 +80,19 @@
         acc[jnp.where(start + u < count, row_table[row // 8] + row % 8, BLK)] += sums[u]
 
 
-def over_chunks(count, work):
-    whole = CAP // CHUNK
+def over_chunks(count, chunk, work):
+    whole = CAP // chunk
 
     def step(c, carry):
-        work(c, CHUNK)
+        work(c, chunk)
         return carry
 
-    lax.fori_loop(0, jnp.minimum((count + CHUNK - 1) // CHUNK, whole), step, 0)
-    if CAP % CHUNK:
-
-        @pl.when(count > whole * CHUNK)
+    lax.fori_loop(0, jnp.minimum((count + chunk - 1) // chunk, whole), step, 0)
+    if CAP % chunk:
+
+        @pl.when(count > whole * chunk)
         def _():
-            work(whole, CAP % CHUNK)
+            work(whole, CAP % chunk)
 
 
 def send_out(acc, parts, outs, sems):
@@ -110,17 +110,17 @@
 TABLES = [pltpu.SMEM((16,), jnp.int32)] * 3
 TILES = [
     pltpu.VMEM((CAP, B, B), jnp.float32),
-    pltpu.SemaphoreType.DMA((-(-CAP // CHUNK),)),
+    pltpu.SemaphoreType.DMA((-(-CAP // min(CHUNKS)),)),
     pltpu.SemaphoreType.DMA((2,)),
 ]
 
 
-def start_tiles(count, tile_copy):
-    for c in range(-(-CAP // CHUNK)):
-
-        @pl.when(c * CHUNK < count)
+def start_tiles(count, chunk, tile_copy):
+    for c in range(-(-CAP // chunk)):
+
+        @pl.when(c * chunk < count)
         def _():
-            tile_copy(c, min(CHUNK, CAP - c * CHUNK)).start()
+            tile_copy(c, min(chunk, CAP - c * chunk)).start()
 
 
 def first_kernel(live, rows_in, cols_in, tiles, panel_cur, panel_prev, *refs):
@@ -130,17 +130,21 @@
     xf, xp, xs, acc, x_sems, out_sems = refs[8:]
     mine = pl.multiple_of(((lax.axis_index("x") * 2 + lax.axis_index("zl")) * 2 + lax.axis_index("core")) * (8 * B), 8 * B)
     pattern = read_pattern((rows_in, cols_in), (rows, cols), p_sems)
-    x_copy = pltpu.make_async_copy(panel_cur, xf, x_sems.at[0])
-    p_copy = pltpu.make_async_copy(panel_prev.at[:, pl.ds(mine, 8 * B)], xp, x_sems.at[1])
-    x_copy.start()
-    count = live[0, 0]
-    tile_copy = copy_tiles(tiles, held, sems)
-    start_tiles(count, tile_copy)
+    x_copies = []
+    for k in range(4):
+        span = pl.ds(k * 32 * B, 32 * B)
+        x_copies.append(pltpu.make_async_copy(panel_cur.at[:, span], xf.at[:, span], x_sems.at[k]))
+        x_copies[k].start()
+    p_copy = pltpu.make_async_copy(panel_prev.at[:, pl.ds(mine, 8 * B)], xp, x_sems.at[4])
+    count, chunk = live[0, 0], CHUNKS[0]
+    tile_copy = copy_tiles(tiles, held, sems, chunk)
+    start_tiles(count, chunk, tile_copy)
     p_copy.start()
     row_places(row_table)
     acc[...] = jnp.zeros_like(acc)
-    x_copy.wait()
     for c in range(BLK):
+        if c % 32 == 0:
+            x_copies[c // 32].wait()
         xs[c] = split(xf[:, c * B : (c + 1) * B])
     for copy in pattern:
         copy.wait()
@@ -149,9 +153,9 @@
 
     def work(c, size):
         tile_copy(c, size).wait()
-        multiply(c * CHUNK, size, count, rows, cols, row_table, None, xs, held, acc)
-
-    over_chunks(count, work)
+        multiply(c * chunk, size, count, rows, cols, row_table, None, xs, held, acc)
+
+    over_chunks(count, chunk, work)
     p_copy.wait()
     for b in range(8):
         prev[b] = xp[:, b * B : (b + 1) * B]
@@ -174,7 +178,7 @@
             pltpu.VMEM((VEC, 8 * B), jnp.float32),
             pltpu.VMEM((BLK, 2 * VEC, B), jnp.bfloat16),
             pltpu.VMEM((BLK + 1, VEC, B), jnp.float32),
-            pltpu.SemaphoreType.DMA((2,)),
+            pltpu.SemaphoreType.DMA((5,)),
             pltpu.SemaphoreType.DMA((n,)),
         ],
         compiler_params=pltpu.CompilerParams(vmem_limit_bytes=26 << 20),
@@ -199,9 +203,9 @@
     xs, acc, flat, sem, out_sems = refs[8:]
     v = acc.shape[1]
     pattern = read_pattern((rows_in, cols_in), (rows, cols), p_sems)
-    count = live[0, 0]
-    tile_copy = copy_tiles(tiles, held, sems)
-    start_tiles(count, tile_copy)
+    count, chunk = live[0, 0], CHUNKS[1]
+    tile_copy = copy_tiles(tiles, held, sems, chunk)
+    start_tiles(count, chunk, tile_copy)
     row_places(row_table)
     col_places(col_table, owners)
     lay_out(x_own, x_other, owners, flat)
@@ -215,9 +219,9 @@
 
     def work(c, size):
         tile_copy(c, size).wait()
-        multiply(c * CHUNK, size, count, rows, cols, row_table, col_table, xs, held, acc)
-
-    over_chunks(count, work)
+        multiply(c * chunk, size, count, rows, cols, row_table, col_table, xs, held, acc)
+
+    over_chunks(count, chunk, work)
     send_out(acc, (v,), (keep, send), out_sems)
     rows_copy.wait()
 

time: 199 us -> 194 us (0.975); the launches traced: 197 us -> 194 us
  waiting for transfers between devices: 69.9 us -> 52.8 us
  starting transfers between devices: 90.4 us -> 107 us
  Pallas kernels: 20.8 us -> 18.1 us
    ppermute x36, waiting for transfers between devices: 61.9 us -> 49.3 us  [exchange(): return lax.ppermute(value, both, pairs)]
    ppermute x36, starting transfers between devices: 55.6 us -> 67.6 us  [exchange(): return lax.ppermute(value, both, pairs)]
    ppermute x12, waiting for transfers between devices: 7.98 us -> 3.54 us  [swap(): return lax.ppermute(value, axis, [(0, 1), (1, 0)])]
    ppermute x12, starting transfers between devices: 34.7 us -> 39 us  [swap(): return lax.ppermute(value, axis, [(0, 1), (1, 0)])]
  transfers between devices with their start and end apart: 48 -> 48, of which waited for: 26 -> 21; matrix products, arithmetic and copies ran while one was open for 6% -> 6% of each run, Pallas kernels for 7% -> 6%
where the time goes in v3:
time: 194 us
  starting transfers between devices  107 us (55%)
  waiting for transfers between devices  52.8 us (27%)
  Pallas kernels  18.1 us (9%)
  other arithmetic  11.6 us (6%)
  between operations  3.27 us (2%)
    ppermute x36, starting transfers between devices, exchange(): return lax.ppermute(value, both, pairs)  67.6 us
    ppermute x36, waiting for transfers between devices, exchange(): return lax.ppermute(value, both, pairs)  49.3 us
    ppermute x12, starting transfers between devices, swap(): return lax.ppermute(value, axis, [(0, 1), (1, 0)])  39 us
    pallas_call x3, Pallas kernels, second_products(): pl.pallas_call(functools.partial(second_kernel, FIRST[g]), out_shape=[plt...  8.99 us
    add x18, other arithmetic, body(): token = functools.reduce(jnp.add, [piece[half:2 * half] for piece in kept])  8.72 us
    pallas_call x1, Pallas kernels, first_products(): pl.pallas_call(first_kernel, out_shape=[pltpu.VMEM((64, v, B), jnp.float3...  5.08 us
    pallas_call x3, Pallas kernels, assemble(): pl.pallas_call(functools.partial(assemble_kernel, FIRST[g], v), out_shape...  4.04 us
  transfers between devices with their start and end apart: 48, of which 21 were waited for; matrix products, arithmetic and copies ran while one was open for 6% of the time, Pallas kernels for 6%

profile of v3, /device:TPU:1, one launch (start us, length us, event | category | flops | bytes accessed | tf_op | source)
XLA Modules:
  0.0 193.8 jit_solution(8224194920136463359)
XLA Ops:
  1.3 5.1 %first.1 = (f32[64,16,128]{2,1,0:T(8,128)S(1)}, f32[64,16,128]{2,1,0:T(8,128)S(1)}, f32[64,24,128]{2,1,0:T(8,128)S(1)}, f32[64,24,128]{2,1,0:T(8,128)}, f32[64,2...) custom-call(s32[1,1]{1,0:T(1,128)S(6)} %copy.36.live, ...), custom_call_target="tpu_custom_call" | custom-call | flops 1 | bytes 1 | tf_op jit(solution)/shard_map/first/pallas_call | solution.py:170
  6.4 7.6 %collective-permute-start.2 = (f32[64,16,128]{2,1,0:T(8,128)S(1)}, f32[64,16,128]{2,1,0:T(8,128)S(1)}, u32[]{:S(2)}, u32[]{:S(2)}) collective-permute-start(f32[64,16,128]{2,1,0:T(8,128)S(1)} %get-tuple-element.158), channel_id=1, source_target_pairs={{0,4},{4,0},{8,12},{12,8},{16,28},{20,24},{24,20},{28,16},{1,5},{5... | collective-permute-start | bytes 1572872 | tf_op jit(solution)/shard_map/ppermute | solution.py:291
  14.1 2.6 %collective-permute-start = (f32[64,24,128]{2,1,0:T(8,128)S(1)}, f32[64,24,128]{2,1,0:T(8,128)}, u32[]{:S(2)}, u32[]{:S(2)}) collective-permute-start(f32[64,24,128]{2,1,0:T(8,128)S(1)} %get-tuple-element.153), channel_id=1, source_target_pairs={{0,4},{4,0},{8,12},{12,8},{16,28},{20,24},{24,20},{28,16},{1,5},{5... | collective-permute-start | bytes 2359304 | tf_op jit(solution)/shard_map/ppermute | solution.py:291
  16.7 3.9 %collective-permute-done.2 = f32[64,16,128]{2,1,0:T(8,128)S(1)} collective-permute-done((f32[64,16,128]{2,1,0:T(8,128)S(1)}, f32[64,16,128]{2,1,0:T(8,128)S(1)}, u32[]{:S(2)}, u32[]{:S(2)}) %collective-permute-start.2) | collective-permute-done | bytes 524320 | tf_op jit(solution)/shard_map/ppermute | solution.py:291
  23.4 7.4 %collective-permute-done.3 = f32[32,16,128]{2,1,0:T(8,128)} collective-permute-done((f32[32,16,128]{2,1,0:T(8,128)}, f32[32,16,128]{2,1,0:T(8,128)}, u32[]{:S(2)}, u32[]{:S(2)}) %collective-permute-start.3) | collective-permute-done | bytes 262176 | tf_op jit(solution)/shard_map/ppermute | solution.py:291
  35.4 5.0 %collective-permute-done = f32[64,24,128]{2,1,0:T(8,128)} collective-permute-done((f32[64,24,128]{2,1,0:T(8,128)S(1)}, f32[64,24,128]{2,1,0:T(8,128)}, u32[]{:S(2)}, u32[]{:S(2)}) %collective-permute-start) | collective-permute-done | bytes 786464 | tf_op jit(solution)/shard_map/ppermute | solution.py:291
  42.4 3.7 %collective-permute-start.8 = (f32[8,16,128]{2,1,0:T(8,128)S(1)}, f32[8,16,128]{2,1,0:T(8,128)S(1)}, u32[]{:S(2)}, u32[]{:S(2)}) collective-permute-start(f32[8,16,128]{2,1,0:T(8,128)S(1)} %slice_add_fusion.17), channel_id=1, source_target_pairs={{0,3},{1,2},{2,1},{3,0},{16,17},{17,16},{18,19},{19,18},{4,7},{5,6... | collective-permute-start | bytes 196616 | tf_op jit(solution)/shard_map/ppermute | solution.py:291
  47.1 4.4 %collective-permute-start.10 = (f32[16,24,128]{2,1,0:T(8,128)S(1)}, f32[16,24,128]{2,1,0:T(8,128)S(1)}, u32[]{:S(2)}, u32[]{:S(2)}) collective-permute-start(f32[16,24,128]{2,1,0:T(8,128)S(1)} %slice_add_fusion.9), channel_id=1, source_target_pairs={{0,1},{1,0},{2,3},{3,2},{16,19},{17,18},{18,17},{19,16},{4,5},{5,4... | collective-permute-start | bytes 589832 | tf_op jit(solution)/shard_map/ppermute | solution.py:291
  54.5 4.0 %collective-permute-done.10 = f32[16,24,128]{2,1,0:T(8,128)S(1)} collective-permute-done((f32[16,24,128]{2,1,0:T(8,128)S(1)}, f32[16,24,128]{2,1,0:T(8,128)S(1)}, u32[]{:S(2)}, u32[]{:S(2)}) %collective-permute-start.10) | collective-permute-done | bytes 196640 | tf_op jit(solution)/shard_map/ppermute | solution.py:291
  59.5 3.7 %collective-permute-start.13 = (f32[16,16,128]{2,1,0:T(8,128)S(1)}, f32[16,16,128]{2,1,0:T(8,128)S(1)}, u32[]{:S(2)}, u32[]{:S(2)}) collective-permute-start(f32[16,16,128]{2,1,0:T(8,128)S(1)} %constant_dynamic-update-slice_fusion), channel_id=1, source_target_pairs={{0,64},{64,0},{128,192},{192,128},{16,208},{80,144},{144,80},{208,... | collective-permute-start | bytes 393224 | tf_op jit(solution)/shard_map/ppermute | solution.py:291
  64.1 4.3 %collective-permute-start.11 = (f32[8,24,128]{2,1,0:T(8,128)S(1)}, f32[8,24,128]{2,1,0:T(8,128)S(1)}, u32[]{:S(2)}, u32[]{:S(2)}) collective-permute-start(f32[8,24,128]{2,1,0:T(8,128)S(1)} %slice_add_fusion.14), channel_id=1, source_target_pairs={{0,3},{1,2},{2,1},{3,0},{16,17},{17,16},{18,19},{19,18},{4,7},{5,6... | collective-permute-start | bytes 294920 | tf_op jit(solution)/shard_map/ppermute | solution.py:291
  75.1 3.2 %collective-permute-start.18 = (f32[16,24,128]{2,1,0:T(8,128)S(1)}, f32[16,24,128]{2,1,0:T(8,128)S(1)}, u32[]{:S(2)}, u32[]{:S(2)}) collective-permute-start(f32[16,24,128]{2,1,0:T(8,128)S(1)} %constant_dynamic-update-slice_fusion.4), channel_id=1, source_target_pairs={{0,64},{64,0},{128,192},{192,128},{16,208},{80,144},{144,80},{208,... | collective-permute-start | bytes 589832 | tf_op jit(solution)/shard_map/ppermute | solution.py:291
  78.3 9.8 %collective-permute-start.21 = (f32[64,16,128]{2,1,0:T(8,128)S(1)}, f32[64,16,128]{2,1,0:T(8,128)S(1)}, u32[]{:S(2)}, u32[]{:S(2)}) collective-permute-start(f32[64,16,128]{2,1,0:T(8,128)S(1)} %constant_dynamic-update-slice_fusion.6.x_own), channel_id=1, source_target_pairs={{0,16},{16,0},{1,17},{17,1},{2,18},{18,2},{3,19},{19,3},{4,20},{20... | collective-permute-start | bytes 1572872 | tf_op jit(solution)/shard_map/ppermute | solution.py:284
  90.2 3.9 %collective-permute-done.17 = f32[16,24,128]{2,1,0:T(8,128)S(1)} collective-permute-done((f32[16,24,128]{2,1,0:T(8,128)S(1)}, f32[16,24,128]{2,1,0:T(8,128)S(1)}, u32[]{:S(2)}, u32[]{:S(2)}) %collective-permute-start.17) | collective-permute-done | bytes 196640 | tf_op jit(solution)/shard_map/ppermute | solution.py:291
  94.9 2.9 %second.3 = (f32[64,16,128]{2,1,0:T(8,128)S(1)}, f32[64,16,128]{2,1,0:T(8,128)S(1)}, f32[64,16384]{1,0:T(8,128)}) custom-call(s32[1,1]{1,0:T(1,128)S(6)} %copy.36.live, s32[1,1,163]{2,1,0:T(1,128)} %rows_in.7, s32[1,1,163]{2,1,0:T(1,128)} %cols_in.7, f32[1,1,163,128,128]{4,3,2,1,0:T(8,128)} %tiles.7, ...), custom_call_target="tpu_custom_call" | custom-call | flops 1 | bytes 1 | tf_op jit(solution)/shard_map/second/pallas_call | solution.py:236
  99.7 4.1 %collective-permute-start.24 = (f32[64,24,128]{2,1,0:T(8,128)S(1)}, f32[64,24,128]{2,1,0:T(8,128)S(1)}, u32[]{:S(2)}, u32[]{:S(2)}) collective-permute-start(f32[64,24,128]{2,1,0:T(8,128)S(1)} %constant_dynamic-update-slice_fusion.14.x_own), channel_id=1, source_target_pairs={{0,16},{16,0},{1,17},{17,1},{2,18},{18,2},{3,19},{19,3},{4,20},{20... | collective-permute-start | bytes 2359304 | tf_op jit(solution)/shard_map/ppermute | solution.py:284
  103.9 4.1 %collective-permute-start.22 = (f32[64,24,128]{2,1,0:T(8,128)S(1)}, f32[64,24,128]{2,1,0:T(8,128)S(1)}, u32[]{:S(2)}, u32[]{:S(2)}) collective-permute-start(f32[64,24,128]{2,1,0:T(8,128)S(1)} %constant_dynamic-update-slice_fusion.16.x_own), channel_id=1, source_target_pairs={{0,16},{16,0},{1,17},{17,1},{2,18},{18,2},{3,19},{19,3},{4,20},{20... | collective-permute-start | bytes 2359304 | tf_op jit(solution)/shard_map/ppermute | solution.py:284
  107.9 3.0 %second.4 = (f32[64,24,128]{2,1,0:T(8,128)S(1)}, f32[64,24,128]{2,1,0:T(8,128)S(1)}, f32[64,16384]{1,0:T(8,128)}) custom-call(s32[1,1]{1,0:T(1,128)S(6)} %copy.36.live, s32[1,1,163]{2,1,0:T(1,128)} %rows_in.7, s32[1,1,163]{2,1,0:T(1,128)} %cols_in.7, f32[1,1,163,128,128]{4,3,2,1,0:T(8,128)} %tiles.7, ...), custom_call_target="tpu_custom_call", output_to_operand_aliasing={{2}: (6, {})} | custom-call | flops 1 | bytes 1 | tf_op jit(solution)/shard_map/second/pallas_call | solution.py:236
  113.1 3.0 %second.5 = (f32[64,24,128]{2,1,0:T(8,128)S(1)}, f32[64,24,128]{2,1,0:T(8,128)S(1)}, f32[64,16384]{1,0:T(8,128)}) custom-call(s32[1,1]{1,0:T(1,128)S(6)} %copy.36.live, s32[1,1,163]{2,1,0:T(1,128)} %rows_in.7, s32[1,1,163]{2,1,0:T(1,128)} %cols_in.7, f32[1,1,163,128,128]{4,3,2,1,0:T(8,128)} %tiles.7, ...), custom_call_target="tpu_custom_call", output_to_operand_aliasing={{2}: (6, {})} | custom-call | flops 1 | bytes 1 | tf_op jit(solution)/shard_map/second/pallas_call | solution.py:236
  116.1 3.3 %collective-permute-start.25 = (f32[64,24,128]{2,1,0:T(8,128)S(1)}, f32[64,24,128]{2,1,0:T(8,128)S(1)}, u32[]{:S(2)}, u32[]{:S(2)}) collective-permute-start(f32[64,24,128]{2,1,0:T(8,128)S(1)} %get-tuple-element.236), channel_id=1, source_target_pairs={{0,4},{4,0},{8,12},{12,8},{16,28},{20,24},{24,20},{28,16},{1,5},{5... | collective-permute-start | bytes 2359304 | tf_op jit(solution)/shard_map/ppermute | solution.py:291
  127.5 2.5 %collective-permute-start.30 = (f32[8,16,128]{2,1,0:T(8,128)S(1)}, f32[8,16,128]{2,1,0:T(8,128)S(1)}, u32[]{:S(2)}, u32[]{:S(2)}) collective-permute-start(f32[8,16,128]{2,1,0:T(8,128)S(1)} %slice_add_fusion.16), channel_id=1, source_target_pairs={{0,3},{1,2},{2,1},{3,0},{16,17},{17,16},{18,19},{19,18},{4,7},{5,6... | collective-permute-start | bytes 196616 | tf_op jit(solution)/shard_map/ppermute | solution.py:291
  130.0 7.3 %collective-permute-done.25 = f32[64,24,128]{2,1,0:T(8,128)S(1)} collective-permute-done((f32[64,24,128]{2,1,0:T(8,128)S(1)}, f32[64,24,128]{2,1,0:T(8,128)S(1)}, u32[]{:S(2)}, u32[]{:S(2)}) %collective-permute-start.25) | collective-permute-done | bytes 786464 | tf_op jit(solution)/shard_map/ppermute | solution.py:291
  141.2 3.1 %collective-permute-done.29 = f32[32,24,128]{2,1,0:T(8,128)S(1)} collective-permute-done((f32[32,24,128]{2,1,0:T(8,128)S(1)}, f32[32,24,128]{2,1,0:T(8,128)S(1)}, u32[]{:S(2)}, u32[]{:S(2)}) %collective-permute-start.29) | collective-permute-done | bytes 393248 | tf_op jit(solution)/shard_map/ppermute | solution.py:291
  147.4 3.7 %collective-permute-start.37 = (f32[16,16,128]{2,1,0:T(8,128)S(1)}, f32[16,16,128]{2,1,0:T(8,128)S(1)}, u32[]{:S(2)}, u32[]{:S(2)}) collective-permute-start(f32[16,16,128]{2,1,0:T(8,128)S(1)} %constant_dynamic-update-slice_fusion.18), channel_id=1, source_target_pairs={{0,64},{64,0},{128,192},{192,128},{16,208},{80,144},{144,80},{208,... | collective-permute-start | bytes 393224 | tf_op jit(solution)/shard_map/ppermute | solution.py:291
  153.7 5.0 %collective-permute-start.39 = (f32[32,16,128]{2,1,0:T(8,128)S(1)}, f32[32,16,128]{2,1,0:T(8,128)S(1)}, u32[]{:S(2)}, u32[]{:S(2)}) collective-permute-start(f32[32,16,128]{2,1,0:T(8,128)S(1)} %constant_dynamic-update-slice_fusion.20), channel_id=1, source_target_pairs={{0,192},{64,128},{128,64},{192,0},{16,80},{80,16},{144,208},{208,1... | collective-permute-start | bytes 786440 | tf_op jit(solution)/shard_map/ppermute | solution.py:291
  162.3 2.9 %collective-permute-start.42 = (f32[16,24,128]{2,1,0:T(8,128)S(1)}, f32[16,24,128]{2,1,0:T(8,128)S(1)}, u32[]{:S(2)}, u32[]{:S(2)}) collective-permute-start(f32[16,24,128]{2,1,0:T(8,128)S(1)} %constant_dynamic-update-slice_fusion.22), channel_id=1, source_target_pairs={{0,64},{64,0},{128,192},{192,128},{16,208},{80,144},{144,80},{208,... | collective-permute-start | bytes 589832 | tf_op jit(solution)/shard_map/ppermute | solution.py:291
  165.2 6.3 %collective-permute-start.45 = (f32[64,16,128]{2,1,0:T(8,128)S(1)}, f32[64,16,128]{2,1,0:T(8,128)S(1)}, u32[]{:S(2)}, u32[]{:S(2)}) collective-permute-start(f32[64,16,128]{2,1,0:T(8,128)S(1)} %constant_dynamic-update-slice_fusion.24.x_own), channel_id=1, source_target_pairs={{0,16},{16,0},{1,17},{17,1},{2,18},{18,2},{3,19},{19,3},{4,20},{20... | collective-permute-start | bytes 1572872 | tf_op jit(solution)/shard_map/ppermute | solution.py:284
  171.6 3.0 %collective-permute-start.41 = (f32[16,24,128]{2,1,0:T(8,128)S(1)}, f32[16,24,128]{2,1,0:T(8,128)S(1)}, u32[]{:S(2)}, u32[]{:S(2)}) collective-permute-start(f32[16,24,128]{2,1,0:T(8,128)S(1)} %constant_dynamic-update-slice_fusion.26), channel_id=1, source_target_pairs={{0,64},{64,0},{128,192},{192,128},{16,208},{80,144},{144,80},{208,... | collective-permute-start | bytes 589832 | tf_op jit(solution)/shard_map/ppermute | solution.py:291
  174.8 2.9 %collective-permute-done.41 = f32[16,24,128]{2,1,0:T(8,128)S(1)} collective-permute-done((f32[16,24,128]{2,1,0:T(8,128)S(1)}, f32[16,24,128]{2,1,0:T(8,128)S(1)}, u32[]{:S(2)}, u32[]{:S(2)}) %collective-permute-start.41) | collective-permute-done | bytes 196640 | tf_op jit(solution)/shard_map/ppermute | solution.py:291
  179.1 2.6 %collective-permute-done.44 = f32[32,24,128]{2,1,0:T(8,128)S(1)} collective-permute-done((f32[32,24,128]{2,1,0:T(8,128)S(1)}, f32[32,24,128]{2,1,0:T(8,128)S(1)}, u32[]{:S(2)}, u32[]{:S(2)}) %collective-permute-start.44) | collective-permute-done | bytes 393248 | tf_op jit(solution)/shard_map/ppermute | solution.py:291
  181.7 4.0 %collective-permute-start.47 = (f32[64,24,128]{2,1,0:T(8,128)S(1)}, f32[64,24,128]{2,1,0:T(8,128)S(1)}, u32[]{:S(2)}, u32[]{:S(2)}) collective-permute-start(f32[64,24,128]{2,1,0:T(8,128)S(1)} %constant_dynamic-update-slice_fusion.32.x_own), channel_id=1, source_target_pairs={{0,16},{16,0},{1,17},{17,1},{2,18},{18,2},{3,19},{19,3},{4,20},{20... | collective-permute-start | bytes 2359304 | tf_op jit(solution)/shard_map/ppermute | solution.py:284
  186.0 4.3 %collective-permute-start.46 = (f32[64,24,128]{2,1,0:T(8,128)S(1)}, f32[64,24,128]{2,1,0:T(8,128)S(1)}, u32[]{:S(2)}, u32[]{:S(2)}) collective-permute-start(f32[64,24,128]{2,1,0:T(8,128)S(1)} %constant_dynamic-update-slice_fusion.34.x_own), channel_id=1, source_target_pairs={{0,16},{16,0},{1,17},{17,1},{2,18},{18,2},{3,19},{19,3},{4,20},{20... | collective-permute-start | bytes 2359304 | tf_op jit(solution)/shard_map/ppermute | solution.py:284
  (133 shorter events, 53.9 us)
Async XLA Ops:
  6.4 14.2 %collective-permute-start.2 = (f32[64,16,128]{2,1,0:T(8,128)S(1)}, f32[64,16,128]{2,1,0:T(8,128)S(1)}, u32[]{:S(2)}, u32[]{:S(2)}) collective-permute-start(f32[64,16,128]{2,1,0:T(8,128)S(1)} %get-tuple-element.158), channel_id=1, source_target_pairs={{0,4},{4,0},{8,12},{12,8},{16,28},{20,24},{24,20},{28,16},{1,5},{5... | collective-permute-start | bytes 1572872 | tf_op jit(solution)/shard_map/ppermute | solution.py:291
  14.0 19.9 %collective-permute-start.1 = (f32[64,24,128]{2,1,0:T(8,128)}, f32[64,24,128]{2,1,0:T(8,128)}, u32[]{:S(2)}, u32[]{:S(2)}) collective-permute-start(f32[64,24,128]{2,1,0:T(8,128)} %get-tuple-element.155), channel_id=1, source_target_pairs={{0,4},{4,0},{8,12},{12,8},{16,28},{20,24},{24,20},{28,16},{1,5},{5... | collective-permute-start | bytes 2359304 | tf_op jit(solution)/shard_map/ppermute | solution.py:291
  14.1 26.3 %collective-permute-start = (f32[64,24,128]{2,1,0:T(8,128)S(1)}, f32[64,24,128]{2,1,0:T(8,128)}, u32[]{:S(2)}, u32[]{:S(2)}) collective-permute-start(f32[64,24,128]{2,1,0:T(8,128)S(1)} %get-tuple-element.153), channel_id=1, source_target_pairs={{0,4},{4,0},{8,12},{12,8},{16,28},{20,24},{24,20},{28,16},{1,5},{5... | collective-permute-start | bytes 2359304 | tf_op jit(solution)/shard_map/ppermute | solution.py:291
  22.1 8.7 %collective-permute-start.3 = (f32[32,16,128]{2,1,0:T(8,128)}, f32[32,16,128]{2,1,0:T(8,128)}, u32[]{:S(2)}, u32[]{:S(2)}) collective-permute-start(f32[32,16,128]{2,1,0:T(8,128)} %slice_add_fusion.5), channel_id=1, source_target_pairs={{0,12},{4,8},{8,4},{12,0},{16,20},{20,16},{24,28},{28,24},{1,13},{... | collective-permute-start | bytes 786440 | tf_op jit(solution)/shard_map/ppermute | solution.py:291
  31.8 9.7 %collective-permute-start.6 = (f32[16,16,128]{2,1,0:T(8,128)S(1)}, f32[16,16,128]{2,1,0:T(8,128)S(1)}, u32[]{:S(2)}, u32[]{:S(2)}) collective-permute-start(f32[16,16,128]{2,1,0:T(8,128)S(1)} %slice_add_fusion.11), channel_id=1, source_target_pairs={{0,1},{1,0},{2,3},{3,2},{16,19},{17,18},{18,17},{19,16},{4,5},{5,4... | collective-permute-start | bytes 393224 | tf_op jit(solution)/shard_map/ppermute | solution.py:291
  35.0 11.1 %collective-permute-start.5 = (f32[32,24,128]{2,1,0:T(8,128)S(1)}, f32[32,24,128]{2,1,0:T(8,128)S(1)}, u32[]{:S(2)}, u32[]{:S(2)}) collective-permute-start(f32[32,24,128]{2,1,0:T(8,128)S(1)} %slice_add_fusion.3), channel_id=1, source_target_pairs={{0,12},{4,8},{8,4},{12,0},{16,20},{20,16},{24,28},{28,24},{1,13},{... | collective-permute-start | bytes 1179656 | tf_op jit(solution)/shard_map/ppermute | solution.py:291
  41.4 10.0 %collective-permute-start.4 = (f32[32,24,128]{2,1,0:T(8,128)S(1)}, f32[32,24,128]{2,1,0:T(8,128)S(1)}, u32[]{:S(2)}, u32[]{:S(2)}) collective-permute-start(f32[32,24,128]{2,1,0:T(8,128)S(1)} %slice_add_fusion.2), channel_id=1, source_target_pairs={{0,12},{4,8},{8,4},{12,0},{16,20},{20,16},{24,28},{28,24},{1,13},{... | collective-permute-start | bytes 1179656 | tf_op jit(solution)/shard_map/ppermute | solution.py:291
  42.4 10.5 %collective-permute-start.8 = (f32[8,16,128]{2,1,0:T(8,128)S(1)}, f32[8,16,128]{2,1,0:T(8,128)S(1)}, u32[]{:S(2)}, u32[]{:S(2)}) collective-permute-start(f32[8,16,128]{2,1,0:T(8,128)S(1)} %slice_add_fusion.17), channel_id=1, source_target_pairs={{0,3},{1,2},{2,1},{3,0},{16,17},{17,16},{18,19},{19,18},{4,7},{5,6... | collective-permute-start | bytes 196616 | tf_op jit(solution)/shard_map/ppermute | solution.py:291
  47.1 11.4 %collective-permute-start.10 = (f32[16,24,128]{2,1,0:T(8,128)S(1)}, f32[16,24,128]{2,1,0:T(8,128)S(1)}, u32[]{:S(2)}, u32[]{:S(2)}) collective-permute-start(f32[16,24,128]{2,1,0:T(8,128)S(1)} %slice_add_fusion.9), channel_id=1, source_target_pairs={{0,1},{1,0},{2,3},{3,2},{16,19},{17,18},{18,17},{19,16},{4,5},{5,4... | collective-permute-start | bytes 589832 | tf_op jit(solution)/shard_map/ppermute | solution.py:291
  52.4 10.8 %collective-permute-start.7 = (f32[16,24,128]{2,1,0:T(8,128)S(1)}, f32[16,24,128]{2,1,0:T(8,128)S(1)}, u32[]{:S(2)}, u32[]{:S(2)}) collective-permute-start(f32[16,24,128]{2,1,0:T(8,128)S(1)} %slice_add_fusion.8), channel_id=1, source_target_pairs={{0,1},{1,0},{2,3},{3,2},{16,19},{17,18},{18,17},{19,16},{4,5},{5,4... | collective-permute-start | bytes 589832 | tf_op jit(solution)/shard_map/ppermute | solution.py:291
  59.4 10.1 %collective-permute-start.12 = (f32[8,24,128]{2,1,0:T(8,128)S(1)}, f32[8,24,128]{2,1,0:T(8,128)S(1)}, u32[]{:S(2)}, u32[]{:S(2)}) collective-permute-start(f32[8,24,128]{2,1,0:T(8,128)S(1)} %slice_add_fusion.15), channel_id=1, source_target_pairs={{0,3},{1,2},{2,1},{3,0},{16,17},{17,16},{18,19},{19,18},{4,7},{5,6... | collective-permute-start | bytes 294920 | tf_op jit(solution)/shard_map/ppermute | solution.py:291
  59.5 8.9 %collective-permute-start.13 = (f32[16,16,128]{2,1,0:T(8,128)S(1)}, f32[16,16,128]{2,1,0:T(8,128)S(1)}, u32[]{:S(2)}, u32[]{:S(2)}) collective-permute-start(f32[16,16,128]{2,1,0:T(8,128)S(1)} %constant_dynamic-update-slice_fusion), channel_id=1, source_target_pairs={{0,64},{64,0},{128,192},{192,128},{16,208},{80,144},{144,80},{208,... | collective-permute-start | bytes 393224 | tf_op jit(solution)/shard_map/ppermute | solution.py:291
  64.1 8.6 %collective-permute-start.11 = (f32[8,24,128]{2,1,0:T(8,128)S(1)}, f32[8,24,128]{2,1,0:T(8,128)S(1)}, u32[]{:S(2)}, u32[]{:S(2)}) collective-permute-start(f32[8,24,128]{2,1,0:T(8,128)S(1)} %slice_add_fusion.14), channel_id=1, source_target_pairs={{0,3},{1,2},{2,1},{3,0},{16,17},{17,16},{18,19},{19,18},{4,7},{5,6... | collective-permute-start | bytes 294920 | tf_op jit(solution)/shard_map/ppermute | solution.py:291
  68.5 9.8 %collective-permute-start.15 = (f32[32,16,128]{2,1,0:T(8,128)S(1)}, f32[32,16,128]{2,1,0:T(8,128)S(1)}, u32[]{:S(2)}, u32[]{:S(2)}) collective-permute-start(f32[32,16,128]{2,1,0:T(8,128)S(1)} %constant_dynamic-update-slice_fusion.2), channel_id=1, source_target_pairs={{0,192},{64,128},{128,64},{192,0},{16,80},{80,16},{144,208},{208,1... | collective-permute-start | bytes 786440 | tf_op jit(solution)/shard_map/ppermute | solution.py:291
  73.7 14.5 %collective-permute-start.14 = (f32[8,24,128]{2,1,0:T(8,128)S(1)}, f32[8,24,128]{2,1,0:T(8,128)S(1)}, u32[]{:S(2)}, u32[]{:S(2)}) collective-permute-start(f32[8,24,128]{2,1,0:T(8,128)S(1)} %slice_subtract_fusion), channel_id=1, source_target_pairs={{0,32},{32,0},{1,33},{33,1},{2,34},{34,2},{3,35},{35,3},{4,36},{36... | collective-permute-start | bytes 294920 | tf_op jit(solution)/shard_map/ppermute | solution.py:284
  75.1 14.6 %collective-permute-start.18 = (f32[16,24,128]{2,1,0:T(8,128)S(1)}, f32[16,24,128]{2,1,0:T(8,128)S(1)}, u32[]{:S(2)}, u32[]{:S(2)}) collective-permute-start(f32[16,24,128]{2,1,0:T(8,128)S(1)} %constant_dynamic-update-slice_fusion.4), channel_id=1, source_target_pairs={{0,64},{64,0},{128,192},{192,128},{16,208},{80,144},{144,80},{208,... | collective-permute-start | bytes 589832 | tf_op jit(solution)/shard_map/ppermute | solution.py:291
  78.3 16.6 %collective-permute-start.21 = (f32[64,16,128]{2,1,0:T(8,128)S(1)}, f32[64,16,128]{2,1,0:T(8,128)S(1)}, u32[]{:S(2)}, u32[]{:S(2)}) collective-permute-start(f32[64,16,128]{2,1,0:T(8,128)S(1)} %constant_dynamic-update-slice_fusion.6.x_own), channel_id=1, source_target_pairs={{0,16},{16,0},{1,17},{17,1},{2,18},{18,2},{3,19},{19,3},{4,20},{20... | collective-permute-start | bytes 1572872 | tf_op jit(solution)/shard_map/ppermute | solution.py:284
  89.7 9.9 %collective-permute-start.20 = (f32[32,24,128]{2,1,0:T(8,128)S(1)}, f32[32,24,128]{2,1,0:T(8,128)S(1)}, u32[]{:S(2)}, u32[]{:S(2)}) collective-permute-start(f32[32,24,128]{2,1,0:T(8,128)S(1)} %constant_dynamic-update-slice_fusion.10), channel_id=1, source_target_pairs={{0,192},{64,128},{128,64},{192,0},{16,80},{80,16},{144,208},{208,1... | collective-permute-start | bytes 1179656 | tf_op jit(solution)/shard_map/ppermute | solution.py:291
  94.1 9.8 %collective-permute-start.19 = (f32[32,24,128]{2,1,0:T(8,128)S(1)}, f32[32,24,128]{2,1,0:T(8,128)S(1)}, u32[]{:S(2)}, u32[]{:S(2)}) collective-permute-start(f32[32,24,128]{2,1,0:T(8,128)S(1)} %constant_dynamic-update-slice_fusion.12), channel_id=1, source_target_pairs={{0,192},{64,128},{128,64},{192,0},{16,80},{80,16},{144,208},{208,1... | collective-permute-start | bytes 1179656 | tf_op jit(solution)/shard_map/ppermute | solution.py:291
  103.7 9.2 %collective-permute-start.23 = (f32[64,16,128]{2,1,0:T(8,128)S(1)}, f32[64,16,128]{2,1,0:T(8,128)S(1)}, u32[]{:S(2)}, u32[]{:S(2)}) collective-permute-start(f32[64,16,128]{2,1,0:T(8,128)S(1)} %get-tuple-element.219), channel_id=1, source_target_pairs={{0,4},{4,0},{8,12},{12,8},{16,28},{20,24},{24,20},{28,16},{1,5},{5... | collective-permute-start | bytes 1572872 | tf_op jit(solution)/shard_map/ppermute | solution.py:291
  103.9 9.2 %collective-permute-start.22 = (f32[64,24,128]{2,1,0:T(8,128)S(1)}, f32[64,24,128]{2,1,0:T(8,128)S(1)}, u32[]{:S(2)}, u32[]{:S(2)}) collective-permute-start(f32[64,24,128]{2,1,0:T(8,128)S(1)} %constant_dynamic-update-slice_fusion.16.x_own), channel_id=1, source_target_pairs={{0,16},{16,0},{1,17},{17,1},{2,18},{18,2},{3,19},{19,3},{4,20},{20... | collective-permute-start | bytes 2359304 | tf_op jit(solution)/shard_map/ppermute | solution.py:284
  111.0 14.9 %collective-permute-start.28 = (f32[64,24,128]{2,1,0:T(8,128)S(1)}, f32[64,24,128]{2,1,0:T(8,128)S(1)}, u32[]{:S(2)}, u32[]{:S(2)}) collective-permute-start(f32[64,24,128]{2,1,0:T(8,128)S(1)} %get-tuple-element.228), channel_id=1, source_target_pairs={{0,4},{4,0},{8,12},{12,8},{16,28},{20,24},{24,20},{28,16},{1,5},{5... | collective-permute-start | bytes 2359304 | tf_op jit(solution)/shard_map/ppermute | solution.py:291
  113.0 8.4 %collective-permute-start.26 = (f32[32,16,128]{2,1,0:T(8,128)S(1)}, f32[32,16,128]{2,1,0:T(8,128)S(1)}, u32[]{:S(2)}, u32[]{:S(2)}) collective-permute-start(f32[32,16,128]{2,1,0:T(8,128)S(1)} %slice_add_fusion.4), channel_id=1, source_target_pairs={{0,12},{4,8},{8,4},{12,0},{16,20},{20,16},{24,28},{28,24},{1,13},{... | collective-permute-start | bytes 786440 | tf_op jit(solution)/shard_map/ppermute | solution.py:291
  116.1 21.2 %collective-permute-start.25 = (f32[64,24,128]{2,1,0:T(8,128)S(1)}, f32[64,24,128]{2,1,0:T(8,128)S(1)}, u32[]{:S(2)}, u32[]{:S(2)}) collective-permute-start(f32[64,24,128]{2,1,0:T(8,128)S(1)} %get-tuple-element.236), channel_id=1, source_target_pairs={{0,4},{4,0},{8,12},{12,8},{16,28},{20,24},{24,20},{28,16},{1,5},{5... | collective-permute-start | bytes 2359304 | tf_op jit(solution)/shard_map/ppermute | solution.py:291
  126.0 11.5 %collective-permute-start.31 = (f32[32,24,128]{2,1,0:T(8,128)S(1)}, f32[32,24,128]{2,1,0:T(8,128)S(1)}, u32[]{:S(2)}, u32[]{:S(2)}) collective-permute-start(f32[32,24,128]{2,1,0:T(8,128)S(1)} %slice_add_fusion.1), channel_id=1, source_target_pairs={{0,12},{4,8},{8,4},{12,0},{16,20},{20,16},{24,28},{28,24},{1,13},{... | collective-permute-start | bytes 1179656 | tf_op jit(solution)/shard_map/ppermute | solution.py:291
  127.5 11.6 %collective-permute-start.30 = (f32[8,16,128]{2,1,0:T(8,128)S(1)}, f32[8,16,128]{2,1,0:T(8,128)S(1)}, u32[]{:S(2)}, u32[]{:S(2)}) collective-permute-start(f32[8,16,128]{2,1,0:T(8,128)S(1)} %slice_add_fusion.16), channel_id=1, source_target_pairs={{0,3},{1,2},{2,1},{3,0},{16,17},{17,16},{18,19},{19,18},{4,7},{5,6... | collective-permute-start | bytes 196616 | tf_op jit(solution)/shard_map/ppermute | solution.py:291
  145.9 12.8 %collective-permute-start.36 = (f32[8,24,128]{2,1,0:T(8,128)S(1)}, f32[8,24,128]{2,1,0:T(8,128)S(1)}, u32[]{:S(2)}, u32[]{:S(2)}) collective-permute-start(f32[8,24,128]{2,1,0:T(8,128)S(1)} %slice_add_fusion.13), channel_id=1, source_target_pairs={{0,3},{1,2},{2,1},{3,0},{16,17},{17,16},{18,19},{19,18},{4,7},{5,6... | collective-permute-start | bytes 294920 | tf_op jit(solution)/shard_map/ppermute | solution.py:291
  153.7 11.5 %collective-permute-start.39 = (f32[32,16,128]{2,1,0:T(8,128)S(1)}, f32[32,16,128]{2,1,0:T(8,128)S(1)}, u32[]{:S(2)}, u32[]{:S(2)}) collective-permute-start(f32[32,16,128]{2,1,0:T(8,128)S(1)} %constant_dynamic-update-slice_fusion.20), channel_id=1, source_target_pairs={{0,192},{64,128},{128,64},{192,0},{16,80},{80,16},{144,208},{208,1... | collective-permute-start | bytes 786440 | tf_op jit(solution)/shard_map/ppermute | solution.py:291
  159.4 12.2 %collective-permute-start.38 = (f32[8,24,128]{2,1,0:T(8,128)S(1)}, f32[8,24,128]{2,1,0:T(8,128)S(1)}, u32[]{:S(2)}, u32[]{:S(2)}) collective-permute-start(f32[8,24,128]{2,1,0:T(8,128)S(1)} %multiply_subtract_fusion), channel_id=1, source_target_pairs={{0,32},{32,0},{1,33},{33,1},{2,34},{34,2},{3,35},{35,3},{4,36},{36... | collective-permute-start | bytes 294920 | tf_op jit(solution)/shard_map/ppermute | solution.py:284
  162.3 12.3 %collective-permute-start.42 = (f32[16,24,128]{2,1,0:T(8,128)S(1)}, f32[16,24,128]{2,1,0:T(8,128)S(1)}, u32[]{:S(2)}, u32[]{:S(2)}) collective-permute-start(f32[16,24,128]{2,1,0:T(8,128)S(1)} %constant_dynamic-update-slice_fusion.22), channel_id=1, source_target_pairs={{0,64},{64,0},{128,192},{192,128},{16,208},{80,144},{144,80},{208,... | collective-permute-start | bytes 589832 | tf_op jit(solution)/shard_map/ppermute | solution.py:291
  165.2 12.6 %collective-permute-start.45 = (f32[64,16,128]{2,1,0:T(8,128)S(1)}, f32[64,16,128]{2,1,0:T(8,128)S(1)}, u32[]{:S(2)}, u32[]{:S(2)}) collective-permute-start(f32[64,16,128]{2,1,0:T(8,128)S(1)} %constant_dynamic-update-slice_fusion.24.x_own), channel_id=1, source_target_pairs={{0,16},{16,0},{1,17},{17,1},{2,18},{18,2},{3,19},{19,3},{4,20},{20... | collective-permute-start | bytes 1572872 | tf_op jit(solution)/shard_map/ppermute | solution.py:284
  181.7 8.5 %collective-permute-start.47 = (f32[64,24,128]{2,1,0:T(8,128)S(1)}, f32[64,24,128]{2,1,0:T(8,128)S(1)}, u32[]{:S(2)}, u32[]{:S(2)}) collective-permute-start(f32[64,24,128]{2,1,0:T(8,128)S(1)} %constant_dynamic-update-slice_fusion.32.x_own), channel_id=1, source_target_pairs={{0,16},{16,0},{1,17},{17,1},{2,18},{18,2},{3,19},{19,3},{4,20},{20... | collective-permute-start | bytes 2359304 | tf_op jit(solution)/shard_map/ppermute | solution.py:284
  (17 other events, 106.9 us)

commit v4 on v3

--- a/solution.py
+++ b/solution.py
@@ -10,7 +10,7 @@
 B = 128
 BLK = 128
 CAP = 163
-CHUNKS = (32, 16)
+CHUNKS = (32, 32)
 VEC = 64
 SIZES = (16, 24, 24)
 FIRST = tuple(sum(SIZES[:g]) for g in range(len(SIZES)))
@@ -169,7 +169,7 @@
     n = 2 * len(SIZES)
     outs = pl.pallas_call(
         first_kernel,
-        out_shape=[pltpu.VMEM((64, v, B), jnp.float32) for v in SIZES for _ in range(2)]
+        out_shape=[jax.ShapeDtypeStruct((64, v, B), jnp.float32) for v in SIZES for _ in range(2)]
         + [pltpu.VMEM((8, VEC, B), jnp.float32)] * 2,
         in_specs=[pl.BlockSpec(memory_space=pltpu.SMEM)] + [free] * 5,
         out_specs=[free] * n + [vmem] * 2,

time: 194 us -> 196 us (1.010); the launches traced: 194 us -> 199 us
  waiting for transfers between devices: 52.8 us -> 60.9 us
  starting transfers between devices: 107 us -> 98.9 us
  Pallas kernels: 18.1 us -> 22.9 us
    ppermute x36, starting transfers between devices: 67.6 us -> 59.5 us  [exchange(): return lax.ppermute(value, both, pairs)]
    ppermute x36, waiting for transfers between devices: 49.3 us -> 55.8 us  [exchange(): return lax.ppermute(value, both, pairs)]
    pallas_call x3, Pallas kernels: 8.99 us -> 12.5 us  [second_products(): pl.pallas_call(functools.partial(second_kernel, FIRST[g]), out_shape=[plt...]
  transfers between devices with their start and end apart: 48 -> 48, of which waited for: 21 -> 21; matrix products, arithmetic and copies ran while one was open for 6% -> 6% of each run, Pallas kernels for 6% -> 8%
where the time goes in v4:
time: 196 us; the launch traced here: 199 us
  starting transfers between devices  98.9 us (50%)
  waiting for transfers between devices  60.9 us (31%)
  Pallas kernels  22.9 us (12%)
  other arithmetic  11.6 us (6%)
  between operations  3.29 us (2%)
    ppermute x36, starting transfers between devices, exchange(): return lax.ppermute(value, both, pairs)  59.5 us
    ppermute x36, waiting for transfers between devices, exchange(): return lax.ppermute(value, both, pairs)  55.8 us
    ppermute x12, starting transfers between devices, swap(): return lax.ppermute(value, axis, [(0, 1), (1, 0)])  39.4 us
    pallas_call x3, Pallas kernels, second_products(): pl.pallas_call(functools.partial(second_kernel, FIRST[g]), out_shape=[plt...  12.5 us
    add x18, other arithmetic, body(): token = functools.reduce(jnp.add, [piece[half:2 * half] for piece in kept])  8.72 us
    pallas_call x1, Pallas kernels, first_products(): pl.pallas_call(first_kernel, out_shape=[jax.ShapeDtypeStruct((64, v, B),...  6.37 us
    ppermute x12, waiting for transfers between devices, swap(): return lax.ppermute(value, axis, [(0, 1), (1, 0)])  5.11 us
    pallas_call x3, Pallas kernels, assemble(): pl.pallas_call(functools.partial(assemble_kernel, FIRST[g], v), out_shape...  4.03 us
  transfers between devices with their start and end apart: 48, of which 21 were waited for; matrix products, arithmetic and copies ran while one was open for 6% of the time, Pallas kernels for 8%

profile of v4, /device:TPU:1, one launch (start us, length us, event | category | flops | bytes accessed | tf_op | source)
XLA Modules:
  0.0 199.0 jit_solution(9396840652259796568)
XLA Ops:
  1.3 6.4 %first.1 = (f32[64,16,128]{2,1,0:T(8,128)S(1)}, f32[64,16,128]{2,1,0:T(8,128)S(1)}, f32[64,24,128]{2,1,0:T(8,128)S(1)}, f32[64,24,128]{2,1,0:T(8,128)}, f32[64,2...) custom-call(s32[1,1]{1,0:T(1,128)S(6)} %copy.36.live, ...), custom_call_target="tpu_custom_call" | custom-call | flops 1 | bytes 1 | tf_op jit(solution)/shard_map/first/pallas_call | solution.py:170
  7.7 3.6 %collective-permute-start.2 = (f32[64,16,128]{2,1,0:T(8,128)S(1)}, f32[64,16,128]{2,1,0:T(8,128)S(1)}, u32[]{:S(2)}, u32[]{:S(2)}) collective-permute-start(f32[64,16,128]{2,1,0:T(8,128)S(1)} %get-tuple-element.158), channel_id=1, source_target_pairs={{0,4},{4,0},{8,12},{12,8},{16,28},{20,24},{24,20},{28,16},{1,5},{5... | collective-permute-start | bytes 1572872 | tf_op jit(solution)/shard_map/ppermute | solution.py:291
  11.4 2.6 %collective-permute-start = (f32[64,24,128]{2,1,0:T(8,128)S(1)}, f32[64,24,128]{2,1,0:T(8,128)}, u32[]{:S(2)}, u32[]{:S(2)}) collective-permute-start(f32[64,24,128]{2,1,0:T(8,128)S(1)} %get-tuple-element.153), channel_id=1, source_target_pairs={{0,4},{4,0},{8,12},{12,8},{16,28},{20,24},{24,20},{28,16},{1,5},{5... | collective-permute-start | bytes 2359304 | tf_op jit(solution)/shard_map/ppermute | solution.py:291
  14.0 3.9 %collective-permute-done.2 = f32[64,16,128]{2,1,0:T(8,128)S(1)} collective-permute-done((f32[64,16,128]{2,1,0:T(8,128)S(1)}, f32[64,16,128]{2,1,0:T(8,128)S(1)}, u32[]{:S(2)}, u32[]{:S(2)}) %collective-permute-start.2) | collective-permute-done | bytes 524320 | tf_op jit(solution)/shard_map/ppermute | solution.py:291
  22.5 5.9 %collective-permute-done.3 = f32[32,16,128]{2,1,0:T(8,128)} collective-permute-done((f32[32,16,128]{2,1,0:T(8,128)}, f32[32,16,128]{2,1,0:T(8,128)}, u32[]{:S(2)}, u32[]{:S(2)}) %collective-permute-start.3) | collective-permute-done | bytes 262176 | tf_op jit(solution)/shard_map/ppermute | solution.py:291
  29.4 5.8 %collective-permute-start.6 = (f32[16,16,128]{2,1,0:T(8,128)S(1)}, f32[16,16,128]{2,1,0:T(8,128)S(1)}, u32[]{:S(2)}, u32[]{:S(2)}) collective-permute-start(f32[16,16,128]{2,1,0:T(8,128)S(1)} %slice_add_fusion.11), channel_id=1, source_target_pairs={{0,1},{1,0},{2,3},{3,2},{16,19},{17,18},{18,17},{19,16},{4,5},{5,4... | collective-permute-start | bytes 393224 | tf_op jit(solution)/shard_map/ppermute | solution.py:291
  41.1 5.6 %collective-permute-start.8 = (f32[8,16,128]{2,1,0:T(8,128)S(1)}, f32[8,16,128]{2,1,0:T(8,128)S(1)}, u32[]{:S(2)}, u32[]{:S(2)}) collective-permute-start(f32[8,16,128]{2,1,0:T(8,128)S(1)} %slice_add_fusion.17), channel_id=1, source_target_pairs={{0,3},{1,2},{2,1},{3,0},{16,17},{17,16},{18,19},{19,18},{4,7},{5,6... | collective-permute-start | bytes 196616 | tf_op jit(solution)/shard_map/ppermute | solution.py:291
  47.7 5.3 %collective-permute-start.10 = (f32[16,24,128]{2,1,0:T(8,128)S(1)}, f32[16,24,128]{2,1,0:T(8,128)S(1)}, u32[]{:S(2)}, u32[]{:S(2)}) collective-permute-start(f32[16,24,128]{2,1,0:T(8,128)S(1)} %slice_add_fusion.9), channel_id=1, source_target_pairs={{0,1},{1,0},{2,3},{3,2},{16,19},{17,18},{18,17},{19,16},{4,5},{5,4... | collective-permute-start | bytes 589832 | tf_op jit(solution)/shard_map/ppermute | solution.py:291
  55.5 3.5 %collective-permute-done.10 = f32[16,24,128]{2,1,0:T(8,128)S(1)} collective-permute-done((f32[16,24,128]{2,1,0:T(8,128)S(1)}, f32[16,24,128]{2,1,0:T(8,128)S(1)}, u32[]{:S(2)}, u32[]{:S(2)}) %collective-permute-start.10) | collective-permute-done | bytes 196640 | tf_op jit(solution)/shard_map/ppermute | solution.py:291
  65.0 3.4 %collective-permute-done.13 = f32[16,16,128]{2,1,0:T(8,128)S(1)} collective-permute-done((f32[16,16,128]{2,1,0:T(8,128)S(1)}, f32[16,16,128]{2,1,0:T(8,128)S(1)}, u32[]{:S(2)}, u32[]{:S(2)}) %collective-permute-start.13) | collective-permute-done | bytes 131104 | tf_op jit(solution)/shard_map/ppermute | solution.py:291
  68.4 2.9 %collective-permute-start.15 = (f32[32,16,128]{2,1,0:T(8,128)S(1)}, f32[32,16,128]{2,1,0:T(8,128)S(1)}, u32[]{:S(2)}, u32[]{:S(2)}) collective-permute-start(f32[32,16,128]{2,1,0:T(8,128)S(1)} %constant_dynamic-update-slice_fusion.2), channel_id=1, source_target_pairs={{0,192},{64,128},{128,64},{192,0},{16,80},{80,16},{144,208},{208,1... | collective-permute-start | bytes 786440 | tf_op jit(solution)/shard_map/ppermute | solution.py:291
  76.0 3.8 %collective-permute-start.18 = (f32[16,24,128]{2,1,0:T(8,128)S(1)}, f32[16,24,128]{2,1,0:T(8,128)S(1)}, u32[]{:S(2)}, u32[]{:S(2)}) collective-permute-start(f32[16,24,128]{2,1,0:T(8,128)S(1)} %constant_dynamic-update-slice_fusion.4), channel_id=1, source_target_pairs={{0,64},{64,0},{128,192},{192,128},{16,208},{80,144},{144,80},{208,... | collective-permute-start | bytes 589832 | tf_op jit(solution)/shard_map/ppermute | solution.py:291
  79.8 11.4 %collective-permute-start.21 = (f32[64,16,128]{2,1,0:T(8,128)S(1)}, f32[64,16,128]{2,1,0:T(8,128)S(1)}, u32[]{:S(2)}, u32[]{:S(2)}) collective-permute-start(f32[64,16,128]{2,1,0:T(8,128)S(1)} %constant_dynamic-update-slice_fusion.6.x_own), channel_id=1, source_target_pairs={{0,16},{16,0},{1,17},{17,1},{2,18},{18,2},{3,19},{19,3},{4,20},{20... | collective-permute-start | bytes 1572872 | tf_op jit(solution)/shard_map/ppermute | solution.py:284
  92.4 4.7 %collective-permute-done.17 = f32[16,24,128]{2,1,0:T(8,128)S(1)} collective-permute-done((f32[16,24,128]{2,1,0:T(8,128)S(1)}, f32[16,24,128]{2,1,0:T(8,128)S(1)}, u32[]{:S(2)}, u32[]{:S(2)}) %collective-permute-start.17) | collective-permute-done | bytes 196640 | tf_op jit(solution)/shard_map/ppermute | solution.py:291
  97.3 4.0 %second.3 = (f32[64,16,128]{2,1,0:T(8,128)S(1)}, f32[64,16,128]{2,1,0:T(8,128)S(1)}, f32[64,16384]{1,0:T(8,128)}) custom-call(s32[1,1]{1,0:T(1,128)S(6)} %copy.36.live, s32[1,1,163]{2,1,0:T(1,128)} %rows_in.7, s32[1,1,163]{2,1,0:T(1,128)} %cols_in.7, f32[1,1,163,128,128]{4,3,2,1,0:T(8,128)} %tiles.7, ...), custom_call_target="tpu_custom_call" | custom-call | flops 1 | bytes 1 | tf_op jit(solution)/shard_map/second/pallas_call | solution.py:236
  101.4 3.6 %collective-permute-start.24 = (f32[64,24,128]{2,1,0:T(8,128)S(1)}, f32[64,24,128]{2,1,0:T(8,128)S(1)}, u32[]{:S(2)}, u32[]{:S(2)}) collective-permute-start(f32[64,24,128]{2,1,0:T(8,128)S(1)} %constant_dynamic-update-slice_fusion.14.x_own), channel_id=1, source_target_pairs={{0,16},{16,0},{1,17},{17,1},{2,18},{18,2},{3,19},{19,3},{4,20},{20... | collective-permute-start | bytes 2359304 | tf_op jit(solution)/shard_map/ppermute | solution.py:284
  105.6 3.6 %collective-permute-start.22 = (f32[64,24,128]{2,1,0:T(8,128)S(1)}, f32[64,24,128]{2,1,0:T(8,128)S(1)}, u32[]{:S(2)}, u32[]{:S(2)}) collective-permute-start(f32[64,24,128]{2,1,0:T(8,128)S(1)} %constant_dynamic-update-slice_fusion.16.x_own), channel_id=1, source_target_pairs={{0,16},{16,0},{1,17},{17,1},{2,18},{18,2},{3,19},{19,3},{4,20},{20... | collective-permute-start | bytes 2359304 | tf_op jit(solution)/shard_map/ppermute | solution.py:284
  109.2 4.2 %second.4 = (f32[64,24,128]{2,1,0:T(8,128)S(1)}, f32[64,24,128]{2,1,0:T(8,128)S(1)}, f32[64,16384]{1,0:T(8,128)}) custom-call(s32[1,1]{1,0:T(1,128)S(6)} %copy.36.live, s32[1,1,163]{2,1,0:T(1,128)} %rows_in.7, s32[1,1,163]{2,1,0:T(1,128)} %cols_in.7, f32[1,1,163,128,128]{4,3,2,1,0:T(8,128)} %tiles.7, ...), custom_call_target="tpu_custom_call", output_to_operand_aliasing={{2}: (6, {})} | custom-call | flops 1 | bytes 1 | tf_op jit(solution)/shard_map/second/pallas_call | solution.py:236
  114.4 4.3 %second.5 = (f32[64,24,128]{2,1,0:T(8,128)S(1)}, f32[64,24,128]{2,1,0:T(8,128)S(1)}, f32[64,16384]{1,0:T(8,128)}) custom-call(s32[1,1]{1,0:T(1,128)S(6)} %copy.36.live, s32[1,1,163]{2,1,0:T(1,128)} %rows_in.7, s32[1,1,163]{2,1,0:T(1,128)} %cols_in.7, f32[1,1,163,128,128]{4,3,2,1,0:T(8,128)} %tiles.7, ...), custom_call_target="tpu_custom_call", output_to_operand_aliasing={{2}: (6, {})} | custom-call | flops 1 | bytes 1 | tf_op jit(solution)/shard_map/second/pallas_call | solution.py:236
  122.8 4.1 %collective-permute-start.27 = (f32[16,16,128]{2,1,0:T(8,128)S(1)}, f32[16,16,128]{2,1,0:T(8,128)S(1)}, u32[]{:S(2)}, u32[]{:S(2)}) collective-permute-start(f32[16,16,128]{2,1,0:T(8,128)S(1)} %slice_add_fusion.10), channel_id=1, source_target_pairs={{0,1},{1,0},{2,3},{3,2},{16,19},{17,18},{18,17},{19,16},{4,5},{5,4... | collective-permute-start | bytes 393224 | tf_op jit(solution)/shard_map/ppermute | solution.py:291
  129.4 4.1 %collective-permute-start.30 = (f32[8,16,128]{2,1,0:T(8,128)S(1)}, f32[8,16,128]{2,1,0:T(8,128)S(1)}, u32[]{:S(2)}, u32[]{:S(2)}) collective-permute-start(f32[8,16,128]{2,1,0:T(8,128)S(1)} %slice_add_fusion.16), channel_id=1, source_target_pairs={{0,3},{1,2},{2,1},{3,0},{16,17},{17,16},{18,19},{19,18},{4,7},{5,6... | collective-permute-start | bytes 196616 | tf_op jit(solution)/shard_map/ppermute | solution.py:291
  133.4 7.6 %collective-permute-done.25 = f32[64,24,128]{2,1,0:T(8,128)S(1)} collective-permute-done((f32[64,24,128]{2,1,0:T(8,128)S(1)}, f32[64,24,128]{2,1,0:T(8,128)S(1)}, u32[]{:S(2)}, u32[]{:S(2)}) %collective-permute-start.25) | collective-permute-done | bytes 786464 | tf_op jit(solution)/shard_map/ppermute | solution.py:291
  141.5 2.7 %collective-permute-start.34 = (f32[16,24,128]{2,1,0:T(8,128)S(1)}, f32[16,24,128]{2,1,0:T(8,128)S(1)}, u32[]{:S(2)}, u32[]{:S(2)}) collective-permute-start(f32[16,24,128]{2,1,0:T(8,128)S(1)} %slice_add_fusion.7), channel_id=1, source_target_pairs={{0,1},{1,0},{2,3},{3,2},{16,19},{17,18},{18,17},{19,16},{4,5},{5,4... | collective-permute-start | bytes 589832 | tf_op jit(solution)/shard_map/ppermute | solution.py:291
  144.4 4.0 %collective-permute-done.29 = f32[32,24,128]{2,1,0:T(8,128)S(1)} collective-permute-done((f32[32,24,128]{2,1,0:T(8,128)S(1)}, f32[32,24,128]{2,1,0:T(8,128)S(1)}, u32[]{:S(2)}, u32[]{:S(2)}) %collective-permute-start.29) | collective-permute-done | bytes 393248 | tf_op jit(solution)/shard_map/ppermute | solution.py:291
  148.4 2.7 %collective-permute-start.32 = (f32[16,24,128]{2,1,0:T(8,128)S(1)}, f32[16,24,128]{2,1,0:T(8,128)S(1)}, u32[]{:S(2)}, u32[]{:S(2)}) collective-permute-start(f32[16,24,128]{2,1,0:T(8,128)S(1)} %slice_add_fusion.6), channel_id=1, source_target_pairs={{0,1},{1,0},{2,3},{3,2},{16,19},{17,18},{18,17},{19,16},{4,5},{5,4... | collective-permute-start | bytes 589832 | tf_op jit(solution)/shard_map/ppermute | solution.py:291
  153.7 5.5 %collective-permute-done.32 = f32[16,24,128]{2,1,0:T(8,128)S(1)} collective-permute-done((f32[16,24,128]{2,1,0:T(8,128)S(1)}, f32[16,24,128]{2,1,0:T(8,128)S(1)}, u32[]{:S(2)}, u32[]{:S(2)}) %collective-permute-start.32) | collective-permute-done | bytes 196640 | tf_op jit(solution)/shard_map/ppermute | solution.py:291
  160.5 3.4 %collective-permute-done.35 = f32[8,24,128]{2,1,0:T(8,128)S(1)} collective-permute-done((f32[8,24,128]{2,1,0:T(8,128)S(1)}, f32[8,24,128]{2,1,0:T(8,128)S(1)}, u32[]{:S(2)}, u32[]{:S(2)}) %collective-permute-start.35) | collective-permute-done | bytes 98336 | tf_op jit(solution)/shard_map/ppermute | solution.py:291
  165.8 9.5 %collective-permute-start.45 = (f32[64,16,128]{2,1,0:T(8,128)S(1)}, f32[64,16,128]{2,1,0:T(8,128)S(1)}, u32[]{:S(2)}, u32[]{:S(2)}) collective-permute-start(f32[64,16,128]{2,1,0:T(8,128)S(1)} %constant_dynamic-update-slice_fusion.24.x_own), channel_id=1, source_target_pairs={{0,16},{16,0},{1,17},{17,1},{2,18},{18,2},{3,19},{19,3},{4,20},{20... | collective-permute-start | bytes 1572872 | tf_op jit(solution)/shard_map/ppermute | solution.py:284
  177.2 3.9 %collective-permute-done.41 = f32[16,24,128]{2,1,0:T(8,128)S(1)} collective-permute-done((f32[16,24,128]{2,1,0:T(8,128)S(1)}, f32[16,24,128]{2,1,0:T(8,128)S(1)}, u32[]{:S(2)}, u32[]{:S(2)}) %collective-permute-start.41) | collective-permute-done | bytes 196640 | tf_op jit(solution)/shard_map/ppermute | solution.py:291
  183.2 3.4 %collective-permute-done.44 = f32[32,24,128]{2,1,0:T(8,128)S(1)} collective-permute-done((f32[32,24,128]{2,1,0:T(8,128)S(1)}, f32[32,24,128]{2,1,0:T(8,128)S(1)}, u32[]{:S(2)}, u32[]{:S(2)}) %collective-permute-start.44) | collective-permute-done | bytes 393248 | tf_op jit(solution)/shard_map/ppermute | solution.py:291
  186.7 4.6 %collective-permute-start.47 = (f32[64,24,128]{2,1,0:T(8,128)S(1)}, f32[64,24,128]{2,1,0:T(8,128)S(1)}, u32[]{:S(2)}, u32[]{:S(2)}) collective-permute-start(f32[64,24,128]{2,1,0:T(8,128)S(1)} %constant_dynamic-update-slice_fusion.32.x_own), channel_id=1, source_target_pairs={{0,16},{16,0},{1,17},{17,1},{2,18},{18,2},{3,19},{19,3},{4,20},{20... | collective-permute-start | bytes 2359304 | tf_op jit(solution)/shard_map/ppermute | solution.py:284
  191.4 4.1 %collective-permute-start.46 = (f32[64,24,128]{2,1,0:T(8,128)S(1)}, f32[64,24,128]{2,1,0:T(8,128)S(1)}, u32[]{:S(2)}, u32[]{:S(2)}) collective-permute-start(f32[64,24,128]{2,1,0:T(8,128)S(1)} %constant_dynamic-update-slice_fusion.34.x_own), channel_id=1, source_target_pairs={{0,16},{16,0},{1,17},{17,1},{2,18},{18,2},{3,19},{19,3},{4,20},{20... | collective-permute-start | bytes 2359304 | tf_op jit(solution)/shard_map/ppermute | solution.py:284
  (133 shorter events, 47.5 us)
Async XLA Ops:
  7.7 10.2 %collective-permute-start.2 = (f32[64,16,128]{2,1,0:T(8,128)S(1)}, f32[64,16,128]{2,1,0:T(8,128)S(1)}, u32[]{:S(2)}, u32[]{:S(2)}) collective-permute-start(f32[64,16,128]{2,1,0:T(8,128)S(1)} %get-tuple-element.158), channel_id=1, source_target_pairs={{0,4},{4,0},{8,12},{12,8},{16,28},{20,24},{24,20},{28,16},{1,5},{5... | collective-permute-start | bytes 1572872 | tf_op jit(solution)/shard_map/ppermute | solution.py:291
  11.3 23.9 %collective-permute-start.1 = (f32[64,24,128]{2,1,0:T(8,128)}, f32[64,24,128]{2,1,0:T(8,128)}, u32[]{:S(2)}, u32[]{:S(2)}) collective-permute-start(f32[64,24,128]{2,1,0:T(8,128)} %get-tuple-element.155), channel_id=1, source_target_pairs={{0,4},{4,0},{8,12},{12,8},{16,28},{20,24},{24,20},{28,16},{1,5},{5... | collective-permute-start | bytes 2359304 | tf_op jit(solution)/shard_map/ppermute | solution.py:291
  11.4 26.3 %collective-permute-start = (f32[64,24,128]{2,1,0:T(8,128)S(1)}, f32[64,24,128]{2,1,0:T(8,128)}, u32[]{:S(2)}, u32[]{:S(2)}) collective-permute-start(f32[64,24,128]{2,1,0:T(8,128)S(1)} %get-tuple-element.153), channel_id=1, source_target_pairs={{0,4},{4,0},{8,12},{12,8},{16,28},{20,24},{24,20},{28,16},{1,5},{5... | collective-permute-start | bytes 2359304 | tf_op jit(solution)/shard_map/ppermute | solution.py:291
  19.4 9.0 %collective-permute-start.3 = (f32[32,16,128]{2,1,0:T(8,128)}, f32[32,16,128]{2,1,0:T(8,128)}, u32[]{:S(2)}, u32[]{:S(2)}) collective-permute-start(f32[32,16,128]{2,1,0:T(8,128)} %slice_add_fusion.5), channel_id=1, source_target_pairs={{0,12},{4,8},{8,4},{12,0},{16,20},{20,16},{24,28},{28,24},{1,13},{... | collective-permute-start | bytes 786440 | tf_op jit(solution)/shard_map/ppermute | solution.py:291
  29.4 10.8 %collective-permute-start.6 = (f32[16,16,128]{2,1,0:T(8,128)S(1)}, f32[16,16,128]{2,1,0:T(8,128)S(1)}, u32[]{:S(2)}, u32[]{:S(2)}) collective-permute-start(f32[16,16,128]{2,1,0:T(8,128)S(1)} %slice_add_fusion.11), channel_id=1, source_target_pairs={{0,1},{1,0},{2,3},{3,2},{16,19},{17,18},{18,17},{19,16},{4,5},{5,4... | collective-permute-start | bytes 393224 | tf_op jit(solution)/shard_map/ppermute | solution.py:291
  36.2 10.4 %collective-permute-start.5 = (f32[32,24,128]{2,1,0:T(8,128)S(1)}, f32[32,24,128]{2,1,0:T(8,128)S(1)}, u32[]{:S(2)}, u32[]{:S(2)}) collective-permute-start(f32[32,24,128]{2,1,0:T(8,128)S(1)} %slice_add_fusion.3), channel_id=1, source_target_pairs={{0,12},{4,8},{8,4},{12,0},{16,20},{20,16},{24,28},{28,24},{1,13},{... | collective-permute-start | bytes 1179656 | tf_op jit(solution)/shard_map/ppermute | solution.py:291
  38.7 14.3 %collective-permute-start.4 = (f32[32,24,128]{2,1,0:T(8,128)S(1)}, f32[32,24,128]{2,1,0:T(8,128)S(1)}, u32[]{:S(2)}, u32[]{:S(2)}) collective-permute-start(f32[32,24,128]{2,1,0:T(8,128)S(1)} %slice_add_fusion.2), channel_id=1, source_target_pairs={{0,12},{4,8},{8,4},{12,0},{16,20},{20,16},{24,28},{28,24},{1,13},{... | collective-permute-start | bytes 1179656 | tf_op jit(solution)/shard_map/ppermute | solution.py:291
  41.1 13.0 %collective-permute-start.8 = (f32[8,16,128]{2,1,0:T(8,128)S(1)}, f32[8,16,128]{2,1,0:T(8,128)S(1)}, u32[]{:S(2)}, u32[]{:S(2)}) collective-permute-start(f32[8,16,128]{2,1,0:T(8,128)S(1)} %slice_add_fusion.17), channel_id=1, source_target_pairs={{0,3},{1,2},{2,1},{3,0},{16,17},{17,16},{18,19},{19,18},{4,7},{5,6... | collective-permute-start | bytes 196616 | tf_op jit(solution)/shard_map/ppermute | solution.py:291
  47.7 11.4 %collective-permute-start.10 = (f32[16,24,128]{2,1,0:T(8,128)S(1)}, f32[16,24,128]{2,1,0:T(8,128)S(1)}, u32[]{:S(2)}, u32[]{:S(2)}) collective-permute-start(f32[16,24,128]{2,1,0:T(8,128)S(1)} %slice_add_fusion.9), channel_id=1, source_target_pairs={{0,1},{1,0},{2,3},{3,2},{16,19},{17,18},{18,17},{19,16},{4,5},{5,4... | collective-permute-start | bytes 589832 | tf_op jit(solution)/shard_map/ppermute | solution.py:291
  54.0 10.0 %collective-permute-start.7 = (f32[16,24,128]{2,1,0:T(8,128)S(1)}, f32[16,24,128]{2,1,0:T(8,128)S(1)}, u32[]{:S(2)}, u32[]{:S(2)}) collective-permute-start(f32[16,24,128]{2,1,0:T(8,128)S(1)} %slice_add_fusion.8), channel_id=1, source_target_pairs={{0,1},{1,0},{2,3},{3,2},{16,19},{17,18},{18,17},{19,16},{4,5},{5,4... | collective-permute-start | bytes 589832 | tf_op jit(solution)/shard_map/ppermute | solution.py:291
  60.0 11.3 %collective-permute-start.12 = (f32[8,24,128]{2,1,0:T(8,128)S(1)}, f32[8,24,128]{2,1,0:T(8,128)S(1)}, u32[]{:S(2)}, u32[]{:S(2)}) collective-permute-start(f32[8,24,128]{2,1,0:T(8,128)S(1)} %slice_add_fusion.15), channel_id=1, source_target_pairs={{0,3},{1,2},{2,1},{3,0},{16,17},{17,16},{18,19},{19,18},{4,7},{5,6... | collective-permute-start | bytes 294920 | tf_op jit(solution)/shard_map/ppermute | solution.py:291
  68.4 11.4 %collective-permute-start.15 = (f32[32,16,128]{2,1,0:T(8,128)S(1)}, f32[32,16,128]{2,1,0:T(8,128)S(1)}, u32[]{:S(2)}, u32[]{:S(2)}) collective-permute-start(f32[32,16,128]{2,1,0:T(8,128)S(1)} %constant_dynamic-update-slice_fusion.2), channel_id=1, source_target_pairs={{0,192},{64,128},{128,64},{192,0},{16,80},{80,16},{144,208},{208,1... | collective-permute-start | bytes 786440 | tf_op jit(solution)/shard_map/ppermute | solution.py:291
  73.3 18.0 %collective-permute-start.14 = (f32[8,24,128]{2,1,0:T(8,128)S(1)}, f32[8,24,128]{2,1,0:T(8,128)S(1)}, u32[]{:S(2)}, u32[]{:S(2)}) collective-permute-start(f32[8,24,128]{2,1,0:T(8,128)S(1)} %slice_subtract_fusion), channel_id=1, source_target_pairs={{0,32},{32,0},{1,33},{33,1},{2,34},{34,2},{3,35},{35,3},{4,36},{36... | collective-permute-start | bytes 294920 | tf_op jit(solution)/shard_map/ppermute | solution.py:284
  76.0 15.7 %collective-permute-start.18 = (f32[16,24,128]{2,1,0:T(8,128)S(1)}, f32[16,24,128]{2,1,0:T(8,128)S(1)}, u32[]{:S(2)}, u32[]{:S(2)}) collective-permute-start(f32[16,24,128]{2,1,0:T(8,128)S(1)} %constant_dynamic-update-slice_fusion.4), channel_id=1, source_target_pairs={{0,64},{64,0},{128,192},{192,128},{16,208},{80,144},{144,80},{208,... | collective-permute-start | bytes 589832 | tf_op jit(solution)/shard_map/ppermute | solution.py:291
  79.8 17.4 %collective-permute-start.21 = (f32[64,16,128]{2,1,0:T(8,128)S(1)}, f32[64,16,128]{2,1,0:T(8,128)S(1)}, u32[]{:S(2)}, u32[]{:S(2)}) collective-permute-start(f32[64,16,128]{2,1,0:T(8,128)S(1)} %constant_dynamic-update-slice_fusion.6.x_own), channel_id=1, source_target_pairs={{0,16},{16,0},{1,17},{17,1},{2,18},{18,2},{3,19},{19,3},{4,20},{20... | collective-permute-start | bytes 1572872 | tf_op jit(solution)/shard_map/ppermute | solution.py:284
  91.8 9.5 %collective-permute-start.20 = (f32[32,24,128]{2,1,0:T(8,128)S(1)}, f32[32,24,128]{2,1,0:T(8,128)S(1)}, u32[]{:S(2)}, u32[]{:S(2)}) collective-permute-start(f32[32,24,128]{2,1,0:T(8,128)S(1)} %constant_dynamic-update-slice_fusion.10), channel_id=1, source_target_pairs={{0,192},{64,128},{128,64},{192,0},{16,80},{80,16},{144,208},{208,1... | collective-permute-start | bytes 1179656 | tf_op jit(solution)/shard_map/ppermute | solution.py:291
  105.0 9.2 %collective-permute-start.23 = (f32[64,16,128]{2,1,0:T(8,128)S(1)}, f32[64,16,128]{2,1,0:T(8,128)S(1)}, u32[]{:S(2)}, u32[]{:S(2)}) collective-permute-start(f32[64,16,128]{2,1,0:T(8,128)S(1)} %get-tuple-element.219), channel_id=1, source_target_pairs={{0,4},{4,0},{8,12},{12,8},{16,28},{20,24},{24,20},{28,16},{1,5},{5... | collective-permute-start | bytes 1572872 | tf_op jit(solution)/shard_map/ppermute | solution.py:291
  105.6 8.8 %collective-permute-start.22 = (f32[64,24,128]{2,1,0:T(8,128)S(1)}, f32[64,24,128]{2,1,0:T(8,128)S(1)}, u32[]{:S(2)}, u32[]{:S(2)}) collective-permute-start(f32[64,24,128]{2,1,0:T(8,128)S(1)} %constant_dynamic-update-slice_fusion.16.x_own), channel_id=1, source_target_pairs={{0,16},{16,0},{1,17},{17,1},{2,18},{18,2},{3,19},{19,3},{4,20},{20... | collective-permute-start | bytes 2359304 | tf_op jit(solution)/shard_map/ppermute | solution.py:284
  113.5 14.9 %collective-permute-start.28 = (f32[64,24,128]{2,1,0:T(8,128)S(1)}, f32[64,24,128]{2,1,0:T(8,128)S(1)}, u32[]{:S(2)}, u32[]{:S(2)}) collective-permute-start(f32[64,24,128]{2,1,0:T(8,128)S(1)} %get-tuple-element.228), channel_id=1, source_target_pairs={{0,4},{4,0},{8,12},{12,8},{16,28},{20,24},{24,20},{28,16},{1,5},{5... | collective-permute-start | bytes 2359304 | tf_op jit(solution)/shard_map/ppermute | solution.py:291
  118.7 22.4 %collective-permute-start.25 = (f32[64,24,128]{2,1,0:T(8,128)S(1)}, f32[64,24,128]{2,1,0:T(8,128)S(1)}, u32[]{:S(2)}, u32[]{:S(2)}) collective-permute-start(f32[64,24,128]{2,1,0:T(8,128)S(1)} %get-tuple-element.236), channel_id=1, source_target_pairs={{0,4},{4,0},{8,12},{12,8},{16,28},{20,24},{24,20},{28,16},{1,5},{5... | collective-permute-start | bytes 2359304 | tf_op jit(solution)/shard_map/ppermute | solution.py:291
  128.5 13.0 %collective-permute-start.31 = (f32[32,24,128]{2,1,0:T(8,128)S(1)}, f32[32,24,128]{2,1,0:T(8,128)S(1)}, u32[]{:S(2)}, u32[]{:S(2)}) collective-permute-start(f32[32,24,128]{2,1,0:T(8,128)S(1)} %slice_add_fusion.1), channel_id=1, source_target_pairs={{0,12},{4,8},{8,4},{12,0},{16,20},{20,16},{24,28},{28,24},{1,13},{... | collective-permute-start | bytes 1179656 | tf_op jit(solution)/shard_map/ppermute | solution.py:291
  129.4 14.8 %collective-permute-start.30 = (f32[8,16,128]{2,1,0:T(8,128)S(1)}, f32[8,16,128]{2,1,0:T(8,128)S(1)}, u32[]{:S(2)}, u32[]{:S(2)}) collective-permute-start(f32[8,16,128]{2,1,0:T(8,128)S(1)} %slice_add_fusion.16), channel_id=1, source_target_pairs={{0,3},{1,2},{2,1},{3,0},{16,17},{17,16},{18,19},{19,18},{4,7},{5,6... | collective-permute-start | bytes 196616 | tf_op jit(solution)/shard_map/ppermute | solution.py:291
  141.5 9.6 %collective-permute-start.34 = (f32[16,24,128]{2,1,0:T(8,128)S(1)}, f32[16,24,128]{2,1,0:T(8,128)S(1)}, u32[]{:S(2)}, u32[]{:S(2)}) collective-permute-start(f32[16,24,128]{2,1,0:T(8,128)S(1)} %slice_add_fusion.7), channel_id=1, source_target_pairs={{0,1},{1,0},{2,3},{3,2},{16,19},{17,18},{18,17},{19,16},{4,5},{5,4... | collective-permute-start | bytes 589832 | tf_op jit(solution)/shard_map/ppermute | solution.py:291
  144.3 9.4 %collective-permute-start.33 = (f32[8,16,128]{2,1,0:T(8,128)S(1)}, f32[8,16,128]{2,1,0:T(8,128)S(1)}, u32[]{:S(2)}, u32[]{:S(2)}) collective-permute-start(f32[8,16,128]{2,1,0:T(8,128)S(1)} %multiply_subtract_fusion.2), channel_id=1, source_target_pairs={{0,32},{32,0},{1,33},{33,1},{2,34},{34,2},{3,35},{35,3},{4,36},{36... | collective-permute-start | bytes 196616 | tf_op jit(solution)/shard_map/ppermute | solution.py:284
  148.4 10.9 %collective-permute-start.32 = (f32[16,24,128]{2,1,0:T(8,128)S(1)}, f32[16,24,128]{2,1,0:T(8,128)S(1)}, u32[]{:S(2)}, u32[]{:S(2)}) collective-permute-start(f32[16,24,128]{2,1,0:T(8,128)S(1)} %slice_add_fusion.6), channel_id=1, source_target_pairs={{0,1},{1,0},{2,3},{3,2},{16,19},{17,18},{18,17},{19,16},{4,5},{5,4... | collective-permute-start | bytes 589832 | tf_op jit(solution)/shard_map/ppermute | solution.py:291
  151.1 9.1 %collective-permute-start.36 = (f32[8,24,128]{2,1,0:T(8,128)S(1)}, f32[8,24,128]{2,1,0:T(8,128)S(1)}, u32[]{:S(2)}, u32[]{:S(2)}) collective-permute-start(f32[8,24,128]{2,1,0:T(8,128)S(1)} %slice_add_fusion.13), channel_id=1, source_target_pairs={{0,3},{1,2},{2,1},{3,0},{16,17},{17,16},{18,19},{19,18},{4,7},{5,6... | collective-permute-start | bytes 294920 | tf_op jit(solution)/shard_map/ppermute | solution.py:291
  163.9 11.3 %collective-permute-start.38 = (f32[8,24,128]{2,1,0:T(8,128)S(1)}, f32[8,24,128]{2,1,0:T(8,128)S(1)}, u32[]{:S(2)}, u32[]{:S(2)}) collective-permute-start(f32[8,24,128]{2,1,0:T(8,128)S(1)} %multiply_subtract_fusion), channel_id=1, source_target_pairs={{0,32},{32,0},{1,33},{33,1},{2,34},{34,2},{3,35},{35,3},{4,36},{36... | collective-permute-start | bytes 294920 | tf_op jit(solution)/shard_map/ppermute | solution.py:284
  165.1 11.1 %collective-permute-start.42 = (f32[16,24,128]{2,1,0:T(8,128)S(1)}, f32[16,24,128]{2,1,0:T(8,128)S(1)}, u32[]{:S(2)}, u32[]{:S(2)}) collective-permute-start(f32[16,24,128]{2,1,0:T(8,128)S(1)} %constant_dynamic-update-slice_fusion.22), channel_id=1, source_target_pairs={{0,64},{64,0},{128,192},{192,128},{16,208},{80,144},{144,80},{208,... | collective-permute-start | bytes 589832 | tf_op jit(solution)/shard_map/ppermute | solution.py:291
  165.8 16.3 %collective-permute-start.45 = (f32[64,16,128]{2,1,0:T(8,128)S(1)}, f32[64,16,128]{2,1,0:T(8,128)S(1)}, u32[]{:S(2)}, u32[]{:S(2)}) collective-permute-start(f32[64,16,128]{2,1,0:T(8,128)S(1)} %constant_dynamic-update-slice_fusion.24.x_own), channel_id=1, source_target_pairs={{0,16},{16,0},{1,17},{17,1},{2,18},{18,2},{3,19},{19,3},{4,20},{20... | collective-permute-start | bytes 1572872 | tf_op jit(solution)/shard_map/ppermute | solution.py:284
  176.3 10.4 %collective-permute-start.44 = (f32[32,24,128]{2,1,0:T(8,128)S(1)}, f32[32,24,128]{2,1,0:T(8,128)S(1)}, u32[]{:S(2)}, u32[]{:S(2)}) collective-permute-start(f32[32,24,128]{2,1,0:T(8,128)S(1)} %constant_dynamic-update-slice_fusion.28), channel_id=1, source_target_pairs={{0,192},{64,128},{128,64},{192,0},{16,80},{80,16},{144,208},{208,1... | collective-permute-start | bytes 1179656 | tf_op jit(solution)/shard_map/ppermute | solution.py:291
  181.1 10.2 %collective-permute-start.43 = (f32[32,24,128]{2,1,0:T(8,128)S(1)}, f32[32,24,128]{2,1,0:T(8,128)S(1)}, u32[]{:S(2)}, u32[]{:S(2)}) collective-permute-start(f32[32,24,128]{2,1,0:T(8,128)S(1)} %constant_dynamic-update-slice_fusion.30), channel_id=1, source_target_pairs={{0,192},{64,128},{128,64},{192,0},{16,80},{80,16},{144,208},{208,1... | collective-permute-start | bytes 1179656 | tf_op jit(solution)/shard_map/ppermute | solution.py:291
  186.7 8.8 %collective-permute-start.47 = (f32[64,24,128]{2,1,0:T(8,128)S(1)}, f32[64,24,128]{2,1,0:T(8,128)S(1)}, u32[]{:S(2)}, u32[]{:S(2)}) collective-permute-start(f32[64,24,128]{2,1,0:T(8,128)S(1)} %constant_dynamic-update-slice_fusion.32.x_own), channel_id=1, source_target_pairs={{0,16},{16,0},{1,17},{17,1},{2,18},{18,2},{3,19},{19,3},{4,20},{20... | collective-permute-start | bytes 2359304 | tf_op jit(solution)/shard_map/ppermute | solution.py:284
  (17 other events, 102.9 us)
